TPU v7x, 32 devices: a whole 2x2x4 slice. The times are simulated.
32 devices in a mesh: dp: 4 (over x, core), mp: 8 (over z, y).
Axes of the slice: x: 2, y: 2, z: 4, core: 2. Of those that a mesh axis runs over, the one named last changes fastest.
Arguments:
- accumulated: bfloat16 [16384, 28672], P('dp', 'mp'), may hold values from -6 to 6
- signs: int32 [8192], replicated, may hold values from 0 to 1
- q_start: bfloat16 [28672, 128], P('mp'), may hold values from -6 to 6
Outputs:
- new_error: bfloat16 [16384, 28672], P('dp', 'mp')
- p_basis: float32 [16384, 128], P('dp')
- q_factor: float32 [28672, 128], P('mp')
Inputs may be any that keep to these rules, and one draw needn't show every extreme that they name: `signs`: 1 keeps a row's sign, 0 negates it.
All inputs are finite; a program needn't handle non-finite values.
Results may differ from a plain program's by a relative error of at most 0.0053.
Values may be sent and summed in bfloat16 or wider, within the bound.
No kernel may reach another device: no remote copies, remote signals or barrier semaphores. Data moves between devices by JAX's collectives and lax.ppermute only.
A program may use at most 256 MiB of HBM per device.

v0:
```python
import math

import jax
import jax.numpy as jnp
from jax import lax
from jax.sharding import PartitionSpec as P

REPLICAS = 2


def from_partner(block, axis, distance):
    count = lax.axis_size(axis)
    route = []
    for low in range(count):
        high = low | 1 << distance
        if high != low and high < count:
            route += [(low, high), (high, low)]
    return lax.ppermute(block, axis, route)


def sylvester(size):
    index = jnp.arange(size, dtype=jnp.int32)
    both = index[:, None] & index[None, :]
    parity = jnp.zeros((size, size), jnp.int32)
    for shift in range(max(size.bit_length() - 1, 1)):
        parity = parity ^ both >> shift & 1
    return (1 - 2 * parity).astype(jnp.float32)


def rotate(block):
    total_rows, width = block.shape
    factors = []
    remaining = total_rows
    while remaining > 1:
        factor = min(32, remaining)
        factors.append(factor)
        remaining = remaining // factor
    cube = block.reshape(tuple(factors) + (width,))
    for which_axis, factor in enumerate(factors):
        cube = jnp.tensordot(
            sylvester(factor), cube, axes=([1], [which_axis]), precision=lax.Precision.HIGHEST
        )
        cube = jnp.moveaxis(cube, 0, which_axis)
    return cube.reshape(total_rows, width)


def local(accumulated, signs, q_start):
    local_rows, columns = accumulated.shape
    dp_count = lax.axis_size("dp")
    group_size = dp_count // REPLICAS
    cross_bits = group_size.bit_length() - 1
    all_bits = dp_count.bit_length() - 1
    dp_index = lax.axis_index("dp")
    position = dp_index % group_size
    first_copy = jnp.where(dp_index < group_size, 1.0, 0.0).astype(jnp.float32)
    local_signs = lax.dynamic_slice_in_dim(signs, position * local_rows, local_rows)
    flipped = jnp.where(local_signs[:, None] == 1, accumulated, -accumulated)
    field = rotate(flipped.astype(jnp.float32))
    for bit_number in range(cross_bits):
        partner = from_partner(field, "dp", bit_number)
        upper_half = dp_index >> bit_number & 1 == 1
        field = jnp.where(upper_half, partner - field, field + partner)
    rotated = (field * (1.0 / math.sqrt(local_rows * group_size))).astype(jnp.bfloat16)
    rotated = lax.optimization_barrier(rotated)
    local_proj = jnp.dot(rotated, q_start, preferred_element_type=jnp.float32)
    projected = lax.psum(local_proj, "mp")
    for bit_number in range(cross_bits, all_bits):
        projected = projected + from_partner(projected, "dp", bit_number)
    own_gram = jnp.dot(projected.T, projected, precision=lax.Precision.HIGHEST) * first_copy
    gram = lax.psum(own_gram, "dp")
    lower = jnp.linalg.cholesky(gram)
    p_basis = jax.scipy.linalg.solve_triangular(lower, projected.T, lower=True).T
    basis16 = p_basis.astype(jnp.bfloat16)
    right_part = jnp.einsum("rc,rk->ck", rotated, basis16, preferred_element_type=jnp.float32)
    q_factor = lax.psum(right_part, "dp") / REPLICAS
    q16 = q_factor.astype(jnp.bfloat16)
    approx = jnp.einsum("rk,ck->rc", basis16, q16, preferred_element_type=jnp.float32)
    new_error = (rotated.astype(jnp.float32) - approx).astype(jnp.bfloat16)
    return (new_error, p_basis, q_factor)


def solution(mesh):
    in_specs = (P("dp", "mp"), P(), P("mp", None))
    out_specs = (P("dp", "mp"), P("dp", None), P("mp", None))
    return jax.shard_map(local, mesh=mesh, in_specs=in_specs, out_specs=out_specs, check_vma=False)
```

profile of v0, /device:TPU:0, one launch (start us, length us, event | category | flops | bytes accessed | tf_op | source)
XLA Modules:
  0.0 906.7 jit_solution(16143393757283168668)
XLA Ops:
  7.2 0.0 all-reduce.4.cloned.1.call-start
  7.2 0.8 dynamic-slice_compare_fusion
  8.0 20.3 %negate_select_fusion = bf16[4096,3584]{1,0:T(8,128)(2,1)} fusion(bf16[4096,3584]{1,0:T(8,128)(2,1)} %param.3, pred[4096]{0:T(1024)(128)(4,1)S(1)} %dynamic-slice_compare_fusion), kind=kLoop, calls=%fused_computation.7 | loop fusion | flops 29360128 | bytes 58724352 | tf_op jit(solution)/shard_map/jit(_where)/select_n | solution.py:57
  28.3 46.2 %reshape.24 = bf16[32,32,4,3584]{3,2,1,0:T(4,128)(2,1)} reshape(bf16[4096,3584]{1,0:T(8,128)(2,1)} %negate_select_fusion) | data formatting | bytes 58720256 | tf_op jit(solution)/shard_map/reshape | solution.py:38
  74.5 53.4 %fusion.8 = f32[32,32,4,3584]{3,0,2,1:T(8,128)} fusion(bf16[32,32,4,3584]{3,2,1,0:T(4,128)(2,1)} %reshape.24), kind=kOutput, calls=%fused_computation.9 | convolution fusion | flops 5637163008 | bytes 88080384 | tf_op jit(solution)/shard_map/dot_general | solution.py:40
  127.9 97.8 %fusion.2 = f32[32,32,4,3584]{3,0,2,1:T(8,128)} fusion(f32[32,32,4,3584]{3,0,2,1:T(8,128)} %fusion.8), kind=kOutput, calls=%fused_computation.2 | convolution fusion | flops 5637163008 | bytes 117440512 | tf_op jit(solution)/shard_map/dot_general | solution.py:40
  225.6 157.6 %fusion.5 = f32[32,32,4,3584]{3,2,1,0:T(4,128)} fusion(f32[32,32,4,3584]{3,0,2,1:T(8,128)} %fusion.2), kind=kOutput, calls=%fused_computation.8 | convolution fusion | flops 704643200 | bytes 117440512 | tf_op jit(solution)/shard_map/dot_general | solution.py:40
  383.2 65.5 %reshape.25 = f32[4096,3584]{1,0:T(8,128)} reshape(f32[32,32,4,3584]{3,2,1,0:T(4,128)} %fusion.5) | data formatting | bytes 117440512 | tf_op jit(solution)/shard_map/reshape | solution.py:44
  448.7 0.5 collective-permute-start
  449.2 85.1 %collective-permute-done = f32[4096,3584]{1,0:T(8,128)} collective-permute-done((f32[4096,3584]{1,0:T(8,128)}, f32[4096,3584]{1,0:T(8,128)}, u32[]{:S(2)}, u32[]{:S(2)}) %collective-permute-start) | collective-permute-done | bytes 58720288 | tf_op jit(solution)/shard_map/ppermute | solution.py:18
  534.3 47.0 %multiply_convert_fusion = bf16[4096,3584]{1,0:T(8,128)(2,1)} fusion(f32[4096,3584]{1,0:T(8,128)} %reshape.25, f32[4096,3584]{1,0:T(8,128)} %collective-permute-done, pred[]{:T(512)S(6)} %eq.12), kind=kLoop, calls=%fused_computation.6 | loop fusion | flops 73400320 | bytes 146800640 | tf_op jit(solution)/shard_map/convert_element_type | solution.py:63
  581.3 14.7 %fusion.50 = f32[4096,128]{1,0:T(8,128)} fusion(bf16[4096,3584]{1,0:T(8,128)(2,1)} %multiply_convert_fusion, bf16[3584,128]{1,0:T(8,128)(2,1)S(1)} %copy-done), kind=kOutput, calls=%fused_computation.61 | convolution fusion | flops 3758096384 | bytes 32374784 | tf_op jit(solution)/shard_map/dot_general | solution.py:65
  596.0 0.0 all-reduce.6.cloned.1.call-start
  596.0 104.6 %all-reduce.4.cloned.1.call-done = f32[4096,128]{1,0:T(8,128)} async-done(((f32[4096,128]{1,0:T(8,128)}), f32[4096,128]{1,0:T(8,128)}) %all-reduce.4.cloned.1.call-update) | async-done | bytes 2097168 | tf_op jit(solution)/shard_map/psum | solution.py:66
  700.6 1.5 collective-permute-start.1
  702.1 46.0 %collective-permute-done.1 = f32[4096,128]{1,0:T(8,128)} collective-permute-done((f32[4096,128]{1,0:T(8,128)}, f32[4096,128]{1,0:T(8,128)}, u32[]{:S(2)}, u32[]{:S(2)}) %collective-permute-start.1) | collective-permute-done | bytes 2097184 | tf_op jit(solution)/shard_map/ppermute | solution.py:18
  748.1 2.4 add.34
  750.5 4.1 convolution_multiply_fusion
  754.6 0.3 all-reduce.8.cloned.1.call-start
  754.9 30.9 %all-reduce.6.cloned.1.call-done = f32[128,128]{0,1:T(8,128)} async-done(((f32[128,128]{0,1:T(8,128)}), f32[128,128]{0,1:T(8,128)}) %all-reduce.6.cloned.1.call-update) | async-done | bytes 65552 | tf_op jit(solution)/shard_map/psum | solution.py:70
  785.8 0.9 copy.7
  786.8 0.9 fusion.17
  787.6 11.7 %cholesky.16 = f32[128,128]{1,0:T(8,128)S(1)} custom-call(f32[128,128]{1,0:T(8,128)S(1)} %fusion.17), custom_call_target="Cholesky" | custom-call | tf_op jit(solution)/shard_map/jit(cholesky)/cholesky | solution.py:71
  799.4 0.6 compare_reduce_fusion
  800.0 0.7 fusion.14
  800.7 9.8 %custom-call.7 = f32[1,128,128]{1,2,0:T(8,128)S(1)} custom-call(f32[1,128,128]{2,1,0:T(8,128)S(1)} %fusion.14), custom_call_target="InvertDiagBlocksLowerTriangular" | custom-call | tf_op jit(solution)/shard_map/jit(_solve_triangular)/triangular_solve | solution.py:72
  810.5 1.8 fusion.15
  812.4 1.3 copy-done.1
  813.7 14.9 %fusion.12 = f32[3584,128]{1,0:T(8,128)} fusion(bf16[4096,3584]{1,0:T(8,128)(2,1)} %multiply_convert_fusion, f32[4096,128]{1,0:T(8,128)S(1)} %fusion.15), kind=kOutput, calls=%fused_computation.15 | convolution fusion | flops 3758620672 | bytes 33292288 | tf_op jit(solution)/shard_map/rc,rk->ck/dot_general | solution.py:74
  828.6 47.3 %all-reduce.8.cloned.1.call-done = f32[3584,128]{1,0:T(8,128)} async-done(((f32[3584,128]{1,0:T(8,128)}), f32[3584,128]{1,0:T(8,128)}) %all-reduce.8.cloned.1.call-update) | async-done | bytes 1835024 | tf_op jit(solution)/shard_map/psum | solution.py:75
  875.8 1.6 broadcast_multiply_fusion
  877.5 22.2 %subtract_convert_fusion = bf16[4096,3584]{1,0:T(8,128)(2,1)} fusion(bf16[4096,3584]{1,0:T(8,128)(2,1)} %multiply_convert_fusion, f32[3584,128]{1,0:T(8,128)S(1)} %broadcast_multiply_fusion, f32[4096,128]{1,0:T(8,128)} %copy-done.1), kind=kOutput, calls=%fused_computation.5 | convolution fusion | flops 3803119616 | bytes 62652416 | tf_op jit(solution)/shard_map/rk,ck->rc/dot_general | solution.py:77
  (9 shorter events, 0.1 us)
Async XLA Ops:
  7.2 574.1 %copy-start = (bf16[3584,128]{1,0:T(8,128)(2,1)S(1)}, bf16[3584,128]{1,0:T(8,128)(2,1)}, u32[]{:S(2)}) copy-start(bf16[3584,128]{1,0:T(8,128)(2,1)} %param.5) | copy-start | bytes 2752516
  7.2 693.4 %all-reduce.4.cloned.1.call-start = ((), (), s32[]{:S(2)}) async-start(), calls=%async_computation | async-start | bytes 4194304 | tf_op jit(solution)/shard_map/psum | solution.py:66
  448.7 85.6 %collective-permute-start = (f32[4096,3584]{1,0:T(8,128)}, f32[4096,3584]{1,0:T(8,128)}, u32[]{:S(2)}, u32[]{:S(2)}) collective-permute-start(f32[4096,3584]{1,0:T(8,128)} %reshape.25), channel_id=1, source_target_pairs={{0,8},{8,0},{16,24},{24,16},{1,9},{9,1},{17,25},{25,17},{2,10},{10... | collective-permute-start | bytes 176160768 | tf_op jit(solution)/shard_map/ppermute | solution.py:18
  596.0 189.9 %all-reduce.6.cloned.1.call-start = ((), (), s32[]{:S(2)}) async-start(), calls=%async_computation.1 | async-start | bytes 131072 | tf_op jit(solution)/shard_map/psum | solution.py:70
  700.6 47.4 %collective-permute-start.1 = (f32[4096,128]{1,0:T(8,128)}, f32[4096,128]{1,0:T(8,128)}, u32[]{:S(2)}, u32[]{:S(2)}) collective-permute-start(f32[4096,128]{1,0:T(8,128)} %all-reduce.4.cloned.1.call-done), channel_id=1, source_target_pairs={{0,16},{16,0},{8,24},{24,8},{1,17},{17,1},{9,25},{25,9},{2,18},{18... | collective-permute-start | bytes 6291464 | tf_op jit(solution)/shard_map/ppermute | solution.py:18
  754.6 121.2 %all-reduce.8.cloned.1.call-start = ((), (), s32[]{:S(2)}) async-start(), calls=%async_computation.2 | async-start | bytes 3670016 | tf_op jit(solution)/shard_map/psum | solution.py:75
  812.4 1.3 copy-start.1
  877.5 22.2 %copy-start.2 = (f32[3584,128]{1,0:T(8,128)}, f32[3584,128]{1,0:T(8,128)S(1)}, u32[]{:S(2)}) copy-start(f32[3584,128]{1,0:T(8,128)S(1)} %broadcast_multiply_fusion) | copy-start | bytes 5505028
Sparse Core Ops, SparseCore 0:
  596.1 104.4 all-reduce.3
  754.7 31.0 all-reduce.5
  828.7 47.1 all-reduce.7
where the time goes:
time: 918 us; the launch traced here: 907 us
  matrix products  366 us (40%)
  waiting for transfers between devices  314 us (34%)
  local copies, waits for them, and re-layouts  114 us (12%)
  other arithmetic  95.8 us (10%)
  between operations  14.3 us (2%)
    dot_general x3, matrix products, rotate(): jnp.tensordot(sylvester(factor), cube, axes=([1], [which_axis]), precisio...  309 us
    ppermute x2, waiting for transfers between devices, from_partner(): return lax.ppermute(block, axis, route)  131 us
    psum x1, waiting for transfers between devices, local(): projected = lax.psum(local_proj, 'mp')  105 us
    reshape x1, local copies, waits for them, and re-layouts, rotate(): return cube.reshape(total_rows, width)  65.5 us
    psum x1, waiting for transfers between devices, local(): q_factor = lax.psum(right_part, 'dp') / REPLICAS  47.3 us
    convert_element_type x1, other arithmetic, local(): (field * (1.0 / math.sqrt(local_rows * group_size))).astype(jnp.bfloat16)  47 us
    reshape x1, local copies, waits for them, and re-layouts, rotate(): cube = block.reshape(tuple(factors) + (width,))  46.2 us
    psum x1, waiting for transfers between devices, local(): gram = lax.psum(own_gram, 'dp')  30.9 us
  transfers between devices with their start and end apart: 5, of which 5 were waited for; matrix products, arithmetic and copies ran while one was open for 0% of the time, Pallas kernels for 0%

commit v1 on v0

v1 whole, which is shorter than its diff:
```python
import functools
import math

import jax
import jax.numpy as jnp
from jax import lax
from jax.experimental import pallas as pl
from jax.experimental.pallas import tpu as pltpu
from jax.sharding import Mesh, PartitionSpec as P

REPLICAS = 2
F32 = jnp.float32
BF16 = jnp.bfloat16
VMEM_BYTES = 56 * 1024 * 1024


def sylvester(size):
    index = jnp.arange(size, dtype=jnp.int32)
    parity = lax.population_count(index[:, None] & index[None, :]) & 1
    return (1 - 2 * parity).astype(F32)


def tile_width(columns):
    return 256 if columns % 256 == 0 else 128


def signed_hadamard(signs, position, group, rows):
    side = min(256, rows)
    parts = []
    for distance in range(group):
        other = position ^ distance
        parity = lax.population_count(position & other) & 1
        mine = lax.dynamic_slice_in_dim(signs, other * rows, rows)
        parts.append(((2 * mine - 1) * (1 - 2 * parity)).reshape(rows // side, 1, side))
    table = sylvester(side)[None]
    return jnp.concatenate([table * part.astype(F32) for part in parts], axis=2).astype(BF16)


def rotate_body(group, scale, *refs):
    block_refs, table_ref, out_ref, field_ref = refs[:group], refs[group], refs[group + 1], refs[group + 2]
    count, side, width = field_ref.shape

    @pl.loop(0, count, unroll=4)
    def _(b):
        rows = pl.ds(pl.multiple_of(b * side, side), side)
        stacked = jnp.concatenate([ref[rows, :] for ref in block_refs], axis=0)
        field_ref[b] = jnp.dot(table_ref[b], stacked, preferred_element_type=F32)

    @pl.loop(0, side // 16)
    def _(i):
        inner = pl.multiple_of(i * 16, 16)
        for start in range(0, width, 128):
            lanes = slice(start, start + 128)
            values = [field_ref[b, pl.ds(inner, 16), lanes] for b in range(count)]
            step = 1
            while step < count:
                for b in range(count):
                    if not b & step:
                        low, high = values[b], values[b | step]
                        values[b], values[b | step] = low + high, low - high
                step *= 2
            for b in range(count):
                out_ref[pl.ds(b * side + inner, 16), lanes] = (values[b] * scale).astype(out_ref.dtype)


def rotate(blocks, table, out_type):
    group = len(blocks)
    rows, columns = blocks[0].shape
    count, side, _ = table.shape
    width = tile_width(columns)
    scale = 1.0 / math.sqrt(rows * group)
    strip = pl.BlockSpec((rows, width), lambda j: (0, j))
    return pl.pallas_call(
        functools.partial(rotate_body, group, scale),
        grid=(columns // width,),
        out_shape=jax.ShapeDtypeStruct((rows, columns), out_type),
        in_specs=[strip] * group + [pl.BlockSpec(table.shape, lambda j: (0, 0, 0))],
        out_specs=strip,
        scratch_shapes=[pltpu.VMEM((count, side, width), F32)],
        compiler_params=pltpu.CompilerParams(vmem_limit_bytes=VMEM_BYTES),
        cost_estimate=pl.CostEstimate(
            flops=2 * rows * columns * side * group,
            bytes_accessed=rows * columns * 2 * (group + 1) + table.size * 2,
            transcendentals=0,
        ),
    )(*blocks, table)


def right_body(group, position_ref, *refs):
    del position_ref
    block_refs, left_ref, out_ref = refs[:group], refs[group], refs[group + 1]
    total = jnp.dot(left_ref[0], block_refs[0][...], preferred_element_type=F32)
    for d in range(1, group):
        total += jnp.dot(left_ref[d], block_refs[d][...], preferred_element_type=F32)
    out_ref[...] = total


def right_share(blocks, left, position, share):
    group = len(blocks)
    rows, _ = blocks[0].shape
    rank = left.shape[1]
    width = tile_width(share)
    steps = share // width
    strip = pl.BlockSpec((rows, width), lambda j, where: (0, where[0] * steps + j))
    return pl.pallas_call(
        functools.partial(right_body, group),
        out_shape=jax.ShapeDtypeStruct((rank, share), F32),
        grid_spec=pltpu.PrefetchScalarGridSpec(
            num_scalar_prefetch=1,
            grid=(steps,),
            in_specs=[strip] * group + [pl.BlockSpec(left.shape, lambda j, where: (0, 0, 0))],
            out_specs=pl.BlockSpec((rank, width), lambda j, where: (0, j)),
        ),
        compiler_params=pltpu.CompilerParams(vmem_limit_bytes=VMEM_BYTES),
        cost_estimate=pl.CostEstimate(
            flops=2 * rows * group * share * rank,
            bytes_accessed=rows * share * 2 * group + left.size * 2 + rank * share * 4,
            transcendentals=0,
        ),
    )(position.reshape(1), *blocks, left)


def residual_body(rotated_ref, basis_ref, right_ref, out_ref):
    rows, _ = rotated_ref.shape
    chunk = min(256, rows)

    @pl.loop(0, rows // chunk, unroll=2)
    def _(i):
        part = pl.ds(pl.multiple_of(i * chunk, chunk), chunk)
        approx = jnp.dot(basis_ref[part, :], right_ref[...], preferred_element_type=F32)
        out_ref[part, :] = (rotated_ref[part, :].astype(F32) - approx).astype(out_ref.dtype)


def residual(rotated, basis16, right16):
    rows, columns = rotated.shape
    rank = basis16.shape[1]
    width = tile_width(columns)
    strip = pl.BlockSpec((rows, width), lambda j: (0, j))
    return pl.pallas_call(
        residual_body,
        grid=(columns // width,),
        out_shape=jax.ShapeDtypeStruct((rows, columns), BF16),
        in_specs=[
            strip,
            pl.BlockSpec((rows, rank), lambda j: (0, 0)),
            pl.BlockSpec((rank, width), lambda j: (0, j)),
        ],
        out_specs=strip,
        compiler_params=pltpu.CompilerParams(vmem_limit_bytes=VMEM_BYTES),
        cost_estimate=pl.CostEstimate(
            flops=2 * rows * columns * rank, bytes_accessed=rows * columns * 4, transcendentals=0
        ),
    )(rotated, basis16, right16)


def from_distance(block, axis, distance):
    count = lax.axis_size(axis)
    return lax.ppermute(block, axis, [(p, p ^ distance) for p in range(count)])


def gather_positions(block, position, dimension):
    group = lax.axis_size("pos")
    if group == 2:
        other = from_distance(block, "pos", 1)
        first = position == 0
        return jnp.concatenate(
            [jnp.where(first, block, other), jnp.where(first, other, block)], axis=dimension
        )
    return lax.all_gather(block, "pos", axis=dimension, tiled=True)


def local(accumulated, signs, q_start):
    rows, columns = accumulated.shape
    rank = q_start.shape[1]
    group = lax.axis_size("pos")
    position = lax.axis_index("pos")

    blocks = [accumulated] + [from_distance(accumulated, "pos", d) for d in range(1, group)]
    table = signed_hadamard(signs, position, group, rows)

    partial = jnp.dot(accumulated, q_start, preferred_element_type=F32)
    mine = lax.psum_scatter(partial, ("rep", "mp"), scatter_dimension=0, tiled=True)
    own16 = lax.all_gather(mine.astype(BF16), ("rep", "mp"), axis=0, tiled=True)
    around16 = [own16] + [from_distance(own16, "pos", d) for d in range(1, group)]

    rotated = rotate(blocks, table, BF16)

    everywhere = jnp.stack(around16)
    if group > 2:
        everywhere = lax.all_gather(own16, "pos", axis=0, tiled=False)
    gram = jnp.einsum("grk,grl->kl", everywhere, everywhere, preferred_element_type=F32)
    lower = jnp.linalg.cholesky(gram)
    inverse = jax.scipy.linalg.solve_triangular(lower, jnp.eye(rank, dtype=F32), lower=True)

    share = columns // group
    if share % 128 == 0:
        left = jnp.stack([part.T for part in around16])
        half = right_share(blocks, left, position, share).astype(BF16)
        half = half.astype(F32) + from_distance(half, "rep", 1).astype(F32)
        right_half = jnp.dot(inverse, half, precision=lax.Precision.HIGHEST) / REPLICAS
        right = gather_positions(right_half, position, 1)
    else:
        whole = right_share(blocks[:1], own16.T[None], jnp.zeros((), jnp.int32), columns)
        whole = lax.psum(whole, ("rep", "pos"))
        right = jnp.dot(inverse, whole, precision=lax.Precision.HIGHEST) / REPLICAS

    turned = rotate(around16, table, F32)
    p_basis = jnp.dot(turned, inverse.T, precision=lax.Precision.HIGHEST)
    new_error = residual(rotated, p_basis.astype(BF16), right.astype(BF16))
    return (new_error, p_basis, right.T)


def solution(mesh):
    dp_count, mp_count = mesh.shape["dp"], mesh.shape["mp"]
    fine = Mesh(
        mesh.devices.reshape(REPLICAS, dp_count // REPLICAS, mp_count), ("rep", "pos", "mp")
    )
    rows_of = ("rep", "pos")
    in_specs = (P(rows_of, "mp"), P(), P("mp", None))
    out_specs = (P(rows_of, "mp"), P(rows_of, None), P("mp", None))
    return jax.shard_map(local, mesh=fine, in_specs=in_specs, out_specs=out_specs, check_vma=False)
```

time: 918 us -> 312 us (0.34); the launches traced: 907 us -> 312 us
  matrix products: 366 us -> 23.2 us
  waiting for transfers between devices: 314 us -> 137 us
  local copies, waits for them, and re-layouts: 114 us -> 5.01 us
  Pallas kernels: 0 us -> 98.1 us
  other arithmetic: 95.8 us -> 32.2 us
    dot_general x7 -> x4, matrix products: 365 us -> 22.9 us  [the longest x1 16.2 us: local(): partial = jnp.dot(accumulated, q_start, preferred_element_type=F32)]
    psum x3 -> x0, waiting for transfers between devices: 183 us -> none  [the longest x1 105 us: local(): projected = lax.psum(local_proj, 'mp')]
    ppermute x2 -> x4, waiting for transfers between devices: 131 us -> 0.01 us  [from_distance(): return lax.ppermute(block, axis, [(p, p ^ distance) for p in range(count)])]
    reshape x2 -> x0, local copies, waits for them, and re-layouts: 112 us -> none  [the longest x1 65.5 us: rotate(): return cube.reshape(total_rows, width)]
    pallas_call x0 -> x4, Pallas kernels: none -> 98.1 us  [the longest x2 51.9 us: rotate(): pl.pallas_call(functools.partial(rotate_body, group, scale), grid=(column...]
    reduce_scatter x0 -> x1, waiting for transfers between devices: none -> 83.8 us  [local(): lax.psum_scatter(partial, ('rep', 'mp'), scatter_dimension=0, tiled=True)]
    all_gather x0 -> x1, waiting for transfers between devices: none -> 53.5 us  [local(): own16 = lax.all_gather(mine.astype(BF16), ('rep', 'mp'), axis=0, tiled=True)]
    convert_element_type x1 -> x5, other arithmetic: 47 us -> 3.87 us  [the longest x1 1.54 us: local(): own16 = lax.all_gather(mine.astype(BF16), ('rep', 'mp'), axis=0, tiled=True)]
  transfers between devices with their start and end apart: 5 -> 6, of which waited for: 5 -> 2; matrix products, arithmetic and copies ran while one was open for 0% -> 18% of each run, Pallas kernels for 0% -> 17%
where the time goes in v1:
time: 312 us
  waiting for transfers between devices  137 us (44%)
  Pallas kernels  98.1 us (31%)
  other arithmetic  32.2 us (10%)
  matrix products  23.2 us (7%)
  between operations  14.2 us (5%)
  local copies, waits for them, and re-layouts  5.01 us (2%)
    reduce_scatter x1, waiting for transfers between devices, local(): lax.psum_scatter(partial, ('rep', 'mp'), scatter_dimension=0, tiled=True)  83.8 us
    all_gather x1, waiting for transfers between devices, local(): own16 = lax.all_gather(mine.astype(BF16), ('rep', 'mp'), axis=0, tiled=True)  53.5 us
    pallas_call x2, Pallas kernels, rotate(): pl.pallas_call(functools.partial(rotate_body, group, scale), grid=(column...  51.9 us
    pallas_call x1, Pallas kernels, residual(): pl.pallas_call(residual_body, grid=(columns // width,), out_shape=jax.Sha...  32.4 us
    dot_general x1, matrix products, local(): partial = jnp.dot(accumulated, q_start, preferred_element_type=F32)  16.2 us
    pallas_call x1, Pallas kernels, right_share(): pl.pallas_call(functools.partial(right_body, group), out_shape=jax.ShapeD...  13.8 us
    another operation x3, other arithmetic, local(): lower = jnp.linalg.cholesky(gram)  12.4 us
    another operation x2, other arithmetic, local(): jax.scipy.linalg.solve_triangular(lower, jnp.eye(rank, dtype=F32), lower=...  10.5 us
  transfers between devices with their start and end apart: 6, of which 2 were waited for; matrix products, arithmetic and copies ran while one was open for 18% of the time, Pallas kernels for 17%

profile of v1, /device:TPU:0, one launch (start us, length us, event | category | flops | bytes accessed | tf_op | source)
XLA Modules:
  0.0 311.7 jit_solution(335058018017986059)
XLA Ops:
  7.2 0.5 collective-permute-start
  7.7 0.6 copy-done
  8.4 16.2 %fusion.18 = f32[4096,128]{0,1:T(8,128)} fusion(bf16[4096,3584]{1,0:T(8,128)(2,1)} %refs_0_.3, bf16[3584,128]{1,0:T(8,128)(2,1)S(1)} %copy-done), kind=kOutput, calls=%fused_computation.33 | convolution fusion | flops 3758096384 | bytes 32374784 | tf_op jit(solution)/shard_map/dot_general | solution.py:181
  24.7 83.8 %reduce-scatter.2.cloned.1.call-done = f32[256,128]{0,1:T(8,128)} async-done(((f32[4096,128]{0,1:T(8,128)}), f32[256,128]{0,1:T(8,128)}) %reduce-scatter.2.cloned.1.call-update) | async-done | bytes 131088 | tf_op jit(solution)/shard_map/reduce_scatter | solution.py:182
  108.5 1.5 convert_element_type.56
  110.1 53.5 %all-gather.2.cloned.1.call-done = bf16[4096,128]{0,1:T(8,128)(2,1)} async-done(((bf16[256,128]{0,1:T(8,128)(2,1)}), bf16[4096,128]{0,1:T(8,128)(2,1)}) %all-gather.2.cloned.1.call-update) | async-done | bytes 1048592 | tf_op jit(solution)/shard_map/all_gather | solution.py:183
  163.6 0.1 subtract_convert_fusion
  163.7 1.3 multiply_convert_fusion.1
  165.0 2.4 pad_maximum_fusion.refs_2_
  167.4 1.3 copy.7.refs_0_
  168.7 0.7 fusion.6
  169.5 0.1 copy.10
  169.6 11.7 %cholesky.17 = f32[128,128]{1,0:T(8,128)S(1)} custom-call(f32[128,128]{1,0:T(8,128)S(1)} %fusion.15), custom_call_target="Cholesky" | custom-call | tf_op jit(solution)/shard_map/jit(cholesky)/cholesky | solution.py:192
  181.3 0.6 compare_reduce_fusion
  182.0 0.7 fusion.12
  182.6 9.8 %custom-call.7 = f32[1,128,128]{1,2,0:T(8,128)S(1)} custom-call(f32[1,128,128]{2,1,0:T(8,128)S(1)} %fusion.12), custom_call_target="InvertDiagBlocksLowerTriangular" | custom-call | tf_op jit(solution)/shard_map/jit(_solve_triangular)/triangular_solve | solution.py:193
  192.4 1.5 pad_maximum_fusion.1.refs_2_
  193.9 13.8 %shard_map.60 = f32[128,1792]{1,0:T(8,128)} custom-call(s32[1]{0:T(128)} %bitcast.6.position_ref, bf16[4096,3584]{1,0:T(8,128)(2,1)} %refs_0_.3, bf16[4096,3584]{1,0:T(8,128)(2,1)} %collective-permute-done.refs_1_, bf16[2,128,4096]{2,1,0:T(8,128)(2,1)} %pad_maximum_fusion.1.refs_2_), custom_call_target="tpu_custom_call" | custom-call | flops 3758096384 | bytes 32374784 | tf_op jit(solution)/shard_map/pallas_call | solution.py:105
  207.8 1.2 convert_element_type.58
  209.0 0.7 collective-permute-start.2
  209.7 0.2 fusion.13
  209.9 1.3 copy.8.refs_1_
  211.2 6.4 %shard_map.59 = f32[4096,128]{1,0:T(8,128)} custom-call(bf16[4096,128]{1,0:T(8,128)(2,1)} %copy.7.refs_0_, bf16[4096,128]{1,0:T(8,128)(2,1)} %copy.8.refs_1_, bf16[16,256,512]{2,1,0:T(8,128)(2,1)} %pad_maximum_fusion.refs_2_), custom_call_target="tpu_custom_call" | custom-call | flops 536870912 | bytes 7340032 | tf_op jit(solution)/shard_map/pallas_call | solution.py:73
  217.6 5.1 %fusion.17 = (bf16[4096,128]{1,0:T(8,128)(2,1)}, f32[4096,128]{1,0:T(8,128)}) fusion(f32[4096,128]{1,0:T(8,128)} %shard_map.59, f32[128,128]{1,0:T(8,128)S(1)} %fusion.13), kind=kOutput, calls=%fused_computation.32 | convolution fusion | flops 805830656 | bytes 5308416 | tf_op jit(solution)/shard_map/dot_general | solution.py:208
  222.7 0.9 convolution_multiply_fusion
  223.6 0.3 collective-permute-start.3
  223.9 45.5 %shard_map.58.rotated_ref = bf16[4096,3584]{1,0:T(8,128)(2,1)} custom-call(bf16[4096,3584]{1,0:T(8,128)(2,1)} %refs_0_.3, bf16[4096,3584]{1,0:T(8,128)(2,1)} %collective-permute-done.refs_1_, bf16[16,256,512]{2,1,0:T(8,128)(2,1)} %pad_maximum_fusion.refs_2_), custom_call_target="tpu_custom_call" | custom-call | flops 15032385536 | bytes 92274688 | tf_op jit(solution)/shard_map/pallas_call | solution.py:73
  269.4 0.1 broadcast_select_fusion.1
  269.5 1.0 fusion.5.right_ref
  270.6 0.2 fusion.4
  270.8 1.7 copy.11
  272.4 32.4 %shard_map.61 = bf16[4096,3584]{1,0:T(8,128)(2,1)} custom-call(bf16[4096,3584]{1,0:T(8,128)(2,1)} %shard_map.58.rotated_ref, bf16[4096,128]{1,0:T(8,128)(2,1)} %get-tuple-element.12.basis_ref, bf16[128,3584]{1,0:T(8,128)(2,1)} %fusion.5.right_ref), custom_call_target="tpu_custom_call" | custom-call | flops 3758096384 | bytes 58720256 | tf_op jit(solution)/shard_map/pallas_call | solution.py:139
  (21 shorter events, 0.2 us)
Async XLA Ops:
  7.2 1.2 copy-start
  7.2 101.3 %reduce-scatter.2.cloned.1.call-start = ((), (), s32[]{:S(2)}) async-start(), calls=%async_computation.1 | async-start | bytes 2228224 | tf_op jit(solution)/shard_map/reduce_scatter | solution.py:182
  7.2 186.7 %collective-permute-start = (bf16[4096,3584]{1,0:T(8,128)(2,1)}, bf16[4096,3584]{1,0:T(8,128)(2,1)}, u32[]{:S(2)}, u32[]{:S(2)}) collective-permute-start(bf16[4096,3584]{1,0:T(8,128)(2,1)} %refs_0_.3), channel_id=1, source_target_pairs={{0,8},{8,0},{1,9},{9,1},{2,10},{10,2},{3,11},{11,3},{4,12},{12,4},... | collective-permute-start | bytes 88080392 | tf_op jit(solution)/shard_map/ppermute | solution.py:158
  24.6 139.0 %copy-start.3 = (s32[8192]{0:T(1024)S(1)}, s32[8192]{0:T(1024)}, u32[]{:S(2)}) copy-start(s32[8192]{0:T(1024)} %param.4) | copy-start | bytes 98308
  24.6 139.0 %all-gather.2.cloned.1.call-start = ((), (), s32[]{:S(2)}) async-start(), calls=%async_computation.2 | async-start | bytes 1114112 | tf_op jit(solution)/shard_map/all_gather | solution.py:183
  163.6 5.1 %collective-permute-start.1 = (bf16[4096,128]{0,1:T(8,128)(2,1)}, bf16[4096,128]{0,1:T(8,128)(2,1)S(1)}, u32[]{:S(2)}, u32[]{:S(2)}) collective-permute-start(bf16[4096,128]{0,1:T(8,128)(2,1)} %all-gather.2.cloned.1.call-done), channel_id=1, source_target_pairs={{0,8},{8,0},{1,9},{9,1},{2,10},{10,2},{3,11},{11,3},{4,12},{12,4},... | collective-permute-start | bytes 3145736 | tf_op jit(solution)/shard_map/ppermute | solution.py:158
  165.0 2.4 copy-start.2
  209.0 13.7 %collective-permute-start.2 = (bf16[128,1792]{1,0:T(8,128)(2,1)S(1)}, bf16[128,1792]{1,0:T(8,128)(2,1)S(1)}, u32[]{:S(2)}, u32[]{:S(2)}) collective-permute-start(bf16[128,1792]{1,0:T(8,128)(2,1)S(1)} %convert_element_type.58), channel_id=1, source_target_pairs={{0,16},{16,0},{1,17},{17,1},{2,18},{18,2},{3,19},{19,3},{4,20},{20... | collective-permute-start | bytes 1376264 | tf_op jit(solution)/shard_map/ppermute | solution.py:158
  223.6 45.8 %collective-permute-start.3 = (f32[128,1792]{1,0:T(8,128)S(1)}, f32[128,1792]{1,0:T(8,128)S(1)}, u32[]{:S(2)}, u32[]{:S(2)}) collective-permute-start(f32[128,1792]{1,0:T(8,128)S(1)} %convolution_multiply_fusion), channel_id=1, source_target_pairs={{0,8},{8,0},{1,9},{9,1},{2,10},{10,2},{3,11},{11,3},{4,12},{12,4},... | collective-permute-start | bytes 2752520 | tf_op jit(solution)/shard_map/ppermute | solution.py:158
  272.4 32.4 %copy-start.1 = (bf16[3584,128]{1,0:T(8,128)(2,1)S(1)}, bf16[3584,128]{1,0:T(8,128)(2,1)}, u32[]{:S(2)}) copy-start(bf16[3584,128]{1,0:T(8,128)(2,1)} %param.5) | copy-start | bytes 2752516
Sparse Core Ops, SparseCore 0:
  24.7 83.7 reduce-scatter.1
  111.8 51.7 all-gather.1

commit v2 on v0

v2 whole, which is shorter than its diff:
```python
import functools
import math

import jax
import jax.numpy as jnp
from jax import lax
from jax.experimental import pallas as pl
from jax.experimental.pallas import tpu as pltpu
from jax.sharding import Mesh, PartitionSpec as P

REPLICAS = 2
F32 = jnp.float32
BF16 = jnp.bfloat16
ANY = pl.BlockSpec(memory_space=pl.ANY)
PARAMS = pltpu.CompilerParams(vmem_limit_bytes=56 * 1024 * 1024)


def cost(flops, size):
    return pl.CostEstimate(flops=flops, bytes_accessed=size, transcendentals=0)


def sylvester(size):
    index = jnp.arange(size, dtype=jnp.int32)
    parity = lax.population_count(index[:, None] & index[None, :]) & 1
    return (1 - 2 * parity).astype(F32)


def butterflies(values):
    values = list(values)
    step = 1
    while step < len(values):
        for low in range(len(values)):
            if not low & step:
                high = low | step
                values[low], values[high] = values[low] + values[high], values[low] - values[high]
        step *= 2
    return values


def tile_width(columns):
    return 256 if columns % 256 == 0 else 128


def minus_one_to(number):
    return 1 - 2 * (lax.population_count(number) & 1)


def signed_hadamard(signs, position, group, rows):
    side = min(256, rows)
    parts = []
    for distance in range(group):
        mine = lax.dynamic_slice_in_dim(signs, (position ^ distance) * rows, rows)
        parts.append((2 * mine - 1) * minus_one_to(position & distance))
    flips = jnp.stack(parts).astype(F32).reshape(group, rows // side, 1, side)
    return (sylvester(side) * flips).astype(BF16)


def rotate_body(group, outs, *refs):
    scale_ref, table_ref = refs[group], refs[group + 1]
    block_refs, out_refs, field_ref = refs[:group], refs[-1 - outs : -1], refs[-1]
    _, count, side, width = field_ref.shape

    @pl.loop(0, count, unroll=8)
    def _(b):
        rows = pl.ds(pl.multiple_of(b * side, side), side)
        parts = [
            jnp.dot(table_ref[d, b], block_refs[d][rows, :], preferred_element_type=F32) for d in range(group)
        ]
        mixed = butterflies(parts) if outs > 1 else [sum(parts[1:], parts[0])]
        for o in range(outs):
            field_ref[o, b] = mixed[o]

    @pl.loop(0, side // 16)
    def _(i):
        inner = pl.multiple_of(i * 16, 16)
        for o in range(outs):
            for start in range(0, width, 128):
                lanes = slice(start, start + 128)
                values = butterflies([field_ref[o, b, pl.ds(inner, 16), lanes] for b in range(count)])
                for b in range(count):
                    turned = (values[b] * scale_ref[o]).astype(out_refs[o].dtype)
                    out_refs[o][pl.ds(b * side + inner, 16), lanes] = turned


def rotate(blocks, table, position, out_type, outs, after=()):
    group = len(blocks)
    rows, columns = blocks[-1].shape
    _, count, side, _ = table.shape
    width = tile_width(columns)
    steps = columns // width
    distances = jnp.arange(group, dtype=jnp.int32)
    scales = (minus_one_to(position) * minus_one_to(position & distances)).astype(F32) / math.sqrt(rows * group)

    def place(block):
        if block.shape[1] == columns:
            return pl.BlockSpec((rows, width), lambda j, where: (0, j))
        return pl.BlockSpec((rows, width), lambda j, where: (0, where[0] * steps + j))

    def body(where_ref, *refs):
        kept = refs[: group + 2] + refs[group + 2 + len(after) :]
        rotate_body(group, outs, *kept)

    return pl.pallas_call(
        body,
        out_shape=[jax.ShapeDtypeStruct((rows, columns), out_type)] * outs,
        grid_spec=pltpu.PrefetchScalarGridSpec(
            num_scalar_prefetch=1,
            grid=(steps,),
            in_specs=[place(block) for block in blocks]
            + [pl.BlockSpec(memory_space=pltpu.SMEM), pl.BlockSpec(table.shape, lambda j, where: (0, 0, 0, 0))]
            + [ANY] * len(after),
            out_specs=[pl.BlockSpec((rows, width), lambda j, where: (0, j))] * outs,
            scratch_shapes=[pltpu.VMEM((outs, count, side, width), F32)],
        ),
        compiler_params=PARAMS,
        cost_estimate=cost(2 * rows * columns * side * group, rows * columns * 2 * (group + outs) + table.size * 2),
    )(position.reshape(1), *blocks, scales, table, *after)


def project(accumulated, q_start, plane, pieces):
    rows, columns = accumulated.shape
    rank = q_start.shape[1]
    piece = rows // pieces
    tall = min(512, piece)
    steps = piece // tall

    def body(where_ref, a_ref, q_ref, *out_refs):
        at = pl.program_id(0)
        product = jnp.dot(a_ref[...], q_ref[...], preferred_element_type=F32)
        for d in range(pieces):

            @pl.when(at // steps == d)
            def _(d=d):
                out_refs[d][...] = product.astype(out_refs[d].dtype)

    def out_place(d):
        return pl.BlockSpec((tall, rank), lambda i, where: (jnp.clip(i - d * steps, 0, steps - 1), 0))

    return pl.pallas_call(
        body,
        out_shape=[jax.ShapeDtypeStruct((piece, rank), F32 if d == 0 else BF16) for d in range(pieces)],
        grid_spec=pltpu.PrefetchScalarGridSpec(
            num_scalar_prefetch=1,
            grid=(pieces * steps,),
            in_specs=[
                pl.BlockSpec((tall, columns), lambda i, where: ((where[0] ^ (i // steps)) * steps + i % steps, 0)),
                pl.BlockSpec((columns, rank), lambda i, where: (0, 0)),
            ],
            out_specs=[out_place(d) for d in range(pieces)],
        ),
        compiler_params=PARAMS,
        cost_estimate=cost(2 * rows * columns * rank, rows * columns * 2),
    )(plane.reshape(1), accumulated, q_start)


def columns_of(accumulated, owner, share, after):
    rows, _ = accumulated.shape
    width = tile_width(share)
    steps = share // width

    def body(where_ref, a_ref, after_ref, out_ref):
        out_ref[...] = a_ref[...]

    return pl.pallas_call(
        body,
        out_shape=jax.ShapeDtypeStruct((rows, share), accumulated.dtype),
        grid_spec=pltpu.PrefetchScalarGridSpec(
            num_scalar_prefetch=1,
            grid=(steps,),
            in_specs=[pl.BlockSpec((rows, width), lambda j, where: (0, where[0] * steps + j)), ANY],
            out_specs=pl.BlockSpec((rows, width), lambda j, where: (0, j)),
        ),
        compiler_params=PARAMS,
        cost_estimate=cost(0, rows * share * 4),
    )(owner.reshape(1), accumulated, after)


def split_sum(own, others, place, pieces):
    rows, rank = own.shape
    piece = rows // pieces

    def body(where_ref, own_ref, *refs):
        other_refs, out_refs = refs[: len(others)], refs[len(others) :]
        for d in range(pieces):
            at = pl.ds(pl.multiple_of((where_ref[0] ^ d) * piece, piece), piece)
            total = own_ref[at, :]
            for ref in other_refs:
                total += ref[at, :].astype(F32)
            out_refs[d][...] = total.astype(out_refs[d].dtype)

    return pl.pallas_call(
        body,
        out_shape=[jax.ShapeDtypeStruct((piece, rank), F32 if d == 0 else BF16) for d in range(pieces)],
        in_specs=[pl.BlockSpec(memory_space=pltpu.SMEM)] + [pl.BlockSpec(memory_space=pltpu.VMEM)] * (1 + len(others)),
        out_specs=[pl.BlockSpec(memory_space=pltpu.VMEM)] * pieces,
        compiler_params=PARAMS,
    )(place.reshape(1), own, *others)


def assemble(parts, place, after=()):
    rows, rank = parts[0].shape
    count = len(parts)

    def body(where_ref, *refs):
        out_ref = refs[-1]
        for d in range(count):
            at = pl.ds(pl.multiple_of((where_ref[0] ^ d) * rows, rows), rows)
            out_ref[at, :] = refs[d][...]

    return pl.pallas_call(
        body,
        out_shape=jax.ShapeDtypeStruct((rows * count, rank), parts[0].dtype),
        in_specs=[pl.BlockSpec(memory_space=pltpu.SMEM)]
        + [pl.BlockSpec(memory_space=pltpu.VMEM)] * count
        + [ANY] * len(after),
        out_specs=pl.BlockSpec(memory_space=pltpu.VMEM),
        compiler_params=PARAMS,
    )(place.reshape(1), *parts, *after)


def right_share(blocks, lefts, position, share):
    group = len(blocks)
    rows, rank = lefts[0].shape
    width = tile_width(share)
    steps = share // width

    def place(block):
        if block.shape[1] == share:
            return pl.BlockSpec((rows, width), lambda j, where: (0, j))
        return pl.BlockSpec((rows, width), lambda j, where: (0, where[0] * steps + j))

    def body(where_ref, *refs):
        block_refs, left_refs, out_ref, flat_ref = refs[:group], refs[group : 2 * group], refs[-2], refs[-1]

        @pl.when(pl.program_id(0) == 0)
        def _():
            for d in range(group):
                flat_ref[d] = left_refs[d][...].T

        total = jnp.dot(flat_ref[0], block_refs[0][...], preferred_element_type=F32)
        for d in range(1, group):
            total += jnp.dot(flat_ref[d], block_refs[d][...], preferred_element_type=F32)
        out_ref[...] = total

    return pl.pallas_call(
        body,
        out_shape=jax.ShapeDtypeStruct((rank, share), F32),
        grid_spec=pltpu.PrefetchScalarGridSpec(
            num_scalar_prefetch=1,
            grid=(steps,),
            in_specs=[place(block) for block in blocks]
            + [pl.BlockSpec((rows, rank), lambda j, where: (0, 0))] * group,
            out_specs=pl.BlockSpec((rank, width), lambda j, where: (0, j)),
            scratch_shapes=[pltpu.VMEM((group, rank, rows), BF16)],
        ),
        compiler_params=PARAMS,
        cost_estimate=cost(2 * rows * group * share * rank, rows * share * 2 * group),
    )(position.reshape(1), *blocks, *lefts)


def residual(rotated, basis16, right16, columns, owner, into=None):
    rows, share = rotated.shape
    rank = basis16.shape[1]
    width = tile_width(share)
    steps = share // width
    chunk = min(512, rows)
    earlier = () if into is None else (into,)

    def body(where_ref, rotated_ref, basis_ref, right_ref, *refs):
        out_ref = refs[-1]
        for start in range(0, rows, chunk):
            part = slice(start, start + chunk)
            approx = jnp.dot(basis_ref[part, :], right_ref[...], preferred_element_type=F32)
            out_ref[part, :] = (rotated_ref[part, :].astype(F32) - approx).astype(out_ref.dtype)

    return pl.pallas_call(
        body,
        out_shape=jax.ShapeDtypeStruct((rows, columns), BF16),
        grid_spec=pltpu.PrefetchScalarGridSpec(
            num_scalar_prefetch=1,
            grid=(steps,),
            in_specs=[
                pl.BlockSpec((rows, width), lambda j, where: (0, j)),
                pl.BlockSpec((rows, rank), lambda j, where: (0, 0)),
                pl.BlockSpec((rank, width), lambda j, where: (0, j)),
            ]
            + [ANY] * len(earlier),
            out_specs=pl.BlockSpec((rows, width), lambda j, where: (0, where[0] * steps + j)),
        ),
        input_output_aliases={4: 0} if earlier else {},
        compiler_params=PARAMS,
        cost_estimate=cost(2 * rows * share * rank, rows * share * 4),
    )(owner.reshape(1), rotated, basis16, right16, *earlier)


def from_distance(block, axis, distance):
    count = lax.axis_size(axis)
    return lax.ppermute(block, axis, [(p, p ^ distance) for p in range(count)])


def from_plane(block, distance):
    count, mp_count = REPLICAS * lax.axis_size("mp"), lax.axis_size("mp")
    change = (distance & 1) | (distance >> 1) * mp_count
    return lax.ppermute(block, ("rep", "mp"), [(p, p ^ change) for p in range(count)])


def from_line(block, distance):
    return from_distance(block, "mp", distance << 1)


def local(accumulated, signs, q_start):
    rows, columns = accumulated.shape
    rank = q_start.shape[1]
    group = lax.axis_size("pos")
    position = lax.axis_index("pos")
    mp_index = lax.axis_index("mp")
    plane = lax.axis_index("rep") * 2 + (mp_index & 1)
    line, lines = mp_index >> 1, lax.axis_size("mp") // 2
    share = columns // group
    shared = share % 128 == 0

    own, *sent = project(accumulated, q_start, plane, 4)
    came = [from_plane(sent[d - 1], d) for d in range(1, 4)]
    if shared:
        blocks = [accumulated] + [
            from_distance(columns_of(accumulated, position ^ d, share, own), "pos", d) for d in range(1, group)
        ]
    else:
        blocks = [accumulated] + [from_distance(accumulated, "pos", d) for d in range(1, group)]
    table = signed_hadamard(signs, position, group, rows)

    own, *sent = split_sum(own, came, line, lines)
    came = [from_line(sent[d - 1], d) for d in range(1, lines)]
    mine16 = sum([part.astype(F32) for part in came], own).astype(BF16)
    near16 = assemble([mine16] + [from_line(mine16, d) for d in range(1, lines)], line)
    far16 = [from_plane(near16, d) for d in range(1, 4)]
    outs = group if shared else 1
    rotated, *away = rotate(blocks, table, position, BF16, outs, after=(near16,))
    rotated = [rotated] + [from_distance(part, "pos", d + 1) for d, part in enumerate(away)]
    own16 = assemble([near16] + far16, plane, after=(rotated[0],))
    around16 = [own16] + [from_distance(own16, "pos", d) for d in range(1, group)]

    if shared:
        half = right_share(blocks, around16, position, share).astype(BF16)
        half = half.astype(F32) + from_distance(half, "rep", 1).astype(F32)
    else:
        half = right_share(blocks[:1], around16[:1], jnp.zeros((), jnp.int32), columns)
        half = lax.psum(half, ("rep", "pos"))

    everywhere = jnp.stack(around16) if group == 2 else lax.all_gather(own16, "pos", axis=0, tiled=False)
    gram = jnp.einsum("grk,grl->kl", everywhere, everywhere, preferred_element_type=F32)
    lower = jnp.linalg.cholesky(gram)
    inverse = jax.scipy.linalg.solve_triangular(lower, jnp.eye(rank, dtype=F32), lower=True)
    (turned,) = rotate(around16, table, position, F32, 1)
    p_basis = jnp.dot(turned, inverse.T, precision=lax.Precision.HIGHEST)
    basis16 = p_basis.astype(BF16)

    right = jnp.dot(inverse, half, precision=lax.Precision.HIGHEST) / REPLICAS
    if not shared:
        new_error = residual(rotated[0], basis16, right.astype(BF16), columns, jnp.zeros((), jnp.int32))
        return (new_error, p_basis, right.T)
    new_error = None
    rights = [right] + [from_distance(right, "pos", d) for d in range(1, group)]
    for d in range(group):
        new_error = residual(rotated[d], basis16, rights[d].astype(BF16), columns, position ^ d, new_error)
    q_factor = jnp.zeros((columns, rank), F32)
    for d in range(group):
        q_factor = lax.dynamic_update_slice_in_dim(q_factor, rights[d].T, (position ^ d) * share, 0)
    return (new_error, p_basis, q_factor)


def solution(mesh):
    dp_count, mp_count = mesh.shape["dp"], mesh.shape["mp"]
    fine = Mesh(
        mesh.devices.reshape(REPLICAS, dp_count // REPLICAS, mp_count), ("rep", "pos", "mp")
    )
    rows_of = ("rep", "pos")
    in_specs = (P(rows_of, "mp"), P(), P("mp", None))
    out_specs = (P(rows_of, "mp"), P(rows_of, None), P("mp", None))
    return jax.shard_map(local, mesh=fine, in_specs=in_specs, out_specs=out_specs, check_vma=False)
```

time: 918 us -> 217 us (0.24); the launches traced: 907 us -> 216 us
  matrix products: 366 us -> 9.31 us
  waiting for transfers between devices: 314 us -> 35 us
  Pallas kernels: 0 us -> 117 us
  local copies, waits for them, and re-layouts: 114 us -> 6.79 us
  other arithmetic: 95.8 us -> 28.8 us
  starting transfers between devices: 2.29 us -> 18.5 us
  between operations: 14.3 us -> 0.86 us
    dot_general x7 -> x3, matrix products: 365 us -> 9.06 us  [the longest x1 5.06 us: local(): p_basis = jnp.dot(turned, inverse.T, precision=lax.Precision.HIGHEST)]
    psum x3 -> x0, waiting for transfers between devices: 183 us -> none  [the longest x1 105 us: local(): projected = lax.psum(local_proj, 'mp')]
    pallas_call x0 -> x10, Pallas kernels: none -> 117 us  [the longest x2 36.9 us: rotate(): pl.pallas_call(body, out_shape=[jax.ShapeDtypeStruct((rows, columns), out...]
    reshape x2 -> x0, local copies, waits for them, and re-layouts: 112 us -> none  [the longest x1 65.5 us: rotate(): return cube.reshape(total_rows, width)]
    ppermute x2 -> x17, waiting for transfers between devices: 131 us -> 35 us  [the longest x6 24 us: from_plane(): lax.ppermute(block, ('rep', 'mp'), [(p, p ^ change) for p in range(count)])]
    convert_element_type x1 -> x6, other arithmetic: 47 us -> 5.41 us  [the longest x1 3.26 us: signed_hadamard(): return (sylvester(side) * flips).astype(BF16)]
    select_n x1 -> x0, other arithmetic: 20.3 us -> none  [local(): flipped = jnp.where(local_signs[:, None] == 1, accumulated, -accumulated)]
    ppermute x2 -> x17, starting transfers between devices: 1.92 us -> 18.5 us  [the longest x11 10.9 us: from_distance(): return lax.ppermute(block, axis, [(p, p ^ distance) for p in range(count)])]
  transfers between devices with their start and end apart: 5 -> 17, of which waited for: 5 -> 10; matrix products, arithmetic and copies ran while one was open for 0% -> 18% of each run, Pallas kernels for 0% -> 19%
where the time goes in v2:
time: 217 us; the launch traced here: 216 us
  Pallas kernels  117 us (54%)
  waiting for transfers between devices  35 us (16%)
  other arithmetic  28.8 us (13%)
  starting transfers between devices  18.5 us (9%)
  matrix products  9.31 us (4%)
  local copies, waits for them, and re-layouts  6.79 us (3%)
    pallas_call x2, Pallas kernels, rotate(): pl.pallas_call(body, out_shape=[jax.ShapeDtypeStruct((rows, columns), out...  36.9 us
    pallas_call x2, Pallas kernels, residual(): pl.pallas_call(body, out_shape=jax.ShapeDtypeStruct((rows, columns), BF16...  30.7 us
    ppermute x6, waiting for transfers between devices, from_plane(): lax.ppermute(block, ('rep', 'mp'), [(p, p ^ change) for p in range(count)])  24 us
    pallas_call x1, Pallas kernels, project(): pl.pallas_call(body, out_shape=[jax.ShapeDtypeStruct((piece, rank), F32 i...  15.8 us
    pallas_call x1, Pallas kernels, right_share(): pl.pallas_call(body, out_shape=jax.ShapeDtypeStruct((rank, share), F32),...  14.2 us
    pallas_call x1, Pallas kernels, columns_of(): pl.pallas_call(body, out_shape=jax.ShapeDtypeStruct((rows, share), accumu...  13.2 us
    another operation x3, other arithmetic, local(): lower = jnp.linalg.cholesky(gram)  12.4 us
    ppermute x11, waiting for transfers between devices, from_distance(): return lax.ppermute(block, axis, [(p, p ^ distance) for p in range(count)])  11 us
  transfers between devices with their start and end apart: 17, of which 10 were waited for; matrix products, arithmetic and copies ran while one was open for 18% of the time, Pallas kernels for 19%

profile of v2, /device:TPU:0, one launch (start us, length us, event | category | flops | bytes accessed | tf_op | source)
XLA Modules:
  0.0 216.0 jit_solution(1803811086945717493)
XLA Ops:
  0.6 15.8 %shard_map.58 = (f32[1024,128]{1,0:T(8,128)}, bf16[1024,128]{1,0:T(8,128)(2,1)}, bf16[1024,128]{1,0:T(8,128)(2,1)}, bf16[1024,128]{1,0:T(8,128)(2,1)}) custom-call(s32[1]{0:T(128)} %bitcast.2.where_ref, bf16[4096,3584]{1,0:T(8,128)(2,1)} %refs_0_.3, bf16[3584,128]{1,0:T(8,128)(2,1)} %q_ref.1), custom_call_target="tpu_custom_call" | custom-call | flops 3758096384 | bytes 29360128 | tf_op jit(solution)/shard_map/pallas_call | solution.py:139
  16.5 13.2 %shard_map.59 = bf16[4096,1792]{1,0:T(8,128)(2,1)} custom-call(s32[1]{0:T(128)} %bitcast.where_ref, bf16[4096,3584]{1,0:T(8,128)(2,1)} %refs_0_.3, f32[1024,128]{1,0:T(8,128)} %get-tuple-element.13.after_ref.own_ref), custom_call_target="tpu_custom_call" | custom-call | bytes 29360128 | tf_op jit(solution)/shard_map/pallas_call | solution.py:164
  30.2 2.5 %collective-permute-start.1 = (bf16[1024,128]{1,0:T(8,128)(2,1)S(1)}, bf16[1024,128]{1,0:T(8,128)(2,1)S(1)}, u32[]{:S(2)}, u32[]{:S(2)}) collective-permute-start(bf16[1024,128]{1,0:T(8,128)(2,1)S(1)} %copy-done.18), channel_id=1, source_target_pairs={{0,1},{1,0},{2,3},{3,2},{4,5},{5,4},{6,7},{7,6},{16,17},{17,16},{1... | collective-permute-start | bytes 786440 | tf_op jit(solution)/shard_map/ppermute | solution.py:304
  32.7 1.5 collective-permute-start.2
  34.3 5.3 %collective-permute-done.1.refs_0_ = bf16[1024,128]{1,0:T(8,128)(2,1)S(1)} collective-permute-done((bf16[1024,128]{1,0:T(8,128)(2,1)S(1)}, bf16[1024,128]{1,0:T(8,128)(2,1)S(1)}, u32[]{:S(2)}, u32[]{:S(2)}) %collective-permute-start.1) | collective-permute-done | bytes 262176 | tf_op jit(solution)/shard_map/ppermute | solution.py:304
  39.6 2.2 %collective-permute-done.2.refs_1_ = bf16[1024,128]{1,0:T(8,128)(2,1)S(1)} collective-permute-done((bf16[1024,128]{1,0:T(8,128)(2,1)S(1)}, bf16[1024,128]{1,0:T(8,128)(2,1)S(1)}, u32[]{:S(2)}, u32[]{:S(2)}) %collective-permute-start.2) | collective-permute-done | bytes 262176 | tf_op jit(solution)/shard_map/ppermute | solution.py:304
  41.8 4.7 %collective-permute-done.3.refs_2_ = bf16[1024,128]{1,0:T(8,128)(2,1)S(1)} collective-permute-done((bf16[1024,128]{1,0:T(8,128)(2,1)S(1)}, bf16[1024,128]{1,0:T(8,128)(2,1)S(1)}, u32[]{:S(2)}, u32[]{:S(2)}) %collective-permute-start.3) | collective-permute-done | bytes 262176 | tf_op jit(solution)/shard_map/ppermute | solution.py:304
  47.2 2.1 shard_map.60
  49.3 1.7 collective-permute-start.4
  51.0 2.6 %collective-permute-start.5 = (bf16[256,128]{1,0:T(8,128)(2,1)}, bf16[256,128]{1,0:T(8,128)(2,1)S(1)}, u32[]{:S(2)}, u32[]{:S(2)}) collective-permute-start(bf16[256,128]{1,0:T(8,128)(2,1)} %get-tuple-element.19), channel_id=1, source_target_pairs={{0,4},{1,5},{2,6},{3,7},{4,0},{5,1},{6,2},{7,3},{8,12},{9,13},{10,... | collective-permute-start | bytes 196616 | tf_op jit(solution)/shard_map/ppermute | solution.py:298
  53.7 3.3 %multiply_convert_fusion.refs_3_ = bf16[2,16,256,256]{3,2,1,0:T(8,128)(2,1)} fusion(f32[2,16,256]{2,1,0:T(8,128)S(1)} %add_convert_fusion.1, f32[256,256]{1,0:T(8,128)S(1)} %subtract_convert_fusion), kind=kLoop, calls=%fused_computation | loop fusion | flops 4194304 | bytes 4489216 | tf_op jit(solution)/shard_map/convert_element_type | solution.py:55
  58.1 1.8 collective-permute-done.6
  59.9 1.4 collective-permute-start.9
  61.4 3.0 %collective-permute-start.7 = (bf16[256,128]{1,0:T(8,128)(2,1)S(1)}, bf16[256,128]{1,0:T(8,128)(2,1)S(1)}, u32[]{:S(2)}, u32[]{:S(2)}) collective-permute-start(bf16[256,128]{1,0:T(8,128)(2,1)S(1)} %add_convert_fusion.refs_0_), channel_id=1, source_target_pairs={{0,2},{1,3},{2,0},{3,1},{4,6},{5,7},{6,4},{7,5},{8,10},{9,11},{10,... | collective-permute-start | bytes 196616 | tf_op jit(solution)/shard_map/ppermute | solution.py:298
  66.1 1.4 collective-permute-done.8.refs_2_
  68.7 1.7 shard_map.61.refs_4_.refs_0_
  70.4 30.8 %shard_map.62 = (bf16[4096,1792]{1,0:T(8,128)(2,1)}, bf16[4096,1792]{1,0:T(8,128)(2,1)}) custom-call(s32[1]{0:T(128)} %bitcast.1.where_ref, bf16[4096,3584]{1,0:T(8,128)(2,1)} %refs_0_.3, bf16[4096,1792]{1,0:T(8,128)(2,1)} %collective-permute-done.refs_1_, f32[2]{0:T(128)} %convert_multiply_fusion.refs_2_, ...), custom_call_target="tpu_custom_call" | custom-call | flops 7516192768 | bytes 62914560 | tf_op jit(solution)/shard_map/pallas_call | solution.py:103
  101.2 2.5 %collective-permute-start.13 = (bf16[1024,128]{1,0:T(8,128)(2,1)S(1)}, bf16[1024,128]{1,0:T(8,128)(2,1)S(1)}, u32[]{:S(2)}, u32[]{:S(2)}) collective-permute-start(bf16[1024,128]{1,0:T(8,128)(2,1)S(1)} %copy-done.2), channel_id=1, source_target_pairs={{0,17},{1,16},{2,19},{3,18},{4,21},{5,20},{6,23},{7,22},{16,1},{17... | collective-permute-start | bytes 786440 | tf_op jit(solution)/shard_map/ppermute | solution.py:304
  104.8 6.6 %collective-permute-done.13.refs_3_ = bf16[1024,128]{1,0:T(8,128)(2,1)S(1)} collective-permute-done((bf16[1024,128]{1,0:T(8,128)(2,1)S(1)}, bf16[1024,128]{1,0:T(8,128)(2,1)S(1)}, u32[]{:S(2)}, u32[]{:S(2)}) %collective-permute-start.13) | collective-permute-done | bytes 262176 | tf_op jit(solution)/shard_map/ppermute | solution.py:304
  111.3 5.2 %collective-permute-done.12.refs_2_ = bf16[1024,128]{1,0:T(8,128)(2,1)S(1)} collective-permute-done((bf16[1024,128]{1,0:T(8,128)(2,1)S(1)}, bf16[1024,128]{1,0:T(8,128)(2,1)S(1)}, u32[]{:S(2)}, u32[]{:S(2)}) %collective-permute-start.12) | collective-permute-done | bytes 262176 | tf_op jit(solution)/shard_map/ppermute | solution.py:304
  117.4 2.2 %shard_map.63.refs_0_.refs_2_ = bf16[4096,128]{1,0:T(8,128)(2,1)} custom-call(s32[1]{0:T(128)} %bitcast.2.where_ref, bf16[1024,128]{1,0:T(8,128)(2,1)} %shard_map.61.refs_4_.refs_0_, bf16[1024,128]{1,0:T(8,128)(2,1)} %copy-done.6, bf16[1024,128]{1,0:T(8,128)(2,1)} %copy-done.5, bf16[1024,128]{1,0:T(8,128)(2,1)} %copy-done.4, ...), custom_call_target="tpu_custom_call" | custom-call | tf_op jit(solution)/shard_map/pallas_call | solution.py:210
  119.6 5.5 %collective-permute-done.14.refs_1_.refs_3_ = bf16[4096,128]{1,0:T(8,128)(2,1)S(1)} collective-permute-done((bf16[4096,128]{1,0:T(8,128)(2,1)}, bf16[4096,128]{1,0:T(8,128)(2,1)S(1)}, u32[]{:S(2)}, u32[]{:S(2)}) %collective-permute-start.14) | collective-permute-done | bytes 1048608 | tf_op jit(solution)/shard_map/ppermute | solution.py:298
  126.1 14.2 %shard_map.65 = f32[128,1792]{1,0:T(8,128)} custom-call(s32[1]{0:T(128)} %bitcast.1.where_ref, bf16[4096,3584]{1,0:T(8,128)(2,1)} %refs_0_.3, bf16[4096,1792]{1,0:T(8,128)(2,1)} %collective-permute-done.refs_1_, bf16[4096,128]{1,0:T(8,128)(2,1)} %shard_map.63.refs_0_.refs_2_, bf16[4096,128]{1,0:T(8,128)(2,1)} %copy-done.1), custom_call_target="tpu_custom_call" | custom-call | flops 3758096384 | bytes 29360128 | tf_op jit(solution)/shard_map/pallas_call | solution.py:245
  141.5 2.3 %fusion.4 = f32[128,128]{1,0:T(8,128)S(1)} fusion(bf16[1,4096,128]{2,1,0:T(8,128)(2,1)} %bitcast.23, bf16[1,4096,128]{2,1,0:T(8,128)(2,1)S(1)} %bitcast.22), kind=kOutput, calls=%fused_computation.6 | convolution fusion | flops 269484032 | bytes 2162688 | tf_op jit(solution)/shard_map/grk,grl->kl/dot_general | solution.py:351
  143.9 11.7 %cholesky.17 = f32[128,128]{1,0:T(8,128)S(1)} custom-call(f32[128,128]{1,0:T(8,128)S(1)} %fusion.13), custom_call_target="Cholesky" | custom-call | tf_op jit(solution)/shard_map/jit(cholesky)/cholesky | solution.py:352
  155.6 1.6 collective-permute-start.15
  158.5 9.8 %custom-call.7 = f32[1,128,128]{1,2,0:T(8,128)S(1)} custom-call(f32[1,128,128]{2,1,0:T(8,128)S(1)} %fusion.10), custom_call_target="InvertDiagBlocksLowerTriangular" | custom-call | tf_op jit(solution)/shard_map/jit(_solve_triangular)/triangular_solve | solution.py:353
  168.6 1.7 fusion.16
  170.3 6.1 %shard_map.64 = f32[4096,128]{1,0:T(8,128)} custom-call(s32[1]{0:T(128)} %bitcast.1.where_ref, bf16[4096,128]{1,0:T(8,128)(2,1)} %shard_map.63.refs_0_.refs_2_, bf16[4096,128]{1,0:T(8,128)(2,1)} %copy-done.1, f32[2]{0:T(128)} %convert_multiply_fusion.refs_2_, bf16[2,16,256,256]{3,2,1,0:T(8,128)(2,1)} %multiply_convert_fusion.refs_3_), custom_call_target="tpu_custom_call" | custom-call | flops 536870912 | bytes 7340032 | tf_op jit(solution)/shard_map/pallas_call | solution.py:103
  176.4 5.1 %fusion.15 = (bf16[4096,128]{1,0:T(8,128)(2,1)}, f32[4096,128]{1,0:T(8,128)}) fusion(f32[4096,128]{1,0:T(8,128)} %shard_map.64, f32[128,128]{1,0:T(8,128)S(1)} %fusion.11), kind=kOutput, calls=%fused_computation.29 | convolution fusion | flops 805830656 | bytes 5308416 | tf_op jit(solution)/shard_map/dot_general | solution.py:355
  181.7 15.4 %shard_map.66.refs_0_ = bf16[4096,3584]{1,0:T(8,128)(2,1)} custom-call(s32[1]{0:T(128)} %bitcast.1.where_ref, bf16[4096,1792]{1,0:T(8,128)(2,1)} %get-tuple-element.22.refs_4_.rotated_ref, bf16[4096,128]{1,0:T(8,128)(2,1)} %get-tuple-element.25.basis_ref, bf16[128,1792]{1,0:T(8,128)(2,1)} %get-tuple-element.27.right_ref), custom_call_target="tpu_custom_call" | custom-call | flops 1879048192 | bytes 29360128 | tf_op jit(solution)/shard_map/pallas_call | solution.py:276
  200.6 15.4 %shard_map.67 = bf16[4096,3584]{1,0:T(8,128)(2,1)} custom-call(s32[1]{0:T(128)} %bitcast.where_ref, bf16[4096,1792]{1,0:T(8,128)(2,1)} %collective-permute-done.10.rotated_ref, bf16[4096,128]{1,0:T(8,128)(2,1)} %get-tuple-element.25.basis_ref, bf16[128,1792]{1,0:T(8,128)(2,1)} %convert_element_type.64.right_ref, ...), custom_call_target="tpu_custom_call", output_to_operand_aliasing={{}: (4, {})} | custom-call | flops 1879048192 | bytes 29360128 | tf_op jit(solution)/shard_map/pallas_call | solution.py:276
  (76 shorter events, 15.0 us)
Async XLA Ops:
  16.5 13.7 %copy-start.18 = (bf16[1024,128]{1,0:T(8,128)(2,1)S(1)}, bf16[1024,128]{1,0:T(8,128)(2,1)}, u32[]{:S(2)}) copy-start(bf16[1024,128]{1,0:T(8,128)(2,1)} %get-tuple-element.14) | copy-start | bytes 786436
  16.5 16.2 %copy-start.17 = (bf16[1024,128]{1,0:T(8,128)(2,1)S(1)}, bf16[1024,128]{1,0:T(8,128)(2,1)}, u32[]{:S(2)}) copy-start(bf16[1024,128]{1,0:T(8,128)(2,1)} %get-tuple-element.15) | copy-start | bytes 786436
  16.5 17.7 %copy-start.16 = (bf16[1024,128]{1,0:T(8,128)(2,1)S(1)}, bf16[1024,128]{1,0:T(8,128)(2,1)}, u32[]{:S(2)}) copy-start(bf16[1024,128]{1,0:T(8,128)(2,1)} %get-tuple-element.16) | copy-start | bytes 786436
  16.5 17.7 %copy-start.15 = (s32[8192]{0:T(1024)S(1)}, s32[8192]{0:T(1024)}, u32[]{:S(2)}) copy-start(s32[8192]{0:T(1024)} %param.4) | copy-start | bytes 98308
  29.7 40.7 %collective-permute-start = (bf16[4096,1792]{1,0:T(8,128)(2,1)}, bf16[4096,1792]{1,0:T(8,128)(2,1)}, u32[]{:S(2)}, u32[]{:S(2)}) collective-permute-start(bf16[4096,1792]{1,0:T(8,128)(2,1)} %shard_map.59), channel_id=1, source_target_pairs={{0,8},{8,0},{1,9},{9,1},{2,10},{10,2},{3,11},{11,3},{4,12},{12,4},... | collective-permute-start | bytes 44040200 | tf_op jit(solution)/shard_map/ppermute | solution.py:298
  30.2 9.5 %collective-permute-start.1 = (bf16[1024,128]{1,0:T(8,128)(2,1)S(1)}, bf16[1024,128]{1,0:T(8,128)(2,1)S(1)}, u32[]{:S(2)}, u32[]{:S(2)}) collective-permute-start(bf16[1024,128]{1,0:T(8,128)(2,1)S(1)} %copy-done.18), channel_id=1, source_target_pairs={{0,1},{1,0},{2,3},{3,2},{4,5},{5,4},{6,7},{7,6},{16,17},{17,16},{1... | collective-permute-start | bytes 786440 | tf_op jit(solution)/shard_map/ppermute | solution.py:304
  32.7 9.1 %collective-permute-start.2 = (bf16[1024,128]{1,0:T(8,128)(2,1)S(1)}, bf16[1024,128]{1,0:T(8,128)(2,1)S(1)}, u32[]{:S(2)}, u32[]{:S(2)}) collective-permute-start(bf16[1024,128]{1,0:T(8,128)(2,1)S(1)} %copy-done.17), channel_id=1, source_target_pairs={{0,16},{1,17},{2,18},{3,19},{4,20},{5,21},{6,22},{7,23},{16,0},{17... | collective-permute-start | bytes 786440 | tf_op jit(solution)/shard_map/ppermute | solution.py:304
  34.2 12.3 %collective-permute-start.3 = (bf16[1024,128]{1,0:T(8,128)(2,1)S(1)}, bf16[1024,128]{1,0:T(8,128)(2,1)S(1)}, u32[]{:S(2)}, u32[]{:S(2)}) collective-permute-start(bf16[1024,128]{1,0:T(8,128)(2,1)S(1)} %copy-done.16), channel_id=1, source_target_pairs={{0,17},{1,16},{2,19},{3,18},{4,21},{5,20},{6,23},{7,22},{16,1},{17... | collective-permute-start | bytes 786440 | tf_op jit(solution)/shard_map/ppermute | solution.py:304
  39.6 6.9 %copy-start.7 = (bf16[1024,128]{1,0:T(8,128)(2,1)}, bf16[1024,128]{1,0:T(8,128)(2,1)S(1)}, u32[]{:S(2)}) copy-start(bf16[1024,128]{1,0:T(8,128)(2,1)S(1)} %collective-permute-done.1.refs_0_) | copy-start | bytes 786436
  41.8 4.7 %copy-start.8 = (bf16[1024,128]{1,0:T(8,128)(2,1)}, bf16[1024,128]{1,0:T(8,128)(2,1)S(1)}, u32[]{:S(2)}) copy-start(bf16[1024,128]{1,0:T(8,128)(2,1)S(1)} %collective-permute-done.2.refs_1_) | copy-start | bytes 786436
  49.3 7.6 %collective-permute-start.4 = (bf16[256,128]{1,0:T(8,128)(2,1)}, bf16[256,128]{1,0:T(8,128)(2,1)S(1)}, u32[]{:S(2)}, u32[]{:S(2)}) collective-permute-start(bf16[256,128]{1,0:T(8,128)(2,1)} %get-tuple-element.18), channel_id=1, source_target_pairs={{0,2},{1,3},{2,0},{3,1},{4,6},{5,7},{6,4},{7,5},{8,10},{9,11},{10,... | collective-permute-start | bytes 196616 | tf_op jit(solution)/shard_map/ppermute | solution.py:298
  51.0 7.0 %collective-permute-start.5 = (bf16[256,128]{1,0:T(8,128)(2,1)}, bf16[256,128]{1,0:T(8,128)(2,1)S(1)}, u32[]{:S(2)}, u32[]{:S(2)}) collective-permute-start(bf16[256,128]{1,0:T(8,128)(2,1)} %get-tuple-element.19), channel_id=1, source_target_pairs={{0,4},{1,5},{2,6},{3,7},{4,0},{5,1},{6,2},{7,3},{8,12},{9,13},{10,... | collective-permute-start | bytes 196616 | tf_op jit(solution)/shard_map/ppermute | solution.py:298
  53.6 6.3 %copy-start.11 = (f32[256,128]{1,0:T(8,128)S(1)}, f32[256,128]{1,0:T(8,128)}, u32[]{:S(2)}) copy-start(f32[256,128]{1,0:T(8,128)} %get-tuple-element.17) | copy-start | bytes 393220
  53.6 6.3 %collective-permute-start.6 = (bf16[256,128]{1,0:T(8,128)(2,1)}, bf16[256,128]{1,0:T(8,128)(2,1)S(1)}, u32[]{:S(2)}, u32[]{:S(2)}) collective-permute-start(bf16[256,128]{1,0:T(8,128)(2,1)} %get-tuple-element.20), channel_id=1, source_target_pairs={{0,6},{1,7},{2,4},{3,5},{4,2},{5,3},{6,0},{7,1},{8,14},{9,15},{10,... | collective-permute-start | bytes 196616 | tf_op jit(solution)/shard_map/ppermute | solution.py:298
  59.9 7.6 %copy-start.10 = (bf16[256,128]{1,0:T(8,128)(2,1)}, bf16[256,128]{1,0:T(8,128)(2,1)S(1)}, u32[]{:S(2)}) copy-start(bf16[256,128]{1,0:T(8,128)(2,1)S(1)} %add_convert_fusion.refs_0_) | copy-start | bytes 196612
  59.9 6.2 %collective-permute-start.9 = (bf16[256,128]{1,0:T(8,128)(2,1)S(1)}, bf16[256,128]{1,0:T(8,128)(2,1)S(1)}, u32[]{:S(2)}, u32[]{:S(2)}) collective-permute-start(bf16[256,128]{1,0:T(8,128)(2,1)S(1)} %add_convert_fusion.refs_0_), channel_id=1, source_target_pairs={{0,6},{1,7},{2,4},{3,5},{4,2},{5,3},{6,0},{7,1},{8,14},{9,15},{10,... | collective-permute-start | bytes 196616 | tf_op jit(solution)/shard_map/ppermute | solution.py:298
  61.4 6.1 %collective-permute-start.8 = (bf16[256,128]{1,0:T(8,128)(2,1)S(1)}, bf16[256,128]{1,0:T(8,128)(2,1)S(1)}, u32[]{:S(2)}, u32[]{:S(2)}) collective-permute-start(bf16[256,128]{1,0:T(8,128)(2,1)S(1)} %add_convert_fusion.refs_0_), channel_id=1, source_target_pairs={{0,4},{1,5},{2,6},{3,7},{4,0},{5,1},{6,2},{7,3},{8,12},{9,13},{10,... | collective-permute-start | bytes 196616 | tf_op jit(solution)/shard_map/ppermute | solution.py:298
  61.4 6.1 %collective-permute-start.7 = (bf16[256,128]{1,0:T(8,128)(2,1)S(1)}, bf16[256,128]{1,0:T(8,128)(2,1)S(1)}, u32[]{:S(2)}, u32[]{:S(2)}) collective-permute-start(bf16[256,128]{1,0:T(8,128)(2,1)S(1)} %add_convert_fusion.refs_0_), channel_id=1, source_target_pairs={{0,2},{1,3},{2,0},{3,1},{4,6},{5,7},{6,4},{7,5},{8,10},{9,11},{10,... | collective-permute-start | bytes 196616 | tf_op jit(solution)/shard_map/ppermute | solution.py:298
  66.1 1.4 copy-start.12
  70.4 30.8 %copy-start.2 = (bf16[1024,128]{1,0:T(8,128)(2,1)S(1)}, bf16[1024,128]{1,0:T(8,128)(2,1)}, u32[]{:S(2)}) copy-start(bf16[1024,128]{1,0:T(8,128)(2,1)} %shard_map.61.refs_4_.refs_0_) | copy-start | bytes 786436
  101.2 99.4 %collective-permute-start.10 = (bf16[4096,1792]{1,0:T(8,128)(2,1)}, bf16[4096,1792]{1,0:T(8,128)(2,1)}, u32[]{:S(2)}, u32[]{:S(2)}) collective-permute-start(bf16[4096,1792]{1,0:T(8,128)(2,1)} %get-tuple-element.21), channel_id=1, source_target_pairs={{0,8},{8,0},{1,9},{9,1},{2,10},{10,2},{3,11},{11,3},{4,12},{12,4},... | collective-permute-start | bytes 44040200 | tf_op jit(solution)/shard_map/ppermute | solution.py:298
  101.2 10.1 %collective-permute-start.13 = (bf16[1024,128]{1,0:T(8,128)(2,1)S(1)}, bf16[1024,128]{1,0:T(8,128)(2,1)S(1)}, u32[]{:S(2)}, u32[]{:S(2)}) collective-permute-start(bf16[1024,128]{1,0:T(8,128)(2,1)S(1)} %copy-done.2), channel_id=1, source_target_pairs={{0,17},{1,16},{2,19},{3,18},{4,21},{5,20},{6,23},{7,22},{16,1},{17... | collective-permute-start | bytes 786440 | tf_op jit(solution)/shard_map/ppermute | solution.py:304
  103.7 12.8 %collective-permute-start.12 = (bf16[1024,128]{1,0:T(8,128)(2,1)S(1)}, bf16[1024,128]{1,0:T(8,128)(2,1)S(1)}, u32[]{:S(2)}, u32[]{:S(2)}) collective-permute-start(bf16[1024,128]{1,0:T(8,128)(2,1)S(1)} %copy-done.2), channel_id=1, source_target_pairs={{0,16},{1,17},{2,18},{3,19},{4,20},{5,21},{6,22},{7,23},{16,0},{17... | collective-permute-start | bytes 786440 | tf_op jit(solution)/shard_map/ppermute | solution.py:304
  104.3 12.3 %collective-permute-start.11 = (bf16[1024,128]{1,0:T(8,128)(2,1)S(1)}, bf16[1024,128]{1,0:T(8,128)(2,1)S(1)}, u32[]{:S(2)}, u32[]{:S(2)}) collective-permute-start(bf16[1024,128]{1,0:T(8,128)(2,1)S(1)} %copy-done.2), channel_id=1, source_target_pairs={{0,1},{1,0},{2,3},{3,2},{4,5},{5,4},{6,7},{7,6},{16,17},{17,16},{1... | collective-permute-start | bytes 786440 | tf_op jit(solution)/shard_map/ppermute | solution.py:304
  111.3 5.2 %copy-start.4 = (bf16[1024,128]{1,0:T(8,128)(2,1)}, bf16[1024,128]{1,0:T(8,128)(2,1)S(1)}, u32[]{:S(2)}) copy-start(bf16[1024,128]{1,0:T(8,128)(2,1)S(1)} %collective-permute-done.13.refs_3_) | copy-start | bytes 786436
  116.6 0.8 copy-start.6
  119.6 21.9 %copy-start = (bf16[4096,128]{1,0:T(8,128)(2,1)S(1)}, bf16[4096,128]{1,0:T(8,128)(2,1)}, u32[]{:S(2)}) copy-start(bf16[4096,128]{1,0:T(8,128)(2,1)} %shard_map.63.refs_0_.refs_2_) | copy-start | bytes 3145732
  119.6 5.5 %collective-permute-start.14 = (bf16[4096,128]{1,0:T(8,128)(2,1)}, bf16[4096,128]{1,0:T(8,128)(2,1)S(1)}, u32[]{:S(2)}, u32[]{:S(2)}) collective-permute-start(bf16[4096,128]{1,0:T(8,128)(2,1)} %shard_map.63.refs_0_.refs_2_), channel_id=1, source_target_pairs={{0,8},{8,0},{1,9},{9,1},{2,10},{10,2},{3,11},{11,3},{4,12},{12,4},... | collective-permute-start | bytes 3145736 | tf_op jit(solution)/shard_map/ppermute | solution.py:298
  125.1 1.0 copy-start.1
  155.6 13.0 %collective-permute-start.15 = (bf16[128,1792]{1,0:T(8,128)(2,1)S(1)}, bf16[128,1792]{1,0:T(8,128)(2,1)S(1)}, u32[]{:S(2)}, u32[]{:S(2)}) collective-permute-start(bf16[128,1792]{1,0:T(8,128)(2,1)S(1)} %convert_element_type.61), channel_id=1, source_target_pairs={{0,16},{16,0},{1,17},{17,1},{2,18},{18,2},{3,19},{19,3},{4,20},{20... | collective-permute-start | bytes 1376264 | tf_op jit(solution)/shard_map/ppermute | solution.py:298
  170.3 27.0 %collective-permute-start.16 = (f32[128,1792]{1,0:T(8,128)S(1)}, f32[128,1792]{1,0:T(8,128)S(1)}, u32[]{:S(2)}, u32[]{:S(2)}) collective-permute-start(f32[128,1792]{1,0:T(8,128)S(1)} %get-tuple-element.28), channel_id=1, source_target_pairs={{0,8},{8,0},{1,9},{9,1},{2,10},{10,2},{3,11},{11,3},{4,12},{12,4},... | collective-permute-start | bytes 2752520 | tf_op jit(solution)/shard_map/ppermute | solution.py:298
  197.3 1.2 copy-start.3
  (4 other events, 2.7 us)

commit v3 on v2

v3 whole, which is shorter than its diff:
```python
import functools
import math

import jax
import jax.numpy as jnp
from jax import lax
from jax.experimental import pallas as pl
from jax.experimental.pallas import tpu as pltpu
from jax.sharding import Mesh, PartitionSpec as P

REPLICAS = 2
PLANE = 2 * REPLICAS
F32 = jnp.float32
BF16 = jnp.bfloat16
ANY = pl.BlockSpec(memory_space=pl.ANY)
VMEM = pl.BlockSpec(memory_space=pltpu.VMEM)
SMEM = pl.BlockSpec(memory_space=pltpu.SMEM)
MIB = 1024 * 1024


def cost(flops, size):
    return pl.CostEstimate(flops=flops, bytes_accessed=size, transcendentals=0)


def params(mib):
    return pltpu.CompilerParams(vmem_limit_bytes=mib * MIB)


def sylvester(size):
    index = jnp.arange(size, dtype=jnp.int32)
    parity = lax.population_count(index[:, None] & index[None, :]) & 1
    return (1 - 2 * parity).astype(F32)


def butterflies(values):
    values = list(values)
    step = 1
    while step < len(values):
        for low in range(len(values)):
            if not low & step:
                high = low | step
                values[low], values[high] = values[low] + values[high], values[low] - values[high]
        step *= 2
    return values


def tile_width(columns):
    return 256 if columns % 256 == 0 else 128


def minus_one_to(number):
    return 1 - 2 * (lax.population_count(number) & 1)


def signed_hadamard(signs, position, group, rows):
    side = min(256, rows)
    parts = []
    for distance in range(group):
        mine = lax.dynamic_slice_in_dim(signs, (position ^ distance) * rows, rows)
        parts.append((2 * mine - 1) * minus_one_to(position & distance))
    flips = jnp.stack(parts).astype(F32).reshape(group, rows // side, 1, side)
    return (sylvester(side) * flips).astype(BF16)


def rotate_body(group, outs, pieces, *refs):
    where_ref, refs = refs[0], refs[1:]
    total = sum(pieces)
    block_refs, at = [], 0
    for number in pieces:
        block_refs.append(refs[at : at + number])
        at += number
    scale_ref, table_ref = refs[total], refs[total + 1]
    fields = 2 if pl.num_programs(0) > 1 else 1
    out_refs, field_refs = refs[-fields - outs : -fields], refs[-fields:]
    _, count, side, width = field_refs[0].shape
    cuts = PLANE if max(pieces) > 1 else 1
    each = count // cuts
    strip = side // count

    def mix(e, inside, field_ref):
        b = (where_ref[1] ^ e) * each + inside
        parts = []
        for d in range(group):
            if pieces[d] > 1:
                array, part = divmod(PLANE - 1 - e, PLANE // pieces[d])
                ref, first = block_refs[d][array], (part * each + inside) * side
            else:
                ref, first = block_refs[d][0], b * side
            rows = pl.ds(pl.multiple_of(first, side), side)
            parts.append(jnp.dot(table_ref[d, b], ref[rows, :], preferred_element_type=F32))
        mixed = butterflies(parts) if outs > 1 else [sum(parts[1:], parts[0])]
        for o in range(outs):
            field_ref[o, b] = mixed[o]

    def spread(i, field_ref):
        for part in range(0, strip, 16):
            inner = pl.multiple_of(i * strip + part, 16)
            for o in range(outs):
                for start in range(0, width, 128):
                    lanes = slice(start, start + 128)
                    values = butterflies([field_ref[o, b, pl.ds(inner, 16), lanes] for b in range(count)])
                    for b in range(count):
                        turned = (values[b] * scale_ref[o]).astype(out_refs[o].dtype)
                        out_refs[o][pl.ds(pl.multiple_of(b * side + inner, 16), 16), lanes] = turned

    def sweep(mixed_ref, spread_ref):
        for e in range(cuts):

            @pl.loop(0, each, unroll=2)
            def _(inside, e=e):
                if mixed_ref is not None:
                    mix(e, inside, mixed_ref)
                if spread_ref is not None:
                    spread(e * each + inside, spread_ref)

    if fields == 1:
        sweep(field_refs[0], None)
        sweep(None, field_refs[0])
        return
    odd = pl.program_id(0) % 2 == 1

    @pl.when(jnp.logical_not(odd))
    def _():
        sweep(field_refs[0], field_refs[1])

    @pl.when(odd)
    def _():
        sweep(field_refs[1], field_refs[0])


def rotate(blocks, table, position, plane, out_type, outs, first=0, steps=None, after=()):
    group = len(blocks)
    pieces = [len(block) for block in blocks]
    rows = sum(piece.shape[0] for piece in blocks[0])
    columns = blocks[-1][0].shape[1]
    _, count, side, _ = table.shape
    width = tile_width(columns)
    tiles = columns // width
    steps = tiles if steps is None else steps
    distances = jnp.arange(group, dtype=jnp.int32)
    scales = (minus_one_to(position) * minus_one_to(position & distances)).astype(F32) / math.sqrt(rows * group)
    where = jnp.stack([position, plane if max(pieces) > 1 else jnp.zeros_like(plane)])

    fields = 2 if steps > 1 else 1

    def place(piece):
        def index(j, where):
            j = first + jnp.minimum(j, steps - 1)
            return 0, j if piece.shape[1] == columns else where[0] * tiles + j

        return pl.BlockSpec((piece.shape[0], width), index)

    flat = [piece for block in blocks for piece in block]
    kept = 1 + len(flat) + 2

    def body(*refs):
        rotate_body(group, outs, pieces, *refs[:kept], *refs[kept + len(after) :])

    size = rows * steps * width
    return pl.pallas_call(
        body,
        out_shape=[jax.ShapeDtypeStruct((rows, steps * width), out_type)] * outs,
        grid_spec=pltpu.PrefetchScalarGridSpec(
            num_scalar_prefetch=1,
            grid=(steps + fields - 1,),
            in_specs=[place(piece) for piece in flat]
            + [pl.BlockSpec(memory_space=pltpu.SMEM), pl.BlockSpec(table.shape, lambda j, where: (0, 0, 0, 0))]
            + [ANY] * len(after),
            out_specs=[pl.BlockSpec((rows, width), lambda j, where: (0, jnp.maximum(j - (fields - 1), 0)))] * outs,
            scratch_shapes=[pltpu.VMEM((outs, count, side, width), F32)] * fields,
        ),
        compiler_params=params(24),
        cost_estimate=cost(2 * size * side * group, size * 2 * (group + outs) + table.size * 2),
    )(where, *flat, scales, table, *after)


def scales_of(position, group, rows):
    distances = jnp.arange(group, dtype=jnp.int32)
    return (minus_one_to(position) * minus_one_to(position & distances)).astype(F32) / math.sqrt(rows * group)


def rotate_and_right(blocks, table, lefts, position, plane):
    group = len(blocks)
    pieces = [len(block) for block in blocks]
    rows = blocks[0][0].shape[0]
    rank = lefts[0].shape[1]
    columns = blocks[-1][0].shape[1]
    _, count, side, _ = table.shape
    width = tile_width(columns)
    tiles = columns // width
    each = count // PLANE
    strip = side // count
    where = jnp.stack([position, plane >> 1])

    def body(where_ref, *refs):
        at, block_refs = 0, []
        for number in pieces:
            block_refs.append(refs[at : at + number])
            at += number
        scale_ref, table_ref = refs[at : at + 2]
        left_refs, out_refs = refs[at + 2 : at + 2 + group], refs[at + 2 + group : at + 2 + 2 * group]
        right_ref, even_ref, odd_ref, flat_ref = refs[-4:]
        step = pl.program_id(0)
        shown = jnp.maximum(step - 1, 0) * width

        def block_rows(d, number, first, size):
            if pieces[d] > 1:
                return block_refs[d][1 - number][pl.ds(first, size), :]
            pair = rows // 2
            start = pl.multiple_of((where_ref[1] ^ number) * pair + first, side)
            return block_refs[d][0][pl.ds(start, size), :]

        def mix(number, inside, field_ref):
            b = (where_ref[1] ^ number) * (count // 2) + inside
            first = pl.multiple_of(inside * side, side)
            parts = [
                jnp.dot(table_ref[d, b], block_rows(d, number, first, side), preferred_element_type=F32)
                for d in range(group)
            ]
            for o, mixed in enumerate(butterflies(parts)):
                field_ref[o, b] = mixed

        def spread(i, field_ref):
            for part in range(0, strip, 16):
                inner = pl.multiple_of(i * strip + part, 16)
                for o in range(group):
                    for start in range(0, width, 128):
                        lanes = slice(start, start + 128)
                        values = butterflies([field_ref[o, b, pl.ds(inner, 16), lanes] for b in range(count)])
                        if o == 0:
                            lanes = pl.ds(pl.multiple_of(shown + start, 128), 128)
                        for b in range(count):
                            turned = (values[b] * scale_ref[o]).astype(BF16)
                            out_refs[o][pl.ds(pl.multiple_of(b * side + inner, 16), 16), lanes] = turned

        def sweep(mixed_ref, spread_ref):
            for number in range(2):

                @pl.loop(0, count // 2, unroll=2)
                def _(inside, number=number):
                    mix(number, inside, mixed_ref)
                    spread(number * (count // 2) + inside, spread_ref)

        @pl.when(step == 0)
        def _():
            for d in range(group):
                flat_ref[d] = left_refs[d][...].T

        total = jnp.zeros((rank, width), F32)
        for d in range(group):
            for number in range(2):
                first = pl.multiple_of((where_ref[1] ^ number) * (rows // 2), 128)
                flat = flat_ref[d, :, pl.ds(first, rows // 2)]
                total += jnp.dot(flat, block_rows(d, number, 0, rows // 2), preferred_element_type=F32)
        right_ref[...] = total

        @pl.when(step % 2 == 0)
        def _():
            sweep(even_ref, odd_ref)

        @pl.when(step % 2 == 1)
        def _():
            sweep(odd_ref, even_ref)

    def place(piece):
        def index(j, where):
            j = jnp.minimum(j, tiles - 1)
            return 0, j if piece.shape[1] == columns else where[0] * tiles + j

        return pl.BlockSpec((piece.shape[0], width), index)

    flat = [piece for block in blocks for piece in block]
    field = pltpu.VMEM((group, count, side, width), F32)
    size = rows * columns
    return pl.pallas_call(
        body,
        out_shape=[pltpu.VMEM((rows, columns), BF16)]
        + [jax.ShapeDtypeStruct((rows, columns), BF16)] * (group - 1)
        + [jax.ShapeDtypeStruct((rank, columns), F32)],
        grid_spec=pltpu.PrefetchScalarGridSpec(
            num_scalar_prefetch=1,
            grid=(tiles + 1,),
            in_specs=[place(piece) for piece in flat] + [SMEM, VMEM] + [VMEM] * group,
            out_specs=[VMEM]
            + [pl.BlockSpec((rows, width), lambda j, where: (0, jnp.maximum(j - 1, 0)))] * (group - 1)
            + [pl.BlockSpec((rank, width), lambda j, where: (0, jnp.minimum(j, tiles - 1)))],
            scratch_shapes=[field, field, pltpu.VMEM((group, rank, rows), BF16)],
        ),
        compiler_params=params(38),
        cost_estimate=cost(2 * size * (side + rank) * group, size * 2 * (2 * group - 1) + table.size * 2),
    )(where, *flat, scales_of(position, group, rows), table, *lefts)


def project(accumulated, q_start, piece_at, position, group, pieces, out_type, after, copies):
    rows, columns = accumulated.shape
    rank = q_start.shape[1]
    share = columns // group
    piece = rows // pieces
    tall = min(512, piece)
    steps = piece // tall

    def body(where_ref, a_ref, q_ref, *refs):
        out_refs = refs[len(after) + len(copies) :]
        out_refs[0][...] = jnp.dot(a_ref[...], q_ref[...], preferred_element_type=F32).astype(out_type)
        for d in range(1, group):
            lanes = pl.ds(pl.multiple_of((where_ref[1] ^ d) * share, 128), share)
            out_refs[d][...] = a_ref[:, lanes]

    return pl.pallas_call(
        body,
        out_shape=[jax.ShapeDtypeStruct((piece, rank), out_type)]
        + [jax.ShapeDtypeStruct((2 * piece, share), BF16)] * (group - 1),
        grid_spec=pltpu.PrefetchScalarGridSpec(
            num_scalar_prefetch=1,
            grid=(steps,),
            in_specs=[
                pl.BlockSpec((tall, columns), lambda i, where: (where[0] * steps + i, 0)),
                pl.BlockSpec((columns, rank), lambda i, where: (0, 0)),
            ]
            + [ANY] * (len(after) + len(copies)),
            out_specs=[pl.BlockSpec((tall, rank), lambda i, where: (i, 0))]
            + [pl.BlockSpec((tall, share), lambda i, where: ((where[0] & 1) * steps + i, 0))] * (group - 1),
        ),
        input_output_aliases={3 + len(after) + d: 1 + d for d in range(len(copies))},
        compiler_params=params(24),
        cost_estimate=cost(2 * piece * columns * rank, piece * columns * 3),
    )(jnp.stack([piece_at, position]), accumulated, q_start, *after, *copies)


def split_sum(own, others, place, pieces):
    rows, rank = own.shape
    piece = rows // pieces

    def body(where_ref, own_ref, *refs):
        other_refs, out_refs = refs[: len(others)], refs[len(others) :]
        for d in range(pieces):
            at = pl.ds(pl.multiple_of((where_ref[0] ^ d) * piece, piece), piece)
            total = own_ref[at, :]
            for ref in other_refs:
                total += ref[at, :].astype(F32)
            out_refs[d][...] = total.astype(out_refs[d].dtype)

    return pl.pallas_call(
        body,
        out_shape=[jax.ShapeDtypeStruct((piece, rank), F32 if d == 0 else BF16) for d in range(pieces)],
        in_specs=[pl.BlockSpec(memory_space=pltpu.SMEM)] + [pl.BlockSpec(memory_space=pltpu.VMEM)] * (1 + len(others)),
        out_specs=[pl.BlockSpec(memory_space=pltpu.VMEM)] * pieces,
        compiler_params=params(24),
    )(place.reshape(1), own, *others)


def assemble(parts, place, after=()):
    rows, rank = parts[0].shape
    count = len(parts)

    def body(where_ref, *refs):
        out_ref = refs[-1]
        for d in range(count):
            at = pl.ds(pl.multiple_of((where_ref[0] ^ d) * rows, rows), rows)
            out_ref[at, :] = refs[d][...]

    return pl.pallas_call(
        body,
        out_shape=jax.ShapeDtypeStruct((rows * count, rank), parts[0].dtype),
        in_specs=[pl.BlockSpec(memory_space=pltpu.SMEM)]
        + [pl.BlockSpec(memory_space=pltpu.VMEM)] * count
        + [ANY] * len(after),
        out_specs=pl.BlockSpec(memory_space=pltpu.VMEM),
        compiler_params=params(24),
    )(place.reshape(1), *parts, *after)


def right_piece(accumulated, left, piece_at, position, shares, earlier):
    rows, columns = accumulated.shape
    piece, rank = left.shape
    share = columns // shares
    width = 896 if share % 896 == 0 else tile_width(share)
    steps = columns // width
    each = steps // shares

    def body(where_ref, a_ref, left_ref, *refs):
        out_refs, gram_ref, turned_ref = refs[len(earlier) : -2], refs[-2], refs[-1]
        at = pl.program_id(0)

        @pl.when(at == 0)
        def _():
            turned_ref[...] = left_ref[...].T
            gram_ref[...] = jnp.dot(turned_ref[...], left_ref[...], preferred_element_type=F32)

        total = jnp.dot(turned_ref[...], a_ref[...], preferred_element_type=F32)
        if earlier:
            total += refs[0][...]
        for d in range(shares):

            @pl.when(at // each == where_ref[1] ^ d)
            def _(d=d):
                out_refs[d][...] = total

    def out_place(d):
        return pl.BlockSpec((rank, width), lambda j, where: (0, jnp.clip(j - (where[1] ^ d) * each, 0, each - 1)))

    whole = pl.BlockSpec((rank, width), lambda j, where: (0, j))
    return pl.pallas_call(
        body,
        out_shape=[jax.ShapeDtypeStruct((rank, share), F32)] * shares + [jax.ShapeDtypeStruct((rank, rank), F32)],
        grid_spec=pltpu.PrefetchScalarGridSpec(
            num_scalar_prefetch=1,
            grid=(steps,),
            in_specs=[
                pl.BlockSpec((piece, width), lambda j, where: (where[0], j)),
                pl.BlockSpec((piece, rank), lambda j, where: (0, 0)),
            ]
            + [whole] * len(earlier),
            out_specs=([out_place(d) for d in range(shares)] if shares > 1 else [whole])
            + [pl.BlockSpec((rank, rank), lambda j, where: (0, 0))],
            scratch_shapes=[pltpu.VMEM((rank, piece), BF16)],
        ),
        compiler_params=params(24),
        cost_estimate=cost(2 * piece * columns * rank, piece * columns * 2),
    )(jnp.stack([piece_at, position if shares > 1 else jnp.zeros_like(position)]), accumulated, left, *earlier)


def halves(value):
    high = value.astype(BF16)
    return high, (value - high.astype(F32)).astype(BF16)


def inverse_factor(gram):
    rank = gram.shape[0]
    lane = lax.broadcasted_iota(jnp.int32, (8, rank), 1)
    row = lax.broadcasted_iota(jnp.int32, (8, rank), 0)
    left = [gram[start : start + 8, :] for start in range(0, rank, 8)]
    right = [jnp.where(lane == row + start, 1.0, 0.0).astype(F32) for start in range(0, rank, 8)]
    scales = [jnp.zeros((8, rank), F32)] * len(left)
    for k in range(rank):
        home, inside = divmod(k, 8)
        pivot_row = left[home][inside : inside + 1, :]
        pivot = left[home][inside : inside + 1, k : k + 1]
        made_row = right[home][inside : inside + 1, :]
        inverse = 1.0 / pivot
        scales[home] = jnp.where(row == inside, lax.rsqrt(jnp.broadcast_to(pivot, (8, rank))), scales[home])
        pivot_row, made_row = pivot_row * inverse, made_row * inverse
        for block in range(home, len(left)):
            if block == home and inside == 7:
                continue
            factor = jnp.broadcast_to(left[block][:, k : k + 1], (8, rank))
            if block == home:
                factor = jnp.where(row > inside, factor, 0.0)
            left[block] = left[block] - factor * pivot_row
            right[block] = right[block] - factor * made_row
    return jnp.concatenate([part * scale for part, scale in zip(right, scales)], axis=0)


def basis_of(blocks, table, position):
    group = len(blocks)
    rows, rank = blocks[0].shape
    _, count, side, _ = table.shape

    def body(*refs):
        block_refs, scale_ref, table_ref = refs[:group], refs[group], refs[group + 1]
        inverse_ref, basis_ref, basis16_ref, field_ref, turned_ref = refs[group + 2 :]

        @pl.loop(0, count, unroll=4)
        def _(b):
            at = pl.ds(pl.multiple_of(b * side, side), side)
            mixed = jnp.dot(table_ref[0, b], block_refs[0][at, :], preferred_element_type=F32)
            for d in range(1, group):
                mixed += jnp.dot(table_ref[d, b], block_refs[d][at, :], preferred_element_type=F32)
            field_ref[b] = mixed

        @pl.loop(0, side // 16, unroll=2)
        def _(i):
            inner = pl.multiple_of(i * 16, 16)
            values = butterflies([field_ref[b, pl.ds(inner, 16), :] for b in range(count)])
            for b in range(count):
                turned_ref[pl.ds(pl.multiple_of(b * side + inner, 16), 16), :] = values[b] * scale_ref[0]

        grams = [jnp.dot(ref[...].T, ref[...], preferred_element_type=F32) for ref in block_refs]
        while len(grams) > 1:
            grams = [low + high for low, high in zip(grams[::2], grams[1::2])]
        inverse = inverse_factor(grams[0])
        inverse_ref[...] = inverse
        high, low = halves(inverse.T)
        turned_high, turned_low = halves(turned_ref[...])
        both = jnp.concatenate([turned_high, turned_low], axis=1)
        basis = jnp.dot(both, jnp.concatenate([high, high], axis=0), preferred_element_type=F32)
        basis += jnp.dot(turned_high, low, preferred_element_type=F32)
        basis_ref[...] = basis
        basis16_ref[...] = basis.astype(BF16)

    return pl.pallas_call(
        body,
        out_shape=[
            jax.ShapeDtypeStruct((rank, rank), F32),
            jax.ShapeDtypeStruct((rows, rank), F32),
            jax.ShapeDtypeStruct((rows, rank), BF16),
        ],
        in_specs=[VMEM] * group + [SMEM, VMEM],
        out_specs=[VMEM] * 3,
        scratch_shapes=[pltpu.VMEM((count, side, rank), F32), pltpu.VMEM((rows, rank), F32)],
        compiler_params=params(28),
        cost_estimate=cost(8 * 10**9, 60 * 10**6),
    )(*blocks, scales_of(position, group, rows), table)


def residual(rotated, basis16, right16, columns, owner, into=None, resident=False):
    rows, share = rotated.shape
    rank = right16.shape[0]
    tall = min(512, rows)
    earlier = () if into is None else (into,)

    def body(where_ref, rotated_ref, basis_ref, right_ref, *refs):
        out_ref = refs[-1]
        part = slice(None)
        if resident:
            part = pl.ds(pl.multiple_of(pl.program_id(0) * tall, tall), tall)
        for start in range(0, share, 256):
            lanes = slice(start, min(start + 256, share))
            approx = jnp.dot(basis_ref[...], right_ref[:, lanes], preferred_element_type=F32)
            out_ref[:, lanes] = (rotated_ref[part, lanes].astype(F32) - approx).astype(out_ref.dtype)

    return pl.pallas_call(
        body,
        out_shape=jax.ShapeDtypeStruct((rows, columns), BF16),
        grid_spec=pltpu.PrefetchScalarGridSpec(
            num_scalar_prefetch=1,
            grid=(rows // tall,),
            in_specs=[
                VMEM if resident else pl.BlockSpec((tall, share), lambda i, where: (i, 0)),
                pl.BlockSpec((tall, rank), lambda i, where: (i, 0)),
                pl.BlockSpec((rank, share), lambda i, where: (0, 0)),
            ]
            + [ANY] * len(earlier),
            out_specs=pl.BlockSpec((tall, share), lambda i, where: (i, where[0])),
        ),
        input_output_aliases={4: 0} if earlier else {},
        compiler_params=params(32 if resident else 16),
        cost_estimate=cost(2 * rows * share * rank, rows * share * 4),
    )(owner.reshape(1), rotated, basis16, right16, *earlier)


def from_distance(block, axis, distance):
    count = lax.axis_size(axis)
    return lax.ppermute(block, axis, [(p, p ^ distance) for p in range(count)])


def from_plane(block, distance):
    count, mp_count = REPLICAS * lax.axis_size("mp"), lax.axis_size("mp")
    change = (distance & 1) | (distance >> 1) * mp_count
    return lax.ppermute(block, ("rep", "mp"), [(p, p ^ change) for p in range(count)])


def from_line(block, distance):
    return from_distance(block, "mp", distance << 1)


def local(accumulated, signs, q_start):
    rows, columns = accumulated.shape
    rank = q_start.shape[1]
    group = lax.axis_size("pos")
    position = lax.axis_index("pos")
    mp_index = lax.axis_index("mp")
    plane = lax.axis_index("rep") * 2 + (mp_index & 1)
    line, lines = mp_index >> 1, lax.axis_size("mp") // 2
    share = columns // group
    shared = share % 128 == 0 and rows % (256 * PLANE) == 0
    others = range(1, group)

    came, after, copies = [], (), []
    other_pieces = [[] for _ in others]
    for d in reversed(range(PLANE)):
        out_type = BF16 if d else F32
        part, *copies = project(
            accumulated, q_start, plane ^ d, position, group if shared else 1, PLANE, out_type, after, copies
        )
        after = (part,)
        if d:
            came.append(from_plane(part, d))
        if d == 1:
            after = (part, came[0])
        if d % 2 == 0:
            for e, copy in enumerate(copies):
                other_pieces[e].append(from_distance(copy, "pos", e + 1))
            copies = []
    table = signed_hadamard(signs, position, group, rows)
    if not shared:
        other_pieces = [[from_distance(accumulated, "pos", d)] for d in others]
    blocks = [[accumulated]] + other_pieces

    own, *sent = split_sum(part, came, line, lines)
    came = [from_line(sent[d - 1], d) for d in range(1, lines)]
    mine16 = sum([part.astype(F32) for part in came], own).astype(BF16)
    near16 = assemble([mine16] + [from_line(mine16, d) for d in range(1, lines)], line)
    far16 = [near16] + [from_plane(near16, d) for d in range(1, PLANE)]
    own16 = assemble(far16, plane)
    around16 = [own16] + [from_distance(own16, "pos", d) for d in others]

    if shared:
        *rotated, half = rotate_and_right(blocks, table, around16, position, plane)
        half = half.astype(BF16)
        rotated = rotated[:1] + [from_distance(part, "pos", d + 1) for d, part in enumerate(rotated[1:])]
        half = half.astype(F32) + from_distance(half, "rep", 1).astype(F32)
    else:
        rotated = rotate(blocks, table, position, plane, BF16, 1)
        totals = []
        for d in range(PLANE):
            *totals, _ = right_piece(accumulated, far16[d], plane ^ d, position, 1, totals)
        half = lax.psum(totals[0], ("rep", "pos"))
    inverse, p_basis, basis16 = basis_of(around16, table, position)

    right = jnp.dot(inverse, half, precision=lax.Precision.HIGHEST) / REPLICAS
    if not shared:
        new_error = residual(rotated[0], basis16, right.astype(BF16), columns, jnp.zeros((), jnp.int32))
        return (new_error, p_basis, right.T)
    new_error = None
    rights = [right] + [from_distance(right, "pos", d) for d in others]
    for d in range(group):
        new_error = residual(
            rotated[d], basis16, rights[d].astype(BF16), columns, position ^ d, new_error, d == 0
        )
    q_factor = jnp.zeros((columns, rank), F32)
    for d in range(group):
        q_factor = lax.dynamic_update_slice_in_dim(q_factor, rights[d].T, (position ^ d) * share, 0)
    return (new_error, p_basis, q_factor)


def solution(mesh):
    dp_count, mp_count = mesh.shape["dp"], mesh.shape["mp"]
    fine = Mesh(
        mesh.devices.reshape(REPLICAS, dp_count // REPLICAS, mp_count), ("rep", "pos", "mp")
    )
    rows_of = ("rep", "pos")
    in_specs = (P(rows_of, "mp"), P(), P("mp", None))
    out_specs = (P(rows_of, "mp"), P(rows_of, None), P("mp", None))
    return jax.shard_map(local, mesh=fine, in_specs=in_specs, out_specs=out_specs, check_vma=False)
```

time: 217 us -> 166 us (0.76)
  other arithmetic: 28.8 us -> 3.8 us
  Pallas kernels: 117 us -> 102 us
  waiting for transfers between devices: 35 us -> 24.9 us
  matrix products: 9.31 us -> 0.92 us
  local copies, waits for them, and re-layouts: 6.79 us -> 13.3 us
    another operation x5 -> x4, other arithmetic: 22.8 us -> 0.3 us  [the longest x3 0.23 us: project(): jnp.stack([piece_at, position])]
    pallas_call x2, Pallas kernels: 30.7 us -> 22.4 us  [residual(): pl.pallas_call(body, out_shape=jax.ShapeDtypeStruct((rows, columns), BF16...]
    ppermute x6, waiting for transfers between devices: 24 us -> 16 us  [from_plane(): lax.ppermute(block, ('rep', 'mp'), [(p, p ^ change) for p in range(count)])]
    dot_general x2 -> x0, matrix products: 7.36 us -> none  [the longest x1 5.06 us: local(): p_basis = jnp.dot(turned, inverse.T, precision=lax.Precision.HIGHEST)]
    unnamed x38 -> x20, local copies, waits for them, and re-layouts: 4.94 us -> 10.6 us
    pallas_call x2, Pallas kernels: 3.88 us -> 0.09 us  [assemble(): pl.pallas_call(body, out_shape=jax.ShapeDtypeStruct((rows * count, rank),...]
    ppermute x11 -> x12, waiting for transfers between devices: 11 us -> 8.96 us  [from_distance(): return lax.ppermute(block, axis, [(p, p ^ distance) for p in range(count)])]
    pallas_call x5 -> x6, Pallas kernels: 80.1 us -> 79.2 us  [the longest x1 38 us: rotate_and_right(): pl.pallas_call(body, out_shape=[pltpu.VMEM((rows, columns), BF16)] + [jax...]
  transfers between devices with their start and end apart: 17 -> 18, of which waited for: 10 -> 10; matrix products, arithmetic and copies ran while one was open for 18% -> 4% of each run, Pallas kernels for 19% -> 26%
where the time goes in v3:
time: 166 us; the launch traced here: 165 us
  Pallas kernels  102 us (61%)
  waiting for transfers between devices  24.9 us (15%)
  starting transfers between devices  19.7 us (12%)
  local copies, waits for them, and re-layouts  13.3 us (8%)
  other arithmetic  3.8 us (2%)
    pallas_call x1, Pallas kernels, rotate_and_right(): pl.pallas_call(body, out_shape=[pltpu.VMEM((rows, columns), BF16)] + [jax...  38 us
    pallas_call x4, Pallas kernels, project(): pl.pallas_call(body, out_shape=[jax.ShapeDtypeStruct((piece, rank), out_t...  24.5 us
    pallas_call x2, Pallas kernels, residual(): pl.pallas_call(body, out_shape=jax.ShapeDtypeStruct((rows, columns), BF16...  22.4 us
    pallas_call x1, Pallas kernels, basis_of(): pl.pallas_call(body, out_shape=[jax.ShapeDtypeStruct((rank, rank), F32),...  16.7 us
    ppermute x6, waiting for transfers between devices, from_plane(): lax.ppermute(block, ('rep', 'mp'), [(p, p ^ change) for p in range(count)])  16 us
    ppermute x12, starting transfers between devices, from_distance(): return lax.ppermute(block, axis, [(p, p ^ distance) for p in range(count)])  11.7 us
    unnamed x20, local copies, waits for them, and re-layouts  10.6 us
    ppermute x12, waiting for transfers between devices, from_distance(): return lax.ppermute(block, axis, [(p, p ^ distance) for p in range(count)])  8.96 us
  transfers between devices with their start and end apart: 18, of which 10 were waited for; matrix products, arithmetic and copies ran while one was open for 4% of the time, Pallas kernels for 26%

profile of v3, /device:TPU:0, one launch (start us, length us, event | category | flops | bytes accessed | tf_op | source)
XLA Modules:
  0.0 165.3 jit_solution(5018435841191045555)
XLA Ops:
  0.7 1.2 copy-done.3
  1.9 6.1 %shard_map.58 = (bf16[1024,128]{1,0:T(8,128)(2,1)S(1)}, bf16[2048,1792]{1,0:T(8,128)(2,1)}) custom-call(s32[2]{0:T(128)S(1)} %get-tuple-element.44.where_ref, bf16[4096,3584]{1,0:T(8,128)(2,1)} %refs_0_.1, bf16[3584,128]{1,0:T(8,128)(2,1)S(1)} %copy-done.3), custom_call_target="tpu_custom_call" | custom-call | flops 939524096 | bytes 11010048 | tf_op jit(solution)/shard_map/pallas_call | solution.py:309
  8.0 3.9 %collective-permute-start.1 = (bf16[1024,128]{1,0:T(8,128)(2,1)S(1)}, bf16[1024,128]{1,0:T(8,128)(2,1)S(1)}, u32[]{:S(2)}, u32[]{:S(2)}) collective-permute-start(bf16[1024,128]{1,0:T(8,128)(2,1)S(1)} %get-tuple-element.21.refs_0_), channel_id=1, source_target_pairs={{0,17},{1,16},{2,19},{3,18},{4,21},{5,20},{6,23},{7,22},{16,1},{17... | collective-permute-start | bytes 786440 | tf_op jit(solution)/shard_map/ppermute | solution.py:550
  11.9 6.1 %shard_map.59 = (bf16[1024,128]{1,0:T(8,128)(2,1)S(1)}, bf16[2048,1792]{1,0:T(8,128)(2,1)}) custom-call(s32[2]{0:T(128)S(1)} %get-tuple-element.43.where_ref, bf16[4096,3584]{1,0:T(8,128)(2,1)} %refs_0_.1, bf16[3584,128]{1,0:T(8,128)(2,1)S(1)} %copy-done.4, bf16[1024,128]{1,0:T(8,128)(2,1)S(1)} %get-tuple-element.21.refs_0_, ...), custom_call_target="tpu_custom_call", output_to_operand_aliasing={{1}: (4, {})} | custom-call | flops 939524096 | bytes 11010048 | tf_op jit(solution)/shard_map/pallas_call | solution.py:309
  18.1 6.1 %shard_map.60 = (bf16[1024,128]{1,0:T(8,128)(2,1)S(1)}, bf16[2048,1792]{1,0:T(8,128)(2,1)}) custom-call(s32[2]{0:T(128)S(1)} %pad_add_fusion.4.where_ref, bf16[4096,3584]{1,0:T(8,128)(2,1)} %refs_0_.1, bf16[3584,128]{1,0:T(8,128)(2,1)S(1)} %copy-done.4, bf16[1024,128]{1,0:T(8,128)(2,1)S(1)} %get-tuple-element.24.refs_0_), custom_call_target="tpu_custom_call" | custom-call | flops 939524096 | bytes 11010048 | tf_op jit(solution)/shard_map/pallas_call | solution.py:309
  24.4 6.1 %shard_map.61 = (f32[1024,128]{1,0:T(8,128)S(1)}, bf16[2048,1792]{1,0:T(8,128)(2,1)}) custom-call(s32[2]{0:T(128)S(1)} %pad_add_fusion.3.where_ref, bf16[4096,3584]{1,0:T(8,128)(2,1)} %refs_0_.1, bf16[3584,128]{1,0:T(8,128)(2,1)S(1)} %copy-done.4, bf16[1024,128]{1,0:T(8,128)(2,1)S(1)} %get-tuple-element.25.refs_0_, ...), custom_call_target="tpu_custom_call", output_to_operand_aliasing={{1}: (5, {})} | custom-call | flops 939524096 | bytes 11010048 | tf_op jit(solution)/shard_map/pallas_call | solution.py:309
  31.6 7.6 %collective-permute-done.3.refs_1_ = bf16[1024,128]{1,0:T(8,128)(2,1)S(1)} collective-permute-done((bf16[1024,128]{1,0:T(8,128)(2,1)S(1)}, bf16[1024,128]{1,0:T(8,128)(2,1)S(1)}, u32[]{:S(2)}, u32[]{:S(2)}) %collective-permute-start.3) | collective-permute-done | bytes 262176 | tf_op jit(solution)/shard_map/ppermute | solution.py:550
  39.6 1.6 collective-permute-start.5
  41.2 2.6 %collective-permute-start.6 = (bf16[256,128]{1,0:T(8,128)(2,1)S(1)}, bf16[256,128]{1,0:T(8,128)(2,1)S(1)}, u32[]{:S(2)}, u32[]{:S(2)}) collective-permute-start(bf16[256,128]{1,0:T(8,128)(2,1)S(1)} %get-tuple-element.31), channel_id=1, source_target_pairs={{0,4},{1,5},{2,6},{3,7},{4,0},{5,1},{6,2},{7,3},{8,12},{9,13},{10,... | collective-permute-start | bytes 196616 | tf_op jit(solution)/shard_map/ppermute | solution.py:544
  44.5 3.2 %collective-permute-done.6 = bf16[256,128]{1,0:T(8,128)(2,1)S(1)} collective-permute-done((bf16[256,128]{1,0:T(8,128)(2,1)S(1)}, bf16[256,128]{1,0:T(8,128)(2,1)S(1)}, u32[]{:S(2)}, u32[]{:S(2)}) %collective-permute-start.6) | collective-permute-done | bytes 65568 | tf_op jit(solution)/shard_map/ppermute | solution.py:544
  47.8 2.1 %collective-permute-done.7 = bf16[256,128]{1,0:T(8,128)(2,1)S(1)} collective-permute-done((bf16[256,128]{1,0:T(8,128)(2,1)S(1)}, bf16[256,128]{1,0:T(8,128)(2,1)S(1)}, u32[]{:S(2)}, u32[]{:S(2)}) %collective-permute-start.7) | collective-permute-done | bytes 65568 | tf_op jit(solution)/shard_map/ppermute | solution.py:544
  49.9 1.1 collective-permute-start.10
  51.5 2.9 %collective-permute-start.8 = (bf16[256,128]{1,0:T(8,128)(2,1)S(1)}, bf16[256,128]{1,0:T(8,128)(2,1)S(1)}, u32[]{:S(2)}, u32[]{:S(2)}) collective-permute-start(bf16[256,128]{1,0:T(8,128)(2,1)S(1)} %add_convert_fusion.refs_0_), channel_id=1, source_target_pairs={{0,2},{1,3},{2,0},{3,1},{4,6},{5,7},{6,4},{7,5},{8,10},{9,11},{10,... | collective-permute-start | bytes 196616 | tf_op jit(solution)/shard_map/ppermute | solution.py:544
  54.4 1.7 %collective-permute-done.10.refs_3_ = bf16[256,128]{1,0:T(8,128)(2,1)S(1)} collective-permute-done((bf16[256,128]{1,0:T(8,128)(2,1)S(1)}, bf16[256,128]{1,0:T(8,128)(2,1)S(1)}, u32[]{:S(2)}, u32[]{:S(2)}) %collective-permute-start.10) | collective-permute-done | bytes 65568 | tf_op jit(solution)/shard_map/ppermute | solution.py:544
  56.1 1.3 collective-permute-done.9.refs_2_
  57.5 1.5 collective-permute-start.13
  59.5 1.5 collective-permute-start.11
  61.1 5.4 %collective-permute-done.13.refs_3_ = bf16[1024,128]{1,0:T(8,128)(2,1)S(1)} collective-permute-done((bf16[1024,128]{1,0:T(8,128)(2,1)S(1)}, bf16[1024,128]{1,0:T(8,128)(2,1)S(1)}, u32[]{:S(2)}, u32[]{:S(2)}) %collective-permute-start.13) | collective-permute-done | bytes 262176 | tf_op jit(solution)/shard_map/ppermute | solution.py:550
  66.5 1.7 %collective-permute-done.12.refs_2_ = bf16[1024,128]{1,0:T(8,128)(2,1)S(1)} collective-permute-done((bf16[1024,128]{1,0:T(8,128)(2,1)S(1)}, bf16[1024,128]{1,0:T(8,128)(2,1)S(1)}, u32[]{:S(2)}, u32[]{:S(2)}) %collective-permute-start.12) | collective-permute-done | bytes 262176 | tf_op jit(solution)/shard_map/ppermute | solution.py:550
  69.5 3.3 %multiply_convert_fusion.refs_4_.refs_3_ = bf16[2,16,256,256]{3,2,1,0:T(8,128)(2,1)} fusion(f32[2,16,256]{2,1,0:T(8,128)S(1)} %add_convert_fusion.1, f32[256,256]{1,0:T(8,128)S(1)} %subtract_convert_fusion), kind=kLoop, calls=%fused_computation | loop fusion | flops 4194304 | bytes 4489216 | tf_op jit(solution)/shard_map/convert_element_type | solution.py:62
  72.8 1.0 copy-done.5
  73.8 38.0 %shard_map.65 = (bf16[4096,1792]{1,0:T(8,128)(2,1)S(1)}, bf16[4096,1792]{1,0:T(8,128)(2,1)}, f32[128,1792]{1,0:T(8,128)S(1)}) custom-call(s32[2]{0:T(128)S(1)} %pad_add_fusion.where_ref, bf16[4096,3584]{1,0:T(8,128)(2,1)} %refs_0_.1, bf16[2048,1792]{1,0:T(8,128)(2,1)} %collective-permute-done.refs_1_, bf16[2048,1792]{1,0:T(8,128)(2,1)} %collective-permute-done.2.refs_2_, ...), custom_call_target="tpu_custom_call" | custom-call | flops 11274289152 | bytes 48234496 | tf_op jit(solution)/shard_map/pallas_call | solution.py:275
  112.3 1.5 collective-permute-start.16
  113.9 2.0 %copy-done.6 = bf16[4096,128]{1,0:T(8,128)(2,1)S(1)} copy-done((bf16[4096,128]{1,0:T(8,128)(2,1)S(1)}, bf16[4096,128]{1,0:T(8,128)(2,1)}, u32[]{:S(2)}) %copy-start.6) | copy-done | bytes 1048600
  115.9 16.7 %shard_map.66 = (f32[128,128]{1,0:T(8,128)S(1)}, f32[4096,128]{1,0:T(8,128)}, bf16[4096,128]{1,0:T(8,128)(2,1)S(1)}) custom-call(bf16[4096,128]{1,0:T(8,128)(2,1)S(1)} %shard_map.64.refs_5_.refs_0_, bf16[4096,128]{1,0:T(8,128)(2,1)S(1)} %copy-done.6, f32[2]{0:T(128)S(1)} %convert_multiply_fusion.refs_3_.refs_2_, bf16[2,16,256,256]{3,2,1,0:T(8,128)(2,1)S(1)} %copy-done), custom_call_target="tpu_custom_call" | custom-call | flops 8000000000 | bytes 60000000 | tf_op jit(solution)/shard_map/pallas_call | solution.py:491
  132.6 0.9 fusion.3
  133.7 1.2 copy.9
  134.9 5.2 %copy-done.2 = bf16[4096,1792]{1,0:T(8,128)(2,1)S(1)} copy-done((bf16[4096,1792]{1,0:T(8,128)(2,1)S(1)}, bf16[4096,1792]{1,0:T(8,128)(2,1)}, u32[]{:S(2)}) %copy-start.2) | copy-done | bytes 14680088
  140.1 8.0 %shard_map.67.refs_0_ = bf16[4096,3584]{1,0:T(8,128)(2,1)} custom-call(s32[1]{0:T(128)} %bitcast.1.where_ref, bf16[4096,1792]{1,0:T(8,128)(2,1)S(1)} %copy-done.2, bf16[4096,128]{1,0:T(8,128)(2,1)S(1)} %get-tuple-element.34.basis_ref, bf16[128,1792]{1,0:T(8,128)(2,1)S(1)} %get-tuple-element.41.right_ref), custom_call_target="tpu_custom_call" | custom-call | flops 1879048192 | bytes 29360128 | tf_op jit(solution)/shard_map/pallas_call | solution.py:522
  148.3 1.2 copy-done.8
  149.9 1.0 constant_dynamic-update-slice_fusion
  150.9 14.4 %shard_map.68 = bf16[4096,3584]{1,0:T(8,128)(2,1)} custom-call(s32[1]{0:T(128)} %bitcast.where_ref, bf16[4096,1792]{1,0:T(8,128)(2,1)} %collective-permute-done.15.rotated_ref, bf16[4096,128]{1,0:T(8,128)(2,1)S(1)} %get-tuple-element.34.basis_ref, bf16[128,1792]{1,0:T(8,128)(2,1)S(1)} %convert_element_type.59.right_ref, ...), custom_call_target="tpu_custom_call", output_to_operand_aliasing={{}: (4, {})} | custom-call | flops 1879048192 | bytes 29360128 | tf_op jit(solution)/shard_map/pallas_call | solution.py:522
  (55 shorter events, 5.9 us)
Async XLA Ops:
  0.7 1.2 copy-start.3
  1.9 10.0 %copy-start.4 = (bf16[3584,128]{1,0:T(8,128)(2,1)S(1)}, bf16[3584,128]{1,0:T(8,128)(2,1)}, u32[]{:S(2)}) copy-start(bf16[3584,128]{1,0:T(8,128)(2,1)} %q_ref.7) | copy-start | bytes 2752516
  8.0 16.3 %collective-permute-start.1 = (bf16[1024,128]{1,0:T(8,128)(2,1)S(1)}, bf16[1024,128]{1,0:T(8,128)(2,1)S(1)}, u32[]{:S(2)}, u32[]{:S(2)}) collective-permute-start(bf16[1024,128]{1,0:T(8,128)(2,1)S(1)} %get-tuple-element.21.refs_0_), channel_id=1, source_target_pairs={{0,17},{1,16},{2,19},{3,18},{4,21},{5,20},{6,23},{7,22},{16,1},{17... | collective-permute-start | bytes 786440 | tf_op jit(solution)/shard_map/ppermute | solution.py:550
  18.1 54.7 %collective-permute-start = (bf16[2048,1792]{1,0:T(8,128)(2,1)}, bf16[2048,1792]{1,0:T(8,128)(2,1)}, u32[]{:S(2)}, u32[]{:S(2)}) collective-permute-start(bf16[2048,1792]{1,0:T(8,128)(2,1)} %get-tuple-element.23), channel_id=1, source_target_pairs={{0,8},{8,0},{1,9},{9,1},{2,10},{10,2},{3,11},{11,3},{4,12},{12,4},... | collective-permute-start | bytes 22020104 | tf_op jit(solution)/shard_map/ppermute | solution.py:544
  24.4 44.9 %copy-start.9 = (s32[8192]{0:T(1024)S(1)}, s32[8192]{0:T(1024)}, u32[]{:S(2)}) copy-start(s32[8192]{0:T(1024)} %param.4) | copy-start | bytes 98308
  30.5 42.3 %collective-permute-start.2 = (bf16[2048,1792]{1,0:T(8,128)(2,1)}, bf16[2048,1792]{1,0:T(8,128)(2,1)}, u32[]{:S(2)}, u32[]{:S(2)}) collective-permute-start(bf16[2048,1792]{1,0:T(8,128)(2,1)} %get-tuple-element.27), channel_id=1, source_target_pairs={{0,8},{8,0},{1,9},{9,1},{2,10},{10,2},{3,11},{11,3},{4,12},{12,4},... | collective-permute-start | bytes 22020104 | tf_op jit(solution)/shard_map/ppermute | solution.py:544
  31.0 8.2 %collective-permute-start.3 = (bf16[1024,128]{1,0:T(8,128)(2,1)S(1)}, bf16[1024,128]{1,0:T(8,128)(2,1)S(1)}, u32[]{:S(2)}, u32[]{:S(2)}) collective-permute-start(bf16[1024,128]{1,0:T(8,128)(2,1)S(1)} %get-tuple-element.24.refs_0_), channel_id=1, source_target_pairs={{0,16},{1,17},{2,18},{3,19},{4,20},{5,21},{6,22},{7,23},{16,0},{17... | collective-permute-start | bytes 786440 | tf_op jit(solution)/shard_map/ppermute | solution.py:550
  31.5 7.9 %collective-permute-start.4 = (bf16[1024,128]{1,0:T(8,128)(2,1)S(1)}, bf16[1024,128]{1,0:T(8,128)(2,1)S(1)}, u32[]{:S(2)}, u32[]{:S(2)}) collective-permute-start(bf16[1024,128]{1,0:T(8,128)(2,1)S(1)} %get-tuple-element.25.refs_0_), channel_id=1, source_target_pairs={{0,1},{1,0},{2,3},{3,2},{4,5},{5,4},{6,7},{7,6},{16,17},{17,16},{1... | collective-permute-start | bytes 786440 | tf_op jit(solution)/shard_map/ppermute | solution.py:550
  39.6 5.0 %collective-permute-start.5 = (bf16[256,128]{1,0:T(8,128)(2,1)S(1)}, bf16[256,128]{1,0:T(8,128)(2,1)S(1)}, u32[]{:S(2)}, u32[]{:S(2)}) collective-permute-start(bf16[256,128]{1,0:T(8,128)(2,1)S(1)} %get-tuple-element.30), channel_id=1, source_target_pairs={{0,2},{1,3},{2,0},{3,1},{4,6},{5,7},{6,4},{7,5},{8,10},{9,11},{10,... | collective-permute-start | bytes 196616 | tf_op jit(solution)/shard_map/ppermute | solution.py:544
  41.2 6.6 %collective-permute-start.6 = (bf16[256,128]{1,0:T(8,128)(2,1)S(1)}, bf16[256,128]{1,0:T(8,128)(2,1)S(1)}, u32[]{:S(2)}, u32[]{:S(2)}) collective-permute-start(bf16[256,128]{1,0:T(8,128)(2,1)S(1)} %get-tuple-element.31), channel_id=1, source_target_pairs={{0,4},{1,5},{2,6},{3,7},{4,0},{5,1},{6,2},{7,3},{8,12},{9,13},{10,... | collective-permute-start | bytes 196616 | tf_op jit(solution)/shard_map/ppermute | solution.py:544
  43.8 6.1 %collective-permute-start.7 = (bf16[256,128]{1,0:T(8,128)(2,1)S(1)}, bf16[256,128]{1,0:T(8,128)(2,1)S(1)}, u32[]{:S(2)}, u32[]{:S(2)}) collective-permute-start(bf16[256,128]{1,0:T(8,128)(2,1)S(1)} %get-tuple-element.32), channel_id=1, source_target_pairs={{0,6},{1,7},{2,4},{3,5},{4,2},{5,3},{6,0},{7,1},{8,14},{9,15},{10,... | collective-permute-start | bytes 196616 | tf_op jit(solution)/shard_map/ppermute | solution.py:544
  49.9 6.2 %collective-permute-start.10 = (bf16[256,128]{1,0:T(8,128)(2,1)S(1)}, bf16[256,128]{1,0:T(8,128)(2,1)S(1)}, u32[]{:S(2)}, u32[]{:S(2)}) collective-permute-start(bf16[256,128]{1,0:T(8,128)(2,1)S(1)} %add_convert_fusion.refs_0_), channel_id=1, source_target_pairs={{0,6},{1,7},{2,4},{3,5},{4,2},{5,3},{6,0},{7,1},{8,14},{9,15},{10,... | collective-permute-start | bytes 196616 | tf_op jit(solution)/shard_map/ppermute | solution.py:544
  51.1 6.4 %collective-permute-start.9 = (bf16[256,128]{1,0:T(8,128)(2,1)S(1)}, bf16[256,128]{1,0:T(8,128)(2,1)S(1)}, u32[]{:S(2)}, u32[]{:S(2)}) collective-permute-start(bf16[256,128]{1,0:T(8,128)(2,1)S(1)} %add_convert_fusion.refs_0_), channel_id=1, source_target_pairs={{0,4},{1,5},{2,6},{3,7},{4,0},{5,1},{6,2},{7,3},{8,12},{9,13},{10,... | collective-permute-start | bytes 196616 | tf_op jit(solution)/shard_map/ppermute | solution.py:544
  51.5 6.0 %collective-permute-start.8 = (bf16[256,128]{1,0:T(8,128)(2,1)S(1)}, bf16[256,128]{1,0:T(8,128)(2,1)S(1)}, u32[]{:S(2)}, u32[]{:S(2)}) collective-permute-start(bf16[256,128]{1,0:T(8,128)(2,1)S(1)} %add_convert_fusion.refs_0_), channel_id=1, source_target_pairs={{0,2},{1,3},{2,0},{3,1},{4,6},{5,7},{6,4},{7,5},{8,10},{9,11},{10,... | collective-permute-start | bytes 196616 | tf_op jit(solution)/shard_map/ppermute | solution.py:544
  57.5 9.0 %collective-permute-start.13 = (bf16[1024,128]{1,0:T(8,128)(2,1)S(1)}, bf16[1024,128]{1,0:T(8,128)(2,1)S(1)}, u32[]{:S(2)}, u32[]{:S(2)}) collective-permute-start(bf16[1024,128]{1,0:T(8,128)(2,1)S(1)} %shard_map.63.refs_0_), channel_id=1, source_target_pairs={{0,17},{1,16},{2,19},{3,18},{4,21},{5,20},{6,23},{7,22},{16,1},{17... | collective-permute-start | bytes 786440 | tf_op jit(solution)/shard_map/ppermute | solution.py:550
  59.0 9.2 %collective-permute-start.12 = (bf16[1024,128]{1,0:T(8,128)(2,1)S(1)}, bf16[1024,128]{1,0:T(8,128)(2,1)S(1)}, u32[]{:S(2)}, u32[]{:S(2)}) collective-permute-start(bf16[1024,128]{1,0:T(8,128)(2,1)S(1)} %shard_map.63.refs_0_), channel_id=1, source_target_pairs={{0,16},{1,17},{2,18},{3,19},{4,20},{5,21},{6,22},{7,23},{16,0},{17... | collective-permute-start | bytes 786440 | tf_op jit(solution)/shard_map/ppermute | solution.py:550
  59.5 9.6 %collective-permute-start.11 = (bf16[1024,128]{1,0:T(8,128)(2,1)S(1)}, bf16[1024,128]{1,0:T(8,128)(2,1)S(1)}, u32[]{:S(2)}, u32[]{:S(2)}) collective-permute-start(bf16[1024,128]{1,0:T(8,128)(2,1)S(1)} %shard_map.63.refs_0_), channel_id=1, source_target_pairs={{0,1},{1,0},{2,3},{3,2},{4,5},{5,4},{6,7},{7,6},{16,17},{17,16},{1... | collective-permute-start | bytes 786440 | tf_op jit(solution)/shard_map/ppermute | solution.py:550
  69.2 3.6 %collective-permute-start.14 = (bf16[4096,128]{1,0:T(8,128)(2,1)S(1)}, bf16[4096,128]{1,0:T(8,128)(2,1)S(1)}, u32[]{:S(2)}, u32[]{:S(2)}) collective-permute-start(bf16[4096,128]{1,0:T(8,128)(2,1)S(1)} %shard_map.64.refs_5_.refs_0_), channel_id=1, source_target_pairs={{0,8},{8,0},{1,9},{9,1},{2,10},{10,2},{3,11},{11,3},{4,12},{12,4},... | collective-permute-start | bytes 3145736 | tf_op jit(solution)/shard_map/ppermute | solution.py:544
  72.8 41.1 %copy-start = (bf16[2,16,256,256]{3,2,1,0:T(8,128)(2,1)S(1)}, bf16[2,16,256,256]{3,2,1,0:T(8,128)(2,1)}, u32[]{:S(2)}) copy-start(bf16[2,16,256,256]{3,2,1,0:T(8,128)(2,1)} %multiply_convert_fusion.refs_4_.refs_3_) | copy-start | bytes 12582916
  72.8 1.0 copy-start.5
  111.7 20.9 %copy-start.1 = (bf16[4096,1792]{1,0:T(8,128)(2,1)}, bf16[4096,1792]{1,0:T(8,128)(2,1)S(1)}, u32[]{:S(2)}) copy-start(bf16[4096,1792]{1,0:T(8,128)(2,1)S(1)} %get-tuple-element.37.rotated_ref) | copy-start | bytes 44040196
  111.7 39.2 %collective-permute-start.15 = (bf16[4096,1792]{1,0:T(8,128)(2,1)}, bf16[4096,1792]{1,0:T(8,128)(2,1)}, u32[]{:S(2)}, u32[]{:S(2)}) collective-permute-start(bf16[4096,1792]{1,0:T(8,128)(2,1)} %get-tuple-element.33), channel_id=1, source_target_pairs={{0,8},{8,0},{1,9},{9,1},{2,10},{10,2},{3,11},{11,3},{4,12},{12,4},... | collective-permute-start | bytes 44040200 | tf_op jit(solution)/shard_map/ppermute | solution.py:544
  112.3 20.3 %collective-permute-start.16 = (bf16[128,1792]{1,0:T(8,128)(2,1)S(1)}, bf16[128,1792]{1,0:T(8,128)(2,1)S(1)}, u32[]{:S(2)}, u32[]{:S(2)}) collective-permute-start(bf16[128,1792]{1,0:T(8,128)(2,1)S(1)} %convert_element_type.56), channel_id=1, source_target_pairs={{0,16},{16,0},{1,17},{17,1},{2,18},{18,2},{3,19},{19,3},{4,20},{20... | collective-permute-start | bytes 1376264 | tf_op jit(solution)/shard_map/ppermute | solution.py:544
  113.9 2.0 %copy-start.6 = (bf16[4096,128]{1,0:T(8,128)(2,1)S(1)}, bf16[4096,128]{1,0:T(8,128)(2,1)}, u32[]{:S(2)}) copy-start(bf16[4096,128]{1,0:T(8,128)(2,1)} %copy-done.5) | copy-start | bytes 3145732
  133.6 14.8 %collective-permute-start.17 = (f32[128,1792]{1,0:T(8,128)S(1)}, f32[128,1792]{1,0:T(8,128)S(1)}, u32[]{:S(2)}, u32[]{:S(2)}) collective-permute-start(f32[128,1792]{1,0:T(8,128)S(1)} %get-tuple-element.42), channel_id=1, source_target_pairs={{0,8},{8,0},{1,9},{9,1},{2,10},{10,2},{3,11},{11,3},{4,12},{12,4},... | collective-permute-start | bytes 2752520 | tf_op jit(solution)/shard_map/ppermute | solution.py:544
  134.9 5.2 %copy-start.2 = (bf16[4096,1792]{1,0:T(8,128)(2,1)S(1)}, bf16[4096,1792]{1,0:T(8,128)(2,1)}, u32[]{:S(2)}) copy-start(bf16[4096,1792]{1,0:T(8,128)(2,1)} %copy-done.1) | copy-start | bytes 44040196
  140.1 8.2 %copy-start.7 = (f32[1792,128]{1,0:T(8,128)S(1)}, f32[1792,128]{1,0:T(8,128)}, u32[]{:S(2)}) copy-start(f32[1792,128]{1,0:T(8,128)} %copy.9) | copy-start | bytes 2752516
  148.3 1.2 copy-start.8

commit v4 on v3

--- a/solution.py
+++ b/solution.py
@@ -199,7 +199,7 @@
             at += number
         scale_ref, table_ref = refs[at : at + 2]
         left_refs, out_refs = refs[at + 2 : at + 2 + group], refs[at + 2 + group : at + 2 + 2 * group]
-        right_ref, even_ref, odd_ref, flat_ref = refs[-4:]
+        right_ref, even_ref, odd_ref, both_ref = refs[-4:]
         step = pl.program_id(0)
         shown = jnp.maximum(step - 1, 0) * width
 
@@ -213,11 +213,12 @@
         def mix(number, inside, field_ref):
             b = (where_ref[1] ^ number) * (count // 2) + inside
             first = pl.multiple_of(inside * side, side)
-            parts = [
-                jnp.dot(table_ref[d, b], block_rows(d, number, first, side), preferred_element_type=F32)
+            products = [
+                jnp.dot(both_ref[d, b], block_rows(d, number, first, side), preferred_element_type=F32)
                 for d in range(group)
             ]
-            for o, mixed in enumerate(butterflies(parts)):
+            right_ref[...] += sum([product[side:] for product in products[1:]], products[0][side:])
+            for o, mixed in enumerate(butterflies([product[:side] for product in products])):
                 field_ref[o, b] = mixed
 
         def spread(i, field_ref):
@@ -238,29 +239,37 @@
 
                 @pl.loop(0, count // 2, unroll=2)
                 def _(inside, number=number):
-                    mix(number, inside, mixed_ref)
-                    spread(number * (count // 2) + inside, spread_ref)
+                    if mixed_ref is not None:
+                        mix(number, inside, mixed_ref)
+                    if spread_ref is not None:
+                        spread(number * (count // 2) + inside, spread_ref)
 
         @pl.when(step == 0)
         def _():
             for d in range(group):
-                flat_ref[d] = left_refs[d][...].T
-
-        total = jnp.zeros((rank, width), F32)
-        for d in range(group):
-            for number in range(2):
-                first = pl.multiple_of((where_ref[1] ^ number) * (rows // 2), 128)
-                flat = flat_ref[d, :, pl.ds(first, rows // 2)]
-                total += jnp.dot(flat, block_rows(d, number, 0, rows // 2), preferred_element_type=F32)
-        right_ref[...] = total
-
-        @pl.when(step % 2 == 0)
+                for b in range(count):
+                    both_ref[d, b, :side, :] = table_ref[d, b]
+                    both_ref[d, b, side:, :] = left_refs[d][b * side : (b + 1) * side, :].T
+
+        @pl.when(step < tiles)
         def _():
-            sweep(even_ref, odd_ref)
-
-        @pl.when(step % 2 == 1)
+            right_ref[...] = jnp.zeros_like(right_ref)
+
+        fields = (even_ref, odd_ref)
+
+        @pl.when(step == 0)
         def _():
-            sweep(odd_ref, even_ref)
+            sweep(fields[0], None)
+
+        for parity in range(2):
+
+            @pl.when((step > 0) & (step < tiles) & (step % 2 == parity))
+            def _(parity=parity):
+                sweep(fields[parity], fields[1 - parity])
+
+        @pl.when(step == tiles)
+        def _():
+            sweep(None, fields[(tiles - 1) % 2])
 
     def place(piece):
         def index(j, where):
@@ -284,47 +293,58 @@
             out_specs=[VMEM]
             + [pl.BlockSpec((rows, width), lambda j, where: (0, jnp.maximum(j - 1, 0)))] * (group - 1)
             + [pl.BlockSpec((rank, width), lambda j, where: (0, jnp.minimum(j, tiles - 1)))],
-            scratch_shapes=[field, field, pltpu.VMEM((group, rank, rows), BF16)],
+            scratch_shapes=[field, field, pltpu.VMEM((group, count, side + rank, side), BF16)],
         ),
-        compiler_params=params(38),
+        compiler_params=params(41),
         cost_estimate=cost(2 * size * (side + rank) * group, size * 2 * (2 * group - 1) + table.size * 2),
     )(where, *flat, scales_of(position, group, rows), table, *lefts)
 
 
-def project(accumulated, q_start, piece_at, position, group, pieces, out_type, after, copies):
+def project(accumulated, q_start, piece_at, position, group, out_types, after):
     rows, columns = accumulated.shape
     rank = q_start.shape[1]
     share = columns // group
-    piece = rows // pieces
+    piece = rows // PLANE
     tall = min(512, piece)
     steps = piece // tall
 
     def body(where_ref, a_ref, q_ref, *refs):
-        out_refs = refs[len(after) + len(copies) :]
-        out_refs[0][...] = jnp.dot(a_ref[...], q_ref[...], preferred_element_type=F32).astype(out_type)
+        out_refs = refs[len(after) :]
+        product = jnp.dot(a_ref[...], q_ref[...], preferred_element_type=F32)
+        for number, out_type in enumerate(out_types):
+
+            @pl.when(pl.program_id(0) // steps == number)
+            def _(number=number, out_type=out_type):
+                out_refs[number][...] = product.astype(out_type)
+
         for d in range(1, group):
             lanes = pl.ds(pl.multiple_of((where_ref[1] ^ d) * share, 128), share)
-            out_refs[d][...] = a_ref[:, lanes]
-
-    return pl.pallas_call(
-        body,
-        out_shape=[jax.ShapeDtypeStruct((piece, rank), out_type)]
+            out_refs[1 + d][...] = a_ref[:, lanes]
+
+    def out_place(number):
+        return pl.BlockSpec((tall, rank), lambda i, where: (jnp.clip(i - number * steps, 0, steps - 1), 0))
+
+    def copy_row(i, where):
+        return ((where[0] ^ (i // steps)) & 1) * steps + i % steps
+
+    return pl.pallas_call(
+        body,
+        out_shape=[jax.ShapeDtypeStruct((piece, rank), out_type) for out_type in out_types]
         + [jax.ShapeDtypeStruct((2 * piece, share), BF16)] * (group - 1),
         grid_spec=pltpu.PrefetchScalarGridSpec(
             num_scalar_prefetch=1,
-            grid=(steps,),
+            grid=(2 * steps,),
             in_specs=[
-                pl.BlockSpec((tall, columns), lambda i, where: (where[0] * steps + i, 0)),
+                pl.BlockSpec((tall, columns), lambda i, where: ((where[0] ^ (i // steps)) * steps + i % steps, 0)),
                 pl.BlockSpec((columns, rank), lambda i, where: (0, 0)),
             ]
-            + [ANY] * (len(after) + len(copies)),
-            out_specs=[pl.BlockSpec((tall, rank), lambda i, where: (i, 0))]
-            + [pl.BlockSpec((tall, share), lambda i, where: ((where[0] & 1) * steps + i, 0))] * (group - 1),
+            + [ANY] * len(after),
+            out_specs=[out_place(0), out_place(1)]
+            + [pl.BlockSpec((tall, share), lambda i, where: (copy_row(i, where), 0))] * (group - 1),
         ),
-        input_output_aliases={3 + len(after) + d: 1 + d for d in range(len(copies))},
         compiler_params=params(24),
-        cost_estimate=cost(2 * piece * columns * rank, piece * columns * 3),
-    )(jnp.stack([piece_at, position]), accumulated, q_start, *after, *copies)
+        cost_estimate=cost(4 * piece * columns * rank, piece * columns * 6),
+    )(jnp.stack([piece_at, position]), accumulated, q_start, *after)
 
 
 def split_sum(own, others, place, pieces):
@@ -498,30 +518,33 @@
         in_specs=[VMEM] * group + [SMEM, VMEM],
         out_specs=[VMEM] * 3,
         scratch_shapes=[pltpu.VMEM((count, side, rank), F32), pltpu.VMEM((rows, rank), F32)],
-        compiler_params=params(28),
+        compiler_params=params(20),
         cost_estimate=cost(8 * 10**9, 60 * 10**6),
     )(*blocks, scales_of(position, group, rows), table)
 
 
-def residual(rotated, basis16, right16, columns, owner, into=None, resident=False):
+def residual(rotated, basis16, right, columns, owner, resident, into=()):
     rows, share = rotated.shape
-    rank = right16.shape[0]
+    rank = right.shape[0]
     tall = min(512, rows)
-    earlier = () if into is None else (into,)
 
     def body(where_ref, rotated_ref, basis_ref, right_ref, *refs):
-        out_ref = refs[-1]
-        part = slice(None)
-        if resident:
-            part = pl.ds(pl.multiple_of(pl.program_id(0) * tall, tall), tall)
+        out_ref, factor_ref, right16_ref = refs[len(into) :]
+
+        @pl.when(pl.program_id(0) == 0)
+        def _():
+            right16_ref[...] = right_ref[...].astype(BF16)
+            factor_ref[...] = right_ref[...].T
+
+        part = pl.ds(pl.multiple_of(pl.program_id(0) * tall, tall), tall) if resident else slice(None)
         for start in range(0, share, 256):
             lanes = slice(start, min(start + 256, share))
-            approx = jnp.dot(basis_ref[...], right_ref[:, lanes], preferred_element_type=F32)
+            approx = jnp.dot(basis_ref[...], right16_ref[:, lanes], preferred_element_type=F32)
             out_ref[:, lanes] = (rotated_ref[part, lanes].astype(F32) - approx).astype(out_ref.dtype)
 
     return pl.pallas_call(
         body,
-        out_shape=jax.ShapeDtypeStruct((rows, columns), BF16),
+        out_shape=[jax.ShapeDtypeStruct((rows, columns), BF16), jax.ShapeDtypeStruct((columns, rank), F32)],
         grid_spec=pltpu.PrefetchScalarGridSpec(
             num_scalar_prefetch=1,
             grid=(rows // tall,),
@@ -530,13 +553,17 @@
                 pl.BlockSpec((tall, rank), lambda i, where: (i, 0)),
                 pl.BlockSpec((rank, share), lambda i, where: (0, 0)),
             ]
-            + [ANY] * len(earlier),
-            out_specs=pl.BlockSpec((tall, share), lambda i, where: (i, where[0])),
+            + [ANY] * len(into),
+            out_specs=[
+                pl.BlockSpec((tall, share), lambda i, where: (i, where[0])),
+                pl.BlockSpec((share, rank), lambda i, where: (where[0], 0)),
+            ],
+            scratch_shapes=[pltpu.VMEM((rank, share), BF16)],
         ),
-        input_output_aliases={4: 0} if earlier else {},
-        compiler_params=params(32 if resident else 16),
-        cost_estimate=cost(2 * rows * share * rank, rows * share * 4),
-    )(owner.reshape(1), rotated, basis16, right16, *earlier)
+        input_output_aliases={4: 0, 5: 1} if into else {},
+        compiler_params=params(16),
+        cost_estimate=cost(2 * rows * share * rank, rows * share * 2),
+    )(owner.reshape(1), rotated, basis16, right, *into)
 
 
 def from_distance(block, axis, distance):
@@ -566,28 +593,25 @@
     shared = share % 128 == 0 and rows % (256 * PLANE) == 0
     others = range(1, group)
 
-    came, after, copies = [], (), []
+    came, after = [], ()
     other_pieces = [[] for _ in others]
-    for d in reversed(range(PLANE)):
-        out_type = BF16 if d else F32
-        part, *copies = project(
-            accumulated, q_start, plane ^ d, position, group if shared else 1, PLANE, out_type, after, copies
+    for d in (3, 1):
+        out_types = (BF16, BF16 if d > 1 else F32)
+        first, second, *copies = project(
+            accumulated, q_start, plane ^ d, position, group if shared else 1, out_types, after
         )
-        after = (part,)
-        if d:
-            came.append(from_plane(part, d))
-        if d == 1:
-            after = (part, came[0])
-        if d % 2 == 0:
-            for e, copy in enumerate(copies):
-                other_pieces[e].append(from_distance(copy, "pos", e + 1))
-            copies = []
+        after = (second,)
+        came.append(from_plane(first, d))
+        if d > 1:
+            came.append(from_plane(second, d - 1))
+        for e, copy in enumerate(copies):
+            other_pieces[e].append(from_distance(copy, "pos", e + 1))
     table = signed_hadamard(signs, position, group, rows)
     if not shared:
         other_pieces = [[from_distance(accumulated, "pos", d)] for d in others]
     blocks = [[accumulated]] + other_pieces
 
-    own, *sent = split_sum(part, came, line, lines)
+    own, *sent = split_sum(second, came, line, lines)
     came = [from_line(sent[d - 1], d) for d in range(1, lines)]
     mine16 = sum([part.astype(F32) for part in came], own).astype(BF16)
     near16 = assemble([mine16] + [from_line(mine16, d) for d in range(1, lines)], line)
@@ -610,17 +634,13 @@
 
     right = jnp.dot(inverse, half, precision=lax.Precision.HIGHEST) / REPLICAS
     if not shared:
-        new_error = residual(rotated[0], basis16, right.astype(BF16), columns, jnp.zeros((), jnp.int32))
-        return (new_error, p_basis, right.T)
-    new_error = None
+        new_error, q_factor = residual(rotated[0], basis16, right, columns, jnp.zeros((), jnp.int32), False)
+        return (new_error, p_basis, q_factor)
     rights = [right] + [from_distance(right, "pos", d) for d in others]
+    results = ()
     for d in range(group):
-        new_error = residual(
-            rotated[d], basis16, rights[d].astype(BF16), columns, position ^ d, new_error, d == 0
-        )
-    q_factor = jnp.zeros((columns, rank), F32)
-    for d in range(group):
-        q_factor = lax.dynamic_update_slice_in_dim(q_factor, rights[d].T, (position ^ d) * share, 0)
+        results = residual(rotated[d], basis16, rights[d], columns, position ^ d, d == 0, results)
+    new_error, q_factor = results
     return (new_error, p_basis, q_factor)
 
 

time: 166 us -> 160 us (0.964)
  local copies, waits for them, and re-layouts: 13.3 us -> 4.6 us
  waiting for transfers between devices: 24.9 us -> 28.7 us
  Pallas kernels: 102 us -> 99 us
  other arithmetic: 3.8 us -> 6.06 us
    unnamed x20 -> x18, local copies, waits for them, and re-layouts: 10.6 us -> 4.58 us
    ppermute x6, waiting for transfers between devices: 16 us -> 19.8 us  [from_plane(): lax.ppermute(block, ('rep', 'mp'), [(p, p ^ change) for p in range(count)])]
    pallas_call x4 -> x2, Pallas kernels: 24.5 us -> 22 us  [project(): pl.pallas_call(body, out_shape=[jax.ShapeDtypeStruct((piece, rank), out_t...]
  transfers between devices with their start and end apart: 18 -> 18, of which waited for: 10 -> 9; matrix products, arithmetic and copies ran while one was open for 4% -> 4% of each run, Pallas kernels for 26% -> 23%
where the time goes in v4:
time: 160 us
  Pallas kernels  99 us (62%)
  waiting for transfers between devices  28.7 us (18%)
  starting transfers between devices  19.5 us (12%)
  other arithmetic  6.06 us (4%)
  local copies, waits for them, and re-layouts  4.6 us (3%)
    pallas_call x1, Pallas kernels, rotate_and_right(): pl.pallas_call(body, out_shape=[pltpu.VMEM((rows, columns), BF16)] + [jax...  36.6 us
    pallas_call x2, Pallas kernels, residual(): pl.pallas_call(body, out_shape=[jax.ShapeDtypeStruct((rows, columns), BF1...  23.5 us
    pallas_call x2, Pallas kernels, project(): pl.pallas_call(body, out_shape=[jax.ShapeDtypeStruct((piece, rank), out_t...  22 us
    ppermute x6, waiting for transfers between devices, from_plane(): lax.ppermute(block, ('rep', 'mp'), [(p, p ^ change) for p in range(count)])  19.8 us
    pallas_call x1, Pallas kernels, basis_of(): pl.pallas_call(body, out_shape=[jax.ShapeDtypeStruct((rank, rank), F32),...  16.7 us
    ppermute x12, starting transfers between devices, from_distance(): return lax.ppermute(block, axis, [(p, p ^ distance) for p in range(count)])  11.4 us
    ppermute x12, waiting for transfers between devices, from_distance(): return lax.ppermute(block, axis, [(p, p ^ distance) for p in range(count)])  8.84 us
    ppermute x6, starting transfers between devices, from_plane(): lax.ppermute(block, ('rep', 'mp'), [(p, p ^ change) for p in range(count)])  8.03 us
  transfers between devices with their start and end apart: 18, of which 9 were waited for; matrix products, arithmetic and copies ran while one was open for 4% of the time, Pallas kernels for 23%

profile of v4, /device:TPU:0, one launch (start us, length us, event | category | flops | bytes accessed | tf_op | source)
XLA Modules:
  0.0 159.5 jit_solution(12588454128654424837)
XLA Ops:
  0.7 1.2 copy-done.3
  1.9 11.0 %shard_map.58 = (bf16[1024,128]{1,0:T(8,128)(2,1)S(1)}, bf16[1024,128]{1,0:T(8,128)(2,1)S(1)}, bf16[2048,1792]{1,0:T(8,128)(2,1)}) custom-call(s32[2]{0:T(128)S(1)} %get-tuple-element.45.where_ref, bf16[4096,3584]{1,0:T(8,128)(2,1)} %refs_0_.1, bf16[3584,128]{1,0:T(8,128)(2,1)S(1)} %copy-done.3), custom_call_target="tpu_custom_call" | custom-call | flops 1879048192 | bytes 22020096 | tf_op jit(solution)/shard_map/pallas_call | solution.py:330
  13.3 11.0 %shard_map.59 = (bf16[1024,128]{1,0:T(8,128)(2,1)S(1)}, f32[1024,128]{1,0:T(8,128)S(1)}, bf16[2048,1792]{1,0:T(8,128)(2,1)}) custom-call(s32[2]{0:T(128)S(1)} %get-tuple-element.46.where_ref, bf16[4096,3584]{1,0:T(8,128)(2,1)} %refs_0_.1, bf16[3584,128]{1,0:T(8,128)(2,1)S(1)} %copy-done.4, bf16[1024,128]{1,0:T(8,128)(2,1)S(1)} %get-tuple-element.24.refs_0_), custom_call_target="tpu_custom_call" | custom-call | flops 1879048192 | bytes 22020096 | tf_op jit(solution)/shard_map/pallas_call | solution.py:330
  24.4 2.9 %collective-permute-start.3 = (bf16[1024,128]{1,0:T(8,128)(2,1)S(1)}, bf16[1024,128]{1,0:T(8,128)(2,1)S(1)}, u32[]{:S(2)}, u32[]{:S(2)}) collective-permute-start(bf16[1024,128]{1,0:T(8,128)(2,1)S(1)} %get-tuple-element.24.refs_0_), channel_id=1, source_target_pairs={{0,16},{1,17},{2,18},{3,19},{4,20},{5,21},{6,22},{7,23},{16,0},{17... | collective-permute-start | bytes 786440 | tf_op jit(solution)/shard_map/ppermute | solution.py:577
  27.3 1.5 collective-permute-start.2
  28.9 11.9 %collective-permute-done.2.refs_0_ = bf16[1024,128]{1,0:T(8,128)(2,1)S(1)} collective-permute-done((bf16[1024,128]{1,0:T(8,128)(2,1)S(1)}, bf16[1024,128]{1,0:T(8,128)(2,1)S(1)}, u32[]{:S(2)}, u32[]{:S(2)}) %collective-permute-start.2) | collective-permute-done | bytes 262176 | tf_op jit(solution)/shard_map/ppermute | solution.py:577
  40.7 1.4 collective-permute-done.4.refs_2_
  42.2 1.6 %collective-permute-start.5 = (bf16[256,128]{1,0:T(8,128)(2,1)S(1)}, bf16[256,128]{1,0:T(8,128)(2,1)S(1)}, u32[]{:S(2)}, u32[]{:S(2)}) collective-permute-start(bf16[256,128]{1,0:T(8,128)(2,1)S(1)} %get-tuple-element.30), channel_id=1, source_target_pairs={{0,2},{1,3},{2,0},{3,1},{4,6},{5,7},{6,4},{7,5},{8,10},{9,11},{10,... | collective-permute-start | bytes 196616 | tf_op jit(solution)/shard_map/ppermute | solution.py:571
  43.9 2.6 %collective-permute-start.6 = (bf16[256,128]{1,0:T(8,128)(2,1)S(1)}, bf16[256,128]{1,0:T(8,128)(2,1)S(1)}, u32[]{:S(2)}, u32[]{:S(2)}) collective-permute-start(bf16[256,128]{1,0:T(8,128)(2,1)S(1)} %get-tuple-element.31), channel_id=1, source_target_pairs={{0,4},{1,5},{2,6},{3,7},{4,0},{5,1},{6,2},{7,3},{8,12},{9,13},{10,... | collective-permute-start | bytes 196616 | tf_op jit(solution)/shard_map/ppermute | solution.py:571
  46.7 3.6 %collective-permute-done.6 = bf16[256,128]{1,0:T(8,128)(2,1)S(1)} collective-permute-done((bf16[256,128]{1,0:T(8,128)(2,1)S(1)}, bf16[256,128]{1,0:T(8,128)(2,1)S(1)}, u32[]{:S(2)}, u32[]{:S(2)}) %collective-permute-start.6) | collective-permute-done | bytes 65568 | tf_op jit(solution)/shard_map/ppermute | solution.py:571
  50.3 2.2 %collective-permute-done.7 = bf16[256,128]{1,0:T(8,128)(2,1)S(1)} collective-permute-done((bf16[256,128]{1,0:T(8,128)(2,1)S(1)}, bf16[256,128]{1,0:T(8,128)(2,1)S(1)}, u32[]{:S(2)}, u32[]{:S(2)}) %collective-permute-start.7) | collective-permute-done | bytes 65568 | tf_op jit(solution)/shard_map/ppermute | solution.py:571
  52.6 0.9 collective-permute-start.10
  53.8 3.2 %collective-permute-start.8 = (bf16[256,128]{1,0:T(8,128)(2,1)S(1)}, bf16[256,128]{1,0:T(8,128)(2,1)S(1)}, u32[]{:S(2)}, u32[]{:S(2)}) collective-permute-start(bf16[256,128]{1,0:T(8,128)(2,1)S(1)} %add_convert_fusion.refs_0_), channel_id=1, source_target_pairs={{0,2},{1,3},{2,0},{3,1},{4,6},{5,7},{6,4},{7,5},{8,10},{9,11},{10,... | collective-permute-start | bytes 196616 | tf_op jit(solution)/shard_map/ppermute | solution.py:571
  57.0 1.8 %collective-permute-done.10.refs_3_ = bf16[256,128]{1,0:T(8,128)(2,1)S(1)} collective-permute-done((bf16[256,128]{1,0:T(8,128)(2,1)S(1)}, bf16[256,128]{1,0:T(8,128)(2,1)S(1)}, u32[]{:S(2)}, u32[]{:S(2)}) %collective-permute-start.10) | collective-permute-done | bytes 65568 | tf_op jit(solution)/shard_map/ppermute | solution.py:571
  58.8 1.2 collective-permute-done.9.refs_2_
  60.0 1.5 collective-permute-start.13
  62.0 1.5 collective-permute-start.11
  63.6 3.9 %collective-permute-done.13.refs_3_ = bf16[1024,128]{1,0:T(8,128)(2,1)S(1)} collective-permute-done((bf16[1024,128]{1,0:T(8,128)(2,1)S(1)}, bf16[1024,128]{1,0:T(8,128)(2,1)S(1)}, u32[]{:S(2)}, u32[]{:S(2)}) %collective-permute-start.13) | collective-permute-done | bytes 262176 | tf_op jit(solution)/shard_map/ppermute | solution.py:577
  67.5 2.4 %collective-permute-done.12.refs_2_ = bf16[1024,128]{1,0:T(8,128)(2,1)S(1)} collective-permute-done((bf16[1024,128]{1,0:T(8,128)(2,1)S(1)}, bf16[1024,128]{1,0:T(8,128)(2,1)S(1)}, u32[]{:S(2)}, u32[]{:S(2)}) %collective-permute-start.12) | collective-permute-done | bytes 262176 | tf_op jit(solution)/shard_map/ppermute | solution.py:577
  70.4 0.7 convert_multiply_fusion.refs_3_.refs_2_
  71.2 0.6 pad_add_fusion.where_ref
  71.9 3.3 %multiply_convert_fusion.refs_4_.refs_3_ = bf16[2,16,256,256]{3,2,1,0:T(8,128)(2,1)} fusion(f32[2,16,256]{2,1,0:T(8,128)S(1)} %add_convert_fusion.1, f32[256,256]{1,0:T(8,128)S(1)} %subtract_convert_fusion), kind=kLoop, calls=%fused_computation | loop fusion | flops 4194304 | bytes 4489216 | tf_op jit(solution)/shard_map/convert_element_type | solution.py:62
  75.2 0.9 copy-done.5
  76.1 36.6 %shard_map.63 = (bf16[4096,1792]{1,0:T(8,128)(2,1)S(1)}, bf16[4096,1792]{1,0:T(8,128)(2,1)}, f32[128,1792]{1,0:T(8,128)}) custom-call(s32[2]{0:T(128)} %pad_add_fusion.where_ref, bf16[4096,3584]{1,0:T(8,128)(2,1)} %refs_0_.1, bf16[2048,1792]{1,0:T(8,128)(2,1)} %collective-permute-done.refs_1_, bf16[2048,1792]{1,0:T(8,128)(2,1)} %collective-permute-done.1.refs_2_, ...), custom_call_target="tpu_custom_call" | custom-call | flops 11274289152 | bytes 48234496 | tf_op jit(solution)/shard_map/pallas_call | solution.py:284
  113.0 1.2 convert_element_type.50
  114.2 1.6 collective-permute-start.16
  115.8 1.2 copy-done.2
  117.0 1.2 copy-done.6
  118.3 16.7 %shard_map.64 = (f32[128,128]{1,0:T(8,128)S(1)}, f32[4096,128]{1,0:T(8,128)}, bf16[4096,128]{1,0:T(8,128)(2,1)S(1)}) custom-call(bf16[4096,128]{1,0:T(8,128)(2,1)S(1)} %copy-done.2, bf16[4096,128]{1,0:T(8,128)(2,1)S(1)} %copy-done.6, f32[2]{0:T(128)S(1)} %copy-done.7, bf16[2,16,256,256]{3,2,1,0:T(8,128)(2,1)S(1)} %copy-done), custom_call_target="tpu_custom_call" | custom-call | flops 8000000000 | bytes 60000000 | tf_op jit(solution)/shard_map/pallas_call | solution.py:511
  135.0 0.9 convolution_multiply_fusion.right_ref
  136.0 8.6 %shard_map.65 = (bf16[4096,3584]{1,0:T(8,128)(2,1)}, f32[3584,128]{1,0:T(8,128)}) custom-call(s32[1]{0:T(128)} %bitcast.1.where_ref, bf16[4096,1792]{1,0:T(8,128)(2,1)S(1)} %get-tuple-element.37.rotated_ref, bf16[4096,128]{1,0:T(8,128)(2,1)S(1)} %get-tuple-element.34.basis_ref, f32[128,1792]{1,0:T(8,128)S(1)} %convolution_multiply_fusion.right_ref), custom_call_target="tpu_custom_call" | custom-call | flops 1879048192 | bytes 14680064 | tf_op jit(solution)/shard_map/pallas_call | solution.py:545
  144.6 15.0 %shard_map.66 = (bf16[4096,3584]{1,0:T(8,128)(2,1)}, f32[3584,128]{1,0:T(8,128)}) custom-call(s32[1]{0:T(128)} %bitcast.where_ref, bf16[4096,1792]{1,0:T(8,128)(2,1)} %collective-permute-done.15.rotated_ref, bf16[4096,128]{1,0:T(8,128)(2,1)S(1)} %get-tuple-element.34.basis_ref, ...), custom_call_target="tpu_custom_call", output_to_operand_aliasing={{0}: (4, {}), {1}: (5, {})} | custom-call | flops 1879048192 | bytes 14680064 | tf_op jit(solution)/shard_map/pallas_call | solution.py:545
  (43 shorter events, 2.9 us)
Async XLA Ops:
  0.7 1.2 copy-start.3
  1.9 11.4 %copy-start.4 = (bf16[3584,128]{1,0:T(8,128)(2,1)S(1)}, bf16[3584,128]{1,0:T(8,128)(2,1)}, u32[]{:S(2)}) copy-start(bf16[3584,128]{1,0:T(8,128)(2,1)} %q_ref.3) | copy-start | bytes 2752516
  12.9 62.3 %collective-permute-start = (bf16[2048,1792]{1,0:T(8,128)(2,1)}, bf16[2048,1792]{1,0:T(8,128)(2,1)}, u32[]{:S(2)}, u32[]{:S(2)}) collective-permute-start(bf16[2048,1792]{1,0:T(8,128)(2,1)} %get-tuple-element.23), channel_id=1, source_target_pairs={{0,8},{8,0},{1,9},{9,1},{2,10},{10,2},{3,11},{11,3},{4,12},{12,4},... | collective-permute-start | bytes 22020104 | tf_op jit(solution)/shard_map/ppermute | solution.py:571
  13.3 57.0 %copy-start.8 = (s32[8192]{0:T(1024)S(1)}, s32[8192]{0:T(1024)}, u32[]{:S(2)}) copy-start(s32[8192]{0:T(1024)} %param.4) | copy-start | bytes 98308
  24.3 50.8 %collective-permute-start.1 = (bf16[2048,1792]{1,0:T(8,128)(2,1)}, bf16[2048,1792]{1,0:T(8,128)(2,1)}, u32[]{:S(2)}, u32[]{:S(2)}) collective-permute-start(bf16[2048,1792]{1,0:T(8,128)(2,1)} %get-tuple-element.25), channel_id=1, source_target_pairs={{0,8},{8,0},{1,9},{9,1},{2,10},{10,2},{3,11},{11,3},{4,12},{12,4},... | collective-permute-start | bytes 22020104 | tf_op jit(solution)/shard_map/ppermute | solution.py:571
  24.4 16.4 %collective-permute-start.3 = (bf16[1024,128]{1,0:T(8,128)(2,1)S(1)}, bf16[1024,128]{1,0:T(8,128)(2,1)S(1)}, u32[]{:S(2)}, u32[]{:S(2)}) collective-permute-start(bf16[1024,128]{1,0:T(8,128)(2,1)S(1)} %get-tuple-element.24.refs_0_), channel_id=1, source_target_pairs={{0,16},{1,17},{2,18},{3,19},{4,20},{5,21},{6,22},{7,23},{16,0},{17... | collective-permute-start | bytes 786440 | tf_op jit(solution)/shard_map/ppermute | solution.py:577
  27.3 13.4 %collective-permute-start.2 = (bf16[1024,128]{1,0:T(8,128)(2,1)S(1)}, bf16[1024,128]{1,0:T(8,128)(2,1)S(1)}, u32[]{:S(2)}, u32[]{:S(2)}) collective-permute-start(bf16[1024,128]{1,0:T(8,128)(2,1)S(1)} %get-tuple-element.27), channel_id=1, source_target_pairs={{0,17},{1,16},{2,19},{3,18},{4,21},{5,20},{6,23},{7,22},{16,1},{17... | collective-permute-start | bytes 786440 | tf_op jit(solution)/shard_map/ppermute | solution.py:577
  28.8 13.3 %collective-permute-start.4 = (bf16[1024,128]{1,0:T(8,128)(2,1)S(1)}, bf16[1024,128]{1,0:T(8,128)(2,1)S(1)}, u32[]{:S(2)}, u32[]{:S(2)}) collective-permute-start(bf16[1024,128]{1,0:T(8,128)(2,1)S(1)} %get-tuple-element.28), channel_id=1, source_target_pairs={{0,1},{1,0},{2,3},{3,2},{4,5},{5,4},{6,7},{7,6},{16,17},{17,16},{1... | collective-permute-start | bytes 786440 | tf_op jit(solution)/shard_map/ppermute | solution.py:577
  42.2 4.5 %collective-permute-start.5 = (bf16[256,128]{1,0:T(8,128)(2,1)S(1)}, bf16[256,128]{1,0:T(8,128)(2,1)S(1)}, u32[]{:S(2)}, u32[]{:S(2)}) collective-permute-start(bf16[256,128]{1,0:T(8,128)(2,1)S(1)} %get-tuple-element.30), channel_id=1, source_target_pairs={{0,2},{1,3},{2,0},{3,1},{4,6},{5,7},{6,4},{7,5},{8,10},{9,11},{10,... | collective-permute-start | bytes 196616 | tf_op jit(solution)/shard_map/ppermute | solution.py:571
  43.9 6.5 %collective-permute-start.6 = (bf16[256,128]{1,0:T(8,128)(2,1)S(1)}, bf16[256,128]{1,0:T(8,128)(2,1)S(1)}, u32[]{:S(2)}, u32[]{:S(2)}) collective-permute-start(bf16[256,128]{1,0:T(8,128)(2,1)S(1)} %get-tuple-element.31), channel_id=1, source_target_pairs={{0,4},{1,5},{2,6},{3,7},{4,0},{5,1},{6,2},{7,3},{8,12},{9,13},{10,... | collective-permute-start | bytes 196616 | tf_op jit(solution)/shard_map/ppermute | solution.py:571
  46.5 6.1 %collective-permute-start.7 = (bf16[256,128]{1,0:T(8,128)(2,1)S(1)}, bf16[256,128]{1,0:T(8,128)(2,1)S(1)}, u32[]{:S(2)}, u32[]{:S(2)}) collective-permute-start(bf16[256,128]{1,0:T(8,128)(2,1)S(1)} %get-tuple-element.32), channel_id=1, source_target_pairs={{0,6},{1,7},{2,4},{3,5},{4,2},{5,3},{6,0},{7,1},{8,14},{9,15},{10,... | collective-permute-start | bytes 196616 | tf_op jit(solution)/shard_map/ppermute | solution.py:571
  52.6 6.3 %collective-permute-start.10 = (bf16[256,128]{1,0:T(8,128)(2,1)S(1)}, bf16[256,128]{1,0:T(8,128)(2,1)S(1)}, u32[]{:S(2)}, u32[]{:S(2)}) collective-permute-start(bf16[256,128]{1,0:T(8,128)(2,1)S(1)} %add_convert_fusion.refs_0_), channel_id=1, source_target_pairs={{0,6},{1,7},{2,4},{3,5},{4,2},{5,3},{6,0},{7,1},{8,14},{9,15},{10,... | collective-permute-start | bytes 196616 | tf_op jit(solution)/shard_map/ppermute | solution.py:571
  53.4 6.6 %collective-permute-start.9 = (bf16[256,128]{1,0:T(8,128)(2,1)S(1)}, bf16[256,128]{1,0:T(8,128)(2,1)S(1)}, u32[]{:S(2)}, u32[]{:S(2)}) collective-permute-start(bf16[256,128]{1,0:T(8,128)(2,1)S(1)} %add_convert_fusion.refs_0_), channel_id=1, source_target_pairs={{0,4},{1,5},{2,6},{3,7},{4,0},{5,1},{6,2},{7,3},{8,12},{9,13},{10,... | collective-permute-start | bytes 196616 | tf_op jit(solution)/shard_map/ppermute | solution.py:571
  53.8 6.2 %collective-permute-start.8 = (bf16[256,128]{1,0:T(8,128)(2,1)S(1)}, bf16[256,128]{1,0:T(8,128)(2,1)S(1)}, u32[]{:S(2)}, u32[]{:S(2)}) collective-permute-start(bf16[256,128]{1,0:T(8,128)(2,1)S(1)} %add_convert_fusion.refs_0_), channel_id=1, source_target_pairs={{0,2},{1,3},{2,0},{3,1},{4,6},{5,7},{6,4},{7,5},{8,10},{9,11},{10,... | collective-permute-start | bytes 196616 | tf_op jit(solution)/shard_map/ppermute | solution.py:571
  60.0 7.4 %collective-permute-start.13 = (bf16[1024,128]{1,0:T(8,128)(2,1)S(1)}, bf16[1024,128]{1,0:T(8,128)(2,1)S(1)}, u32[]{:S(2)}, u32[]{:S(2)}) collective-permute-start(bf16[1024,128]{1,0:T(8,128)(2,1)S(1)} %shard_map.61.refs_0_), channel_id=1, source_target_pairs={{0,17},{1,16},{2,19},{3,18},{4,21},{5,20},{6,23},{7,22},{16,1},{17... | collective-permute-start | bytes 786440 | tf_op jit(solution)/shard_map/ppermute | solution.py:577
  61.5 8.4 %collective-permute-start.12 = (bf16[1024,128]{1,0:T(8,128)(2,1)S(1)}, bf16[1024,128]{1,0:T(8,128)(2,1)S(1)}, u32[]{:S(2)}, u32[]{:S(2)}) collective-permute-start(bf16[1024,128]{1,0:T(8,128)(2,1)S(1)} %shard_map.61.refs_0_), channel_id=1, source_target_pairs={{0,16},{1,17},{2,18},{3,19},{4,20},{5,21},{6,22},{7,23},{16,0},{17... | collective-permute-start | bytes 786440 | tf_op jit(solution)/shard_map/ppermute | solution.py:577
  62.0 8.1 %collective-permute-start.11 = (bf16[1024,128]{1,0:T(8,128)(2,1)S(1)}, bf16[1024,128]{1,0:T(8,128)(2,1)S(1)}, u32[]{:S(2)}, u32[]{:S(2)}) collective-permute-start(bf16[1024,128]{1,0:T(8,128)(2,1)S(1)} %shard_map.61.refs_0_), channel_id=1, source_target_pairs={{0,1},{1,0},{2,3},{3,2},{4,5},{5,4},{6,7},{7,6},{16,17},{17,16},{1... | collective-permute-start | bytes 786440 | tf_op jit(solution)/shard_map/ppermute | solution.py:577
  70.2 4.9 %copy-start.1 = (bf16[4096,128]{1,0:T(8,128)(2,1)}, bf16[4096,128]{1,0:T(8,128)(2,1)S(1)}, u32[]{:S(2)}) copy-start(bf16[4096,128]{1,0:T(8,128)(2,1)S(1)} %shard_map.62.refs_5_.refs_0_) | copy-start | bytes 3145732
  70.3 4.9 %collective-permute-start.14 = (bf16[4096,128]{1,0:T(8,128)(2,1)S(1)}, bf16[4096,128]{1,0:T(8,128)(2,1)S(1)}, u32[]{:S(2)}, u32[]{:S(2)}) collective-permute-start(bf16[4096,128]{1,0:T(8,128)(2,1)S(1)} %shard_map.62.refs_5_.refs_0_), channel_id=1, source_target_pairs={{0,8},{8,0},{1,9},{9,1},{2,10},{10,2},{3,11},{11,3},{4,12},{12,4},... | collective-permute-start | bytes 3145736 | tf_op jit(solution)/shard_map/ppermute | solution.py:571
  75.1 40.7 %copy-start = (bf16[2,16,256,256]{3,2,1,0:T(8,128)(2,1)S(1)}, bf16[2,16,256,256]{3,2,1,0:T(8,128)(2,1)}, u32[]{:S(2)}) copy-start(bf16[2,16,256,256]{3,2,1,0:T(8,128)(2,1)} %multiply_convert_fusion.refs_4_.refs_3_) | copy-start | bytes 12582916
  75.1 40.7 %copy-start.7 = (f32[2]{0:T(128)S(1)}, f32[2]{0:T(128)}, u32[]{:S(2)}) copy-start(f32[2]{0:T(128)} %convert_multiply_fusion.refs_3_.refs_2_) | copy-start | bytes 28
  75.1 1.0 copy-start.5
  112.7 31.9 %collective-permute-start.15 = (bf16[4096,1792]{1,0:T(8,128)(2,1)}, bf16[4096,1792]{1,0:T(8,128)(2,1)}, u32[]{:S(2)}, u32[]{:S(2)}) collective-permute-start(bf16[4096,1792]{1,0:T(8,128)(2,1)} %get-tuple-element.33), channel_id=1, source_target_pairs={{0,8},{8,0},{1,9},{9,1},{2,10},{10,2},{3,11},{11,3},{4,12},{12,4},... | collective-permute-start | bytes 44040200 | tf_op jit(solution)/shard_map/ppermute | solution.py:571
  114.2 20.8 %collective-permute-start.16 = (bf16[128,1792]{1,0:T(8,128)(2,1)S(1)}, bf16[128,1792]{1,0:T(8,128)(2,1)S(1)}, u32[]{:S(2)}, u32[]{:S(2)}) collective-permute-start(bf16[128,1792]{1,0:T(8,128)(2,1)S(1)} %convert_element_type.50), channel_id=1, source_target_pairs={{0,16},{16,0},{1,17},{17,1},{2,18},{18,2},{3,19},{19,3},{4,20},{20... | collective-permute-start | bytes 1376264 | tf_op jit(solution)/shard_map/ppermute | solution.py:571
  115.8 1.2 copy-start.2
  117.0 1.2 copy-start.6
  135.9 8.7 %collective-permute-start.17 = (f32[128,1792]{1,0:T(8,128)S(1)}, f32[128,1792]{1,0:T(8,128)S(1)}, u32[]{:S(2)}, u32[]{:S(2)}) collective-permute-start(f32[128,1792]{1,0:T(8,128)S(1)} %convolution_multiply_fusion.right_ref), channel_id=1, source_target_pairs={{0,8},{8,0},{1,9},{9,1},{2,10},{10,2},{3,11},{11,3},{4,12},{12,4},... | collective-permute-start | bytes 2752520 | tf_op jit(solution)/shard_map/ppermute | solution.py:571

commit v5 on v4

--- a/solution.py
+++ b/solution.py
@@ -199,7 +199,7 @@
             at += number
         scale_ref, table_ref = refs[at : at + 2]
         left_refs, out_refs = refs[at + 2 : at + 2 + group], refs[at + 2 + group : at + 2 + 2 * group]
-        right_ref, even_ref, odd_ref, both_ref = refs[-4:]
+        right_ref, even_ref, odd_ref, both_ref, total_ref = refs[-5:]
         step = pl.program_id(0)
         shown = jnp.maximum(step - 1, 0) * width
 
@@ -217,7 +217,7 @@
                 jnp.dot(both_ref[d, b], block_rows(d, number, first, side), preferred_element_type=F32)
                 for d in range(group)
             ]
-            right_ref[...] += sum([product[side:] for product in products[1:]], products[0][side:])
+            total_ref[...] += sum([product[side:] for product in products[1:]], products[0][side:])
             for o, mixed in enumerate(butterflies([product[:side] for product in products])):
                 field_ref[o, b] = mixed
 
@@ -253,7 +253,7 @@
 
         @pl.when(step < tiles)
         def _():
-            right_ref[...] = jnp.zeros_like(right_ref)
+            total_ref[...] = jnp.zeros_like(total_ref)
 
         fields = (even_ref, odd_ref)
 
@@ -266,6 +266,10 @@
             @pl.when((step > 0) & (step < tiles) & (step % 2 == parity))
             def _(parity=parity):
                 sweep(fields[parity], fields[1 - parity])
+
+        @pl.when(step < tiles)
+        def _():
+            right_ref[...] = total_ref[...].astype(BF16)
 
         @pl.when(step == tiles)
         def _():
@@ -285,7 +289,7 @@
         body,
         out_shape=[pltpu.VMEM((rows, columns), BF16)]
         + [jax.ShapeDtypeStruct((rows, columns), BF16)] * (group - 1)
-        + [jax.ShapeDtypeStruct((rank, columns), F32)],
+        + [jax.ShapeDtypeStruct((rank, columns), BF16)],
         grid_spec=pltpu.PrefetchScalarGridSpec(
             num_scalar_prefetch=1,
             grid=(tiles + 1,),
@@ -293,14 +297,19 @@
             out_specs=[VMEM]
             + [pl.BlockSpec((rows, width), lambda j, where: (0, jnp.maximum(j - 1, 0)))] * (group - 1)
             + [pl.BlockSpec((rank, width), lambda j, where: (0, jnp.minimum(j, tiles - 1)))],
-            scratch_shapes=[field, field, pltpu.VMEM((group, count, side + rank, side), BF16)],
+            scratch_shapes=[
+                field,
+                field,
+                pltpu.VMEM((group, count, side + rank, side), BF16),
+                pltpu.VMEM((rank, width), F32),
+            ],
         ),
         compiler_params=params(41),
         cost_estimate=cost(2 * size * (side + rank) * group, size * 2 * (2 * group - 1) + table.size * 2),
     )(where, *flat, scales_of(position, group, rows), table, *lefts)
 
 
-def project(accumulated, q_start, piece_at, position, group, out_types, after):
+def project(accumulated, q_start, piece_at, position, group, out_types, after, copies=()):
     rows, columns = accumulated.shape
     rank = q_start.shape[1]
     share = columns // group
@@ -309,7 +318,7 @@
     steps = piece // tall
 
     def body(where_ref, a_ref, q_ref, *refs):
-        out_refs = refs[len(after) :]
+        out_refs = refs[len(after) + len(copies) :]
         product = jnp.dot(a_ref[...], q_ref[...], preferred_element_type=F32)
         for number, out_type in enumerate(out_types):
 
@@ -319,7 +328,7 @@
 
         for d in range(1, group):
             lanes = pl.ds(pl.multiple_of((where_ref[1] ^ d) * share, 128), share)
-            out_refs[1 + d][...] = a_ref[:, lanes]
+            out_refs[len(out_types) + d - 1][...] = a_ref[:, lanes]
 
     def out_place(number):
         return pl.BlockSpec((tall, rank), lambda i, where: (jnp.clip(i - number * steps, 0, steps - 1), 0))
@@ -333,18 +342,19 @@
         + [jax.ShapeDtypeStruct((2 * piece, share), BF16)] * (group - 1),
         grid_spec=pltpu.PrefetchScalarGridSpec(
             num_scalar_prefetch=1,
-            grid=(2 * steps,),
+            grid=(len(out_types) * steps,),
             in_specs=[
                 pl.BlockSpec((tall, columns), lambda i, where: ((where[0] ^ (i // steps)) * steps + i % steps, 0)),
                 pl.BlockSpec((columns, rank), lambda i, where: (0, 0)),
             ]
-            + [ANY] * len(after),
-            out_specs=[out_place(0), out_place(1)]
+            + [ANY] * (len(after) + len(copies)),
+            out_specs=[out_place(number) for number in range(len(out_types))]
             + [pl.BlockSpec((tall, share), lambda i, where: (copy_row(i, where), 0))] * (group - 1),
         ),
+        input_output_aliases={3 + len(after) + d: len(out_types) + d for d in range(len(copies))},
         compiler_params=params(24),
-        cost_estimate=cost(4 * piece * columns * rank, piece * columns * 6),
-    )(jnp.stack([piece_at, position]), accumulated, q_start, *after)
+        cost_estimate=cost(2 * len(out_types) * piece * columns * rank, len(out_types) * piece * columns * 3),
+    )(jnp.stack([piece_at, position]), accumulated, q_start, *after, *copies)
 
 
 def split_sum(own, others, place, pieces):
@@ -457,9 +467,9 @@
         pivot_row = left[home][inside : inside + 1, :]
         pivot = left[home][inside : inside + 1, k : k + 1]
         made_row = right[home][inside : inside + 1, :]
-        inverse = 1.0 / pivot
-        scales[home] = jnp.where(row == inside, lax.rsqrt(jnp.broadcast_to(pivot, (8, rank))), scales[home])
-        pivot_row, made_row = pivot_row * inverse, made_row * inverse
+        root = lax.rsqrt(jnp.broadcast_to(pivot, (1, rank)))
+        scales[home] = jnp.where(row == inside, root, scales[home])
+        pivot_row, made_row = pivot_row * root * root, made_row * root * root
         for block in range(home, len(left)):
             if block == home and inside == 7:
                 continue
@@ -518,7 +528,7 @@
         in_specs=[VMEM] * group + [SMEM, VMEM],
         out_specs=[VMEM] * 3,
         scratch_shapes=[pltpu.VMEM((count, side, rank), F32), pltpu.VMEM((rows, rank), F32)],
-        compiler_params=params(20),
+        compiler_params=params(10),
         cost_estimate=cost(8 * 10**9, 60 * 10**6),
     )(*blocks, scales_of(position, group, rows), table)
 
@@ -561,7 +571,7 @@
             scratch_shapes=[pltpu.VMEM((rank, share), BF16)],
         ),
         input_output_aliases={4: 0, 5: 1} if into else {},
-        compiler_params=params(16),
+        compiler_params=params(10),
         cost_estimate=cost(2 * rows * share * rank, rows * share * 2),
     )(owner.reshape(1), rotated, basis16, right, *into)
 
@@ -593,25 +603,28 @@
     shared = share % 128 == 0 and rows % (256 * PLANE) == 0
     others = range(1, group)
 
-    came, after = [], ()
+    came, after, copies = [], (), ()
     other_pieces = [[] for _ in others]
-    for d in (3, 1):
-        out_types = (BF16, BF16 if d > 1 else F32)
-        first, second, *copies = project(
-            accumulated, q_start, plane ^ d, position, group if shared else 1, out_types, after
+    for sent in ((3,), (2,), (1,), (0,)):
+        out_types = [BF16 if d else F32 for d in sent]
+        results = project(
+            accumulated, q_start, plane ^ sent[0], position, group if shared else 1, out_types, after, copies
         )
-        after = (second,)
-        came.append(from_plane(first, d))
-        if d > 1:
-            came.append(from_plane(second, d - 1))
-        for e, copy in enumerate(copies):
-            other_pieces[e].append(from_distance(copy, "pos", e + 1))
+        parts, copies = results[: len(sent)], tuple(results[len(sent) :])
+        after = (parts[-1],)
+        came += [from_plane(part, d) for part, d in zip(parts, sent) if d]
+        if sent[0] == 1:
+            after += (came[0],)
+        if sent[0] % 2 == 0:
+            for e, copy in enumerate(copies):
+                other_pieces[e].append(from_distance(copy, "pos", e + 1))
+            copies = ()
     table = signed_hadamard(signs, position, group, rows)
     if not shared:
         other_pieces = [[from_distance(accumulated, "pos", d)] for d in others]
     blocks = [[accumulated]] + other_pieces
 
-    own, *sent = split_sum(second, came, line, lines)
+    own, *sent = split_sum(parts[0], came, line, lines)
     came = [from_line(sent[d - 1], d) for d in range(1, lines)]
     mine16 = sum([part.astype(F32) for part in came], own).astype(BF16)
     near16 = assemble([mine16] + [from_line(mine16, d) for d in range(1, lines)], line)
@@ -621,7 +634,6 @@
 
     if shared:
         *rotated, half = rotate_and_right(blocks, table, around16, position, plane)
-        half = half.astype(BF16)
         rotated = rotated[:1] + [from_distance(part, "pos", d + 1) for d, part in enumerate(rotated[1:])]
         half = half.astype(F32) + from_distance(half, "rep", 1).astype(F32)
     else:

time: 160 us -> 152 us (0.950)
  waiting for transfers between devices: 28.7 us -> 24.9 us
  Pallas kernels: 99 us -> 96.2 us
    pallas_call x2, Pallas kernels: 23.5 us -> 17.2 us  [residual(): pl.pallas_call(body, out_shape=[jax.ShapeDtypeStruct((rows, columns), BF1...]
    ppermute x6, waiting for transfers between devices: 19.8 us -> 16 us  [from_plane(): lax.ppermute(block, ('rep', 'mp'), [(p, p ^ change) for p in range(count)])]
    pallas_call x2 -> x4, Pallas kernels: 22 us -> 25.4 us  [project(): pl.pallas_call(body, out_shape=[jax.ShapeDtypeStruct((piece, rank), out_t...]
    unnamed x18 -> x20, local copies, waits for them, and re-layouts: 4.58 us -> 4.59 us
  transfers between devices with their start and end apart: 18 -> 18, of which waited for: 9 -> 10; matrix products, arithmetic and copies ran while one was open for 4% -> 4% of each run, Pallas kernels for 23% -> 29%
where the time goes in v5:
time: 152 us
  Pallas kernels  96.2 us (63%)
  waiting for transfers between devices  24.9 us (16%)
  starting transfers between devices  19.3 us (13%)
  other arithmetic  4.84 us (3%)
  local copies, waits for them, and re-layouts  4.6 us (3%)
    pallas_call x1, Pallas kernels, rotate_and_right(): pl.pallas_call(body, out_shape=[pltpu.VMEM((rows, columns), BF16)] + [jax...  36.6 us
    pallas_call x4, Pallas kernels, project(): pl.pallas_call(body, out_shape=[jax.ShapeDtypeStruct((piece, rank), out_t...  25.4 us
    pallas_call x2, Pallas kernels, residual(): pl.pallas_call(body, out_shape=[jax.ShapeDtypeStruct((rows, columns), BF1...  17.2 us
    pallas_call x1, Pallas kernels, basis_of(): pl.pallas_call(body, out_shape=[jax.ShapeDtypeStruct((rank, rank), F32),...  16.8 us
    ppermute x6, waiting for transfers between devices, from_plane(): lax.ppermute(block, ('rep', 'mp'), [(p, p ^ change) for p in range(count)])  16 us
    ppermute x12, starting transfers between devices, from_distance(): return lax.ppermute(block, axis, [(p, p ^ distance) for p in range(count)])  11.3 us
    ppermute x12, waiting for transfers between devices, from_distance(): return lax.ppermute(block, axis, [(p, p ^ distance) for p in range(count)])  8.96 us
    ppermute x6, starting transfers between devices, from_plane(): lax.ppermute(block, ('rep', 'mp'), [(p, p ^ change) for p in range(count)])  8.02 us
  transfers between devices with their start and end apart: 18, of which 10 were waited for; matrix products, arithmetic and copies ran while one was open for 4% of the time, Pallas kernels for 29%

profile of v5, /device:TPU:0, one launch (start us, length us, event | category | flops | bytes accessed | tf_op | source)
XLA Modules:
  0.0 151.6 jit_solution(13880995146991973865)
XLA Ops:
  0.7 1.2 copy-done.1
  1.9 6.3 %shard_map.58 = (bf16[1024,128]{1,0:T(8,128)(2,1)S(1)}, bf16[2048,1792]{1,0:T(8,128)(2,1)}) custom-call(s32[2]{0:T(128)S(1)} %get-tuple-element.50.where_ref, bf16[4096,3584]{1,0:T(8,128)(2,1)} %refs_0_.1, bf16[3584,128]{1,0:T(8,128)(2,1)S(1)} %copy-done.1), custom_call_target="tpu_custom_call" | custom-call | flops 939524096 | bytes 11010048 | tf_op jit(solution)/shard_map/pallas_call | solution.py:339
  8.2 3.9 %collective-permute-start.1 = (bf16[1024,128]{1,0:T(8,128)(2,1)S(1)}, bf16[1024,128]{1,0:T(8,128)(2,1)S(1)}, u32[]{:S(2)}, u32[]{:S(2)}) collective-permute-start(bf16[1024,128]{1,0:T(8,128)(2,1)S(1)} %get-tuple-element.25.refs_0_), channel_id=1, source_target_pairs={{0,17},{1,16},{2,19},{3,18},{4,21},{5,20},{6,23},{7,22},{16,1},{17... | collective-permute-start | bytes 786440 | tf_op jit(solution)/shard_map/ppermute | solution.py:587
  12.1 6.3 %shard_map.59 = (bf16[1024,128]{1,0:T(8,128)(2,1)S(1)}, bf16[2048,1792]{1,0:T(8,128)(2,1)}) custom-call(s32[2]{0:T(128)S(1)} %get-tuple-element.49.where_ref, bf16[4096,3584]{1,0:T(8,128)(2,1)} %refs_0_.1, bf16[3584,128]{1,0:T(8,128)(2,1)S(1)} %copy-done.2, bf16[1024,128]{1,0:T(8,128)(2,1)S(1)} %get-tuple-element.25.refs_0_, ...), custom_call_target="tpu_custom_call", output_to_operand_aliasing={{1}: (4, {})} | custom-call | flops 939524096 | bytes 11010048 | tf_op jit(solution)/shard_map/pallas_call | solution.py:339
  18.6 6.3 %shard_map.60 = (bf16[1024,128]{1,0:T(8,128)(2,1)S(1)}, bf16[2048,1792]{1,0:T(8,128)(2,1)}) custom-call(s32[2]{0:T(128)S(1)} %pad_add_fusion.4.where_ref, bf16[4096,3584]{1,0:T(8,128)(2,1)} %refs_0_.1, bf16[3584,128]{1,0:T(8,128)(2,1)S(1)} %copy-done.2, bf16[1024,128]{1,0:T(8,128)(2,1)S(1)} %get-tuple-element.28.refs_0_), custom_call_target="tpu_custom_call" | custom-call | flops 939524096 | bytes 11010048 | tf_op jit(solution)/shard_map/pallas_call | solution.py:339
  25.0 6.3 %shard_map.61 = (f32[1024,128]{1,0:T(8,128)S(1)}, bf16[2048,1792]{1,0:T(8,128)(2,1)}) custom-call(s32[2]{0:T(128)S(1)} %pad_add_fusion.3.where_ref, bf16[4096,3584]{1,0:T(8,128)(2,1)} %refs_0_.1, bf16[3584,128]{1,0:T(8,128)(2,1)S(1)} %copy-done.2, bf16[1024,128]{1,0:T(8,128)(2,1)S(1)} %get-tuple-element.29.refs_0_, ...), custom_call_target="tpu_custom_call", output_to_operand_aliasing={{1}: (5, {})} | custom-call | flops 939524096 | bytes 11010048 | tf_op jit(solution)/shard_map/pallas_call | solution.py:339
  32.4 7.6 %collective-permute-done.3.refs_1_ = bf16[1024,128]{1,0:T(8,128)(2,1)S(1)} collective-permute-done((bf16[1024,128]{1,0:T(8,128)(2,1)S(1)}, bf16[1024,128]{1,0:T(8,128)(2,1)S(1)}, u32[]{:S(2)}, u32[]{:S(2)}) %collective-permute-start.3) | collective-permute-done | bytes 262176 | tf_op jit(solution)/shard_map/ppermute | solution.py:587
  40.4 1.6 %collective-permute-start.5 = (bf16[256,128]{1,0:T(8,128)(2,1)S(1)}, bf16[256,128]{1,0:T(8,128)(2,1)S(1)}, u32[]{:S(2)}, u32[]{:S(2)}) collective-permute-start(bf16[256,128]{1,0:T(8,128)(2,1)S(1)} %get-tuple-element.34), channel_id=1, source_target_pairs={{0,2},{1,3},{2,0},{3,1},{4,6},{5,7},{6,4},{7,5},{8,10},{9,11},{10,... | collective-permute-start | bytes 196616 | tf_op jit(solution)/shard_map/ppermute | solution.py:581
  42.1 2.6 %collective-permute-start.6 = (bf16[256,128]{1,0:T(8,128)(2,1)S(1)}, bf16[256,128]{1,0:T(8,128)(2,1)S(1)}, u32[]{:S(2)}, u32[]{:S(2)}) collective-permute-start(bf16[256,128]{1,0:T(8,128)(2,1)S(1)} %get-tuple-element.35), channel_id=1, source_target_pairs={{0,4},{1,5},{2,6},{3,7},{4,0},{5,1},{6,2},{7,3},{8,12},{9,13},{10,... | collective-permute-start | bytes 196616 | tf_op jit(solution)/shard_map/ppermute | solution.py:581
  45.4 3.2 %collective-permute-done.6 = bf16[256,128]{1,0:T(8,128)(2,1)S(1)} collective-permute-done((bf16[256,128]{1,0:T(8,128)(2,1)S(1)}, bf16[256,128]{1,0:T(8,128)(2,1)S(1)}, u32[]{:S(2)}, u32[]{:S(2)}) %collective-permute-start.6) | collective-permute-done | bytes 65568 | tf_op jit(solution)/shard_map/ppermute | solution.py:581
  48.6 2.1 %collective-permute-done.7 = bf16[256,128]{1,0:T(8,128)(2,1)S(1)} collective-permute-done((bf16[256,128]{1,0:T(8,128)(2,1)S(1)}, bf16[256,128]{1,0:T(8,128)(2,1)S(1)}, u32[]{:S(2)}, u32[]{:S(2)}) %collective-permute-start.7) | collective-permute-done | bytes 65568 | tf_op jit(solution)/shard_map/ppermute | solution.py:581
  50.8 1.1 collective-permute-start.10
  52.3 2.9 %collective-permute-start.8 = (bf16[256,128]{1,0:T(8,128)(2,1)S(1)}, bf16[256,128]{1,0:T(8,128)(2,1)S(1)}, u32[]{:S(2)}, u32[]{:S(2)}) collective-permute-start(bf16[256,128]{1,0:T(8,128)(2,1)S(1)} %add_convert_fusion.refs_0_), channel_id=1, source_target_pairs={{0,2},{1,3},{2,0},{3,1},{4,6},{5,7},{6,4},{7,5},{8,10},{9,11},{10,... | collective-permute-start | bytes 196616 | tf_op jit(solution)/shard_map/ppermute | solution.py:581
  55.2 1.7 %collective-permute-done.10.refs_3_ = bf16[256,128]{1,0:T(8,128)(2,1)S(1)} collective-permute-done((bf16[256,128]{1,0:T(8,128)(2,1)S(1)}, bf16[256,128]{1,0:T(8,128)(2,1)S(1)}, u32[]{:S(2)}, u32[]{:S(2)}) %collective-permute-start.10) | collective-permute-done | bytes 65568 | tf_op jit(solution)/shard_map/ppermute | solution.py:581
  57.0 1.3 collective-permute-done.9.refs_2_
  58.3 1.5 collective-permute-start.13
  60.4 1.5 %collective-permute-start.11 = (bf16[1024,128]{1,0:T(8,128)(2,1)S(1)}, bf16[1024,128]{1,0:T(8,128)(2,1)S(1)}, u32[]{:S(2)}, u32[]{:S(2)}) collective-permute-start(bf16[1024,128]{1,0:T(8,128)(2,1)S(1)} %shard_map.63.refs_0_), channel_id=1, source_target_pairs={{0,1},{1,0},{2,3},{3,2},{4,5},{5,4},{6,7},{7,6},{16,17},{17,16},{1... | collective-permute-start | bytes 786440 | tf_op jit(solution)/shard_map/ppermute | solution.py:587
  61.9 5.4 %collective-permute-done.13.refs_3_ = bf16[1024,128]{1,0:T(8,128)(2,1)S(1)} collective-permute-done((bf16[1024,128]{1,0:T(8,128)(2,1)S(1)}, bf16[1024,128]{1,0:T(8,128)(2,1)S(1)}, u32[]{:S(2)}, u32[]{:S(2)}) %collective-permute-start.13) | collective-permute-done | bytes 262176 | tf_op jit(solution)/shard_map/ppermute | solution.py:587
  67.3 1.7 %collective-permute-done.12.refs_2_ = bf16[1024,128]{1,0:T(8,128)(2,1)S(1)} collective-permute-done((bf16[1024,128]{1,0:T(8,128)(2,1)S(1)}, bf16[1024,128]{1,0:T(8,128)(2,1)S(1)}, u32[]{:S(2)}, u32[]{:S(2)}) %collective-permute-start.12) | collective-permute-done | bytes 262176 | tf_op jit(solution)/shard_map/ppermute | solution.py:587
  69.0 0.9 collective-permute-done.11.refs_1_
  70.2 0.7 convert_multiply_fusion.refs_3_.refs_2_
  70.9 0.6 pad_add_fusion.where_ref
  71.5 3.3 %multiply_convert_fusion.refs_4_.refs_3_ = bf16[2,16,256,256]{3,2,1,0:T(8,128)(2,1)} fusion(f32[2,16,256]{2,1,0:T(8,128)S(1)} %add_convert_fusion.1, f32[256,256]{1,0:T(8,128)S(1)} %subtract_convert_fusion), kind=kLoop, calls=%fused_computation | loop fusion | flops 4194304 | bytes 4489216 | tf_op jit(solution)/shard_map/convert_element_type | solution.py:62
  74.8 0.9 copy-done.5
  75.7 36.6 %shard_map.65 = (bf16[4096,1792]{1,0:T(8,128)(2,1)S(1)}, bf16[4096,1792]{1,0:T(8,128)(2,1)}, bf16[128,1792]{1,0:T(8,128)(2,1)}) custom-call(s32[2]{0:T(128)} %pad_add_fusion.where_ref, bf16[4096,3584]{1,0:T(8,128)(2,1)} %refs_0_.1, bf16[2048,1792]{1,0:T(8,128)(2,1)} %collective-permute-done.refs_1_, bf16[2048,1792]{1,0:T(8,128)(2,1)} %collective-permute-done.2.refs_2_, ...), custom_call_target="tpu_custom_call" | custom-call | flops 11274289152 | bytes 48234496 | tf_op jit(solution)/shard_map/pallas_call | solution.py:288
  112.6 1.5 collective-permute-start.16
  114.1 1.2 copy-done.4
  115.3 1.2 copy-done.6
  116.6 16.8 %shard_map.66 = (f32[128,128]{1,0:T(8,128)S(1)}, f32[4096,128]{1,0:T(8,128)}, bf16[4096,128]{1,0:T(8,128)(2,1)S(1)}) custom-call(bf16[4096,128]{1,0:T(8,128)(2,1)S(1)} %copy-done.4, bf16[4096,128]{1,0:T(8,128)(2,1)S(1)} %copy-done.6, f32[2]{0:T(128)S(1)} %copy-done.7, bf16[2,16,256,256]{3,2,1,0:T(8,128)(2,1)S(1)} %copy-done), custom_call_target="tpu_custom_call" | custom-call | flops 8000000000 | bytes 60000000 | tf_op jit(solution)/shard_map/pallas_call | solution.py:521
  133.4 0.9 convolution_multiply_fusion.right_ref
  134.4 8.6 %shard_map.67 = (bf16[4096,3584]{1,0:T(8,128)(2,1)}, f32[3584,128]{1,0:T(8,128)}) custom-call(s32[1]{0:T(128)} %bitcast.1.where_ref, bf16[4096,1792]{1,0:T(8,128)(2,1)S(1)} %get-tuple-element.41.rotated_ref, bf16[4096,128]{1,0:T(8,128)(2,1)S(1)} %get-tuple-element.38.basis_ref, f32[128,1792]{1,0:T(8,128)S(1)} %convolution_multiply_fusion.right_ref), custom_call_target="tpu_custom_call" | custom-call | flops 1879048192 | bytes 14680064 | tf_op jit(solution)/shard_map/pallas_call | solution.py:555
  143.0 8.6 %shard_map.68 = (bf16[4096,3584]{1,0:T(8,128)(2,1)}, f32[3584,128]{1,0:T(8,128)}) custom-call(s32[1]{0:T(128)} %bitcast.where_ref, bf16[4096,1792]{1,0:T(8,128)(2,1)S(1)} %collective-permute-done.15.rotated_ref, bf16[4096,128]{1,0:T(8,128)(2,1)S(1)} %get-tuple-element.38.basis_ref, ...), custom_call_target="tpu_custom_call", output_to_operand_aliasing={{0}: (4, {}), {1}: (5, {})} | custom-call | flops 1879048192 | bytes 14680064 | tf_op jit(solution)/shard_map/pallas_call | solution.py:555
  (48 shorter events, 4.0 us)
Async XLA Ops:
  0.7 1.2 copy-start.1
  1.9 10.2 %copy-start.2 = (bf16[3584,128]{1,0:T(8,128)(2,1)S(1)}, bf16[3584,128]{1,0:T(8,128)(2,1)}, u32[]{:S(2)}) copy-start(bf16[3584,128]{1,0:T(8,128)(2,1)} %q_ref.7) | copy-start | bytes 2752516
  8.2 16.7 %collective-permute-start.1 = (bf16[1024,128]{1,0:T(8,128)(2,1)S(1)}, bf16[1024,128]{1,0:T(8,128)(2,1)S(1)}, u32[]{:S(2)}, u32[]{:S(2)}) collective-permute-start(bf16[1024,128]{1,0:T(8,128)(2,1)S(1)} %get-tuple-element.25.refs_0_), channel_id=1, source_target_pairs={{0,17},{1,16},{2,19},{3,18},{4,21},{5,20},{6,23},{7,22},{16,1},{17... | collective-permute-start | bytes 786440 | tf_op jit(solution)/shard_map/ppermute | solution.py:587
  18.5 56.3 %collective-permute-start = (bf16[2048,1792]{1,0:T(8,128)(2,1)}, bf16[2048,1792]{1,0:T(8,128)(2,1)}, u32[]{:S(2)}, u32[]{:S(2)}) collective-permute-start(bf16[2048,1792]{1,0:T(8,128)(2,1)} %get-tuple-element.27), channel_id=1, source_target_pairs={{0,8},{8,0},{1,9},{9,1},{2,10},{10,2},{3,11},{11,3},{4,12},{12,4},... | collective-permute-start | bytes 22020104 | tf_op jit(solution)/shard_map/ppermute | solution.py:581
  25.0 45.2 %copy-start.9 = (s32[8192]{0:T(1024)S(1)}, s32[8192]{0:T(1024)}, u32[]{:S(2)}) copy-start(s32[8192]{0:T(1024)} %param.4) | copy-start | bytes 98308
  31.3 43.5 %collective-permute-start.2 = (bf16[2048,1792]{1,0:T(8,128)(2,1)}, bf16[2048,1792]{1,0:T(8,128)(2,1)}, u32[]{:S(2)}, u32[]{:S(2)}) collective-permute-start(bf16[2048,1792]{1,0:T(8,128)(2,1)} %get-tuple-element.31), channel_id=1, source_target_pairs={{0,8},{8,0},{1,9},{9,1},{2,10},{10,2},{3,11},{11,3},{4,12},{12,4},... | collective-permute-start | bytes 22020104 | tf_op jit(solution)/shard_map/ppermute | solution.py:581
  31.8 8.2 %collective-permute-start.3 = (bf16[1024,128]{1,0:T(8,128)(2,1)S(1)}, bf16[1024,128]{1,0:T(8,128)(2,1)S(1)}, u32[]{:S(2)}, u32[]{:S(2)}) collective-permute-start(bf16[1024,128]{1,0:T(8,128)(2,1)S(1)} %get-tuple-element.28.refs_0_), channel_id=1, source_target_pairs={{0,16},{1,17},{2,18},{3,19},{4,20},{5,21},{6,22},{7,23},{16,0},{17... | collective-permute-start | bytes 786440 | tf_op jit(solution)/shard_map/ppermute | solution.py:587
  32.4 7.9 %collective-permute-start.4 = (bf16[1024,128]{1,0:T(8,128)(2,1)S(1)}, bf16[1024,128]{1,0:T(8,128)(2,1)S(1)}, u32[]{:S(2)}, u32[]{:S(2)}) collective-permute-start(bf16[1024,128]{1,0:T(8,128)(2,1)S(1)} %get-tuple-element.29.refs_0_), channel_id=1, source_target_pairs={{0,1},{1,0},{2,3},{3,2},{4,5},{5,4},{6,7},{7,6},{16,17},{17,16},{1... | collective-permute-start | bytes 786440 | tf_op jit(solution)/shard_map/ppermute | solution.py:587
  40.4 5.0 %collective-permute-start.5 = (bf16[256,128]{1,0:T(8,128)(2,1)S(1)}, bf16[256,128]{1,0:T(8,128)(2,1)S(1)}, u32[]{:S(2)}, u32[]{:S(2)}) collective-permute-start(bf16[256,128]{1,0:T(8,128)(2,1)S(1)} %get-tuple-element.34), channel_id=1, source_target_pairs={{0,2},{1,3},{2,0},{3,1},{4,6},{5,7},{6,4},{7,5},{8,10},{9,11},{10,... | collective-permute-start | bytes 196616 | tf_op jit(solution)/shard_map/ppermute | solution.py:581
  42.1 6.6 %collective-permute-start.6 = (bf16[256,128]{1,0:T(8,128)(2,1)S(1)}, bf16[256,128]{1,0:T(8,128)(2,1)S(1)}, u32[]{:S(2)}, u32[]{:S(2)}) collective-permute-start(bf16[256,128]{1,0:T(8,128)(2,1)S(1)} %get-tuple-element.35), channel_id=1, source_target_pairs={{0,4},{1,5},{2,6},{3,7},{4,0},{5,1},{6,2},{7,3},{8,12},{9,13},{10,... | collective-permute-start | bytes 196616 | tf_op jit(solution)/shard_map/ppermute | solution.py:581
  44.6 6.1 %collective-permute-start.7 = (bf16[256,128]{1,0:T(8,128)(2,1)S(1)}, bf16[256,128]{1,0:T(8,128)(2,1)S(1)}, u32[]{:S(2)}, u32[]{:S(2)}) collective-permute-start(bf16[256,128]{1,0:T(8,128)(2,1)S(1)} %get-tuple-element.36), channel_id=1, source_target_pairs={{0,6},{1,7},{2,4},{3,5},{4,2},{5,3},{6,0},{7,1},{8,14},{9,15},{10,... | collective-permute-start | bytes 196616 | tf_op jit(solution)/shard_map/ppermute | solution.py:581
  50.8 6.2 %collective-permute-start.10 = (bf16[256,128]{1,0:T(8,128)(2,1)S(1)}, bf16[256,128]{1,0:T(8,128)(2,1)S(1)}, u32[]{:S(2)}, u32[]{:S(2)}) collective-permute-start(bf16[256,128]{1,0:T(8,128)(2,1)S(1)} %add_convert_fusion.refs_0_), channel_id=1, source_target_pairs={{0,6},{1,7},{2,4},{3,5},{4,2},{5,3},{6,0},{7,1},{8,14},{9,15},{10,... | collective-permute-start | bytes 196616 | tf_op jit(solution)/shard_map/ppermute | solution.py:581
  51.9 6.4 %collective-permute-start.9 = (bf16[256,128]{1,0:T(8,128)(2,1)S(1)}, bf16[256,128]{1,0:T(8,128)(2,1)S(1)}, u32[]{:S(2)}, u32[]{:S(2)}) collective-permute-start(bf16[256,128]{1,0:T(8,128)(2,1)S(1)} %add_convert_fusion.refs_0_), channel_id=1, source_target_pairs={{0,4},{1,5},{2,6},{3,7},{4,0},{5,1},{6,2},{7,3},{8,12},{9,13},{10,... | collective-permute-start | bytes 196616 | tf_op jit(solution)/shard_map/ppermute | solution.py:581
  52.3 6.0 %collective-permute-start.8 = (bf16[256,128]{1,0:T(8,128)(2,1)S(1)}, bf16[256,128]{1,0:T(8,128)(2,1)S(1)}, u32[]{:S(2)}, u32[]{:S(2)}) collective-permute-start(bf16[256,128]{1,0:T(8,128)(2,1)S(1)} %add_convert_fusion.refs_0_), channel_id=1, source_target_pairs={{0,2},{1,3},{2,0},{3,1},{4,6},{5,7},{6,4},{7,5},{8,10},{9,11},{10,... | collective-permute-start | bytes 196616 | tf_op jit(solution)/shard_map/ppermute | solution.py:581
  58.3 8.9 %collective-permute-start.13 = (bf16[1024,128]{1,0:T(8,128)(2,1)S(1)}, bf16[1024,128]{1,0:T(8,128)(2,1)S(1)}, u32[]{:S(2)}, u32[]{:S(2)}) collective-permute-start(bf16[1024,128]{1,0:T(8,128)(2,1)S(1)} %shard_map.63.refs_0_), channel_id=1, source_target_pairs={{0,17},{1,16},{2,19},{3,18},{4,21},{5,20},{6,23},{7,22},{16,1},{17... | collective-permute-start | bytes 786440 | tf_op jit(solution)/shard_map/ppermute | solution.py:587
  59.8 9.2 %collective-permute-start.12 = (bf16[1024,128]{1,0:T(8,128)(2,1)S(1)}, bf16[1024,128]{1,0:T(8,128)(2,1)S(1)}, u32[]{:S(2)}, u32[]{:S(2)}) collective-permute-start(bf16[1024,128]{1,0:T(8,128)(2,1)S(1)} %shard_map.63.refs_0_), channel_id=1, source_target_pairs={{0,16},{1,17},{2,18},{3,19},{4,20},{5,21},{6,22},{7,23},{16,0},{17... | collective-permute-start | bytes 786440 | tf_op jit(solution)/shard_map/ppermute | solution.py:587
  60.4 9.6 %collective-permute-start.11 = (bf16[1024,128]{1,0:T(8,128)(2,1)S(1)}, bf16[1024,128]{1,0:T(8,128)(2,1)S(1)}, u32[]{:S(2)}, u32[]{:S(2)}) collective-permute-start(bf16[1024,128]{1,0:T(8,128)(2,1)S(1)} %shard_map.63.refs_0_), channel_id=1, source_target_pairs={{0,1},{1,0},{2,3},{3,2},{4,5},{5,4},{6,7},{7,6},{16,17},{17,16},{1... | collective-permute-start | bytes 786440 | tf_op jit(solution)/shard_map/ppermute | solution.py:587
  70.0 4.8 %copy-start.3 = (bf16[4096,128]{1,0:T(8,128)(2,1)}, bf16[4096,128]{1,0:T(8,128)(2,1)S(1)}, u32[]{:S(2)}) copy-start(bf16[4096,128]{1,0:T(8,128)(2,1)S(1)} %shard_map.64.refs_5_.refs_0_) | copy-start | bytes 3145732
  70.0 4.7 %collective-permute-start.14 = (bf16[4096,128]{1,0:T(8,128)(2,1)S(1)}, bf16[4096,128]{1,0:T(8,128)(2,1)S(1)}, u32[]{:S(2)}, u32[]{:S(2)}) collective-permute-start(bf16[4096,128]{1,0:T(8,128)(2,1)S(1)} %shard_map.64.refs_5_.refs_0_), channel_id=1, source_target_pairs={{0,8},{8,0},{1,9},{9,1},{2,10},{10,2},{3,11},{11,3},{4,12},{12,4},... | collective-permute-start | bytes 3145736 | tf_op jit(solution)/shard_map/ppermute | solution.py:581
  74.8 39.3 %copy-start = (bf16[2,16,256,256]{3,2,1,0:T(8,128)(2,1)S(1)}, bf16[2,16,256,256]{3,2,1,0:T(8,128)(2,1)}, u32[]{:S(2)}) copy-start(bf16[2,16,256,256]{3,2,1,0:T(8,128)(2,1)} %multiply_convert_fusion.refs_4_.refs_3_) | copy-start | bytes 12582916
  74.8 39.3 %copy-start.7 = (f32[2]{0:T(128)S(1)}, f32[2]{0:T(128)}, u32[]{:S(2)}) copy-start(f32[2]{0:T(128)} %convert_multiply_fusion.refs_3_.refs_2_) | copy-start | bytes 28
  74.8 1.0 copy-start.5
  112.4 30.6 %collective-permute-start.15 = (bf16[4096,1792]{1,0:T(8,128)(2,1)}, bf16[4096,1792]{1,0:T(8,128)(2,1)S(1)}, u32[]{:S(2)}, u32[]{:S(2)}) collective-permute-start(bf16[4096,1792]{1,0:T(8,128)(2,1)} %get-tuple-element.37), channel_id=1, source_target_pairs={{0,8},{8,0},{1,9},{9,1},{2,10},{10,2},{3,11},{11,3},{4,12},{12,4},... | collective-permute-start | bytes 44040200 | tf_op jit(solution)/shard_map/ppermute | solution.py:581
  112.6 20.8 %collective-permute-start.16 = (bf16[128,1792]{1,0:T(8,128)(2,1)}, bf16[128,1792]{1,0:T(8,128)(2,1)S(1)}, u32[]{:S(2)}, u32[]{:S(2)}) collective-permute-start(bf16[128,1792]{1,0:T(8,128)(2,1)} %get-tuple-element.40), channel_id=1, source_target_pairs={{0,16},{16,0},{1,17},{17,1},{2,18},{18,2},{3,19},{19,3},{4,20},{20... | collective-permute-start | bytes 1376264 | tf_op jit(solution)/shard_map/ppermute | solution.py:581
  114.1 1.2 copy-start.4
  115.3 1.2 copy-start.6
  116.6 16.8 %copy-start.8 = (bf16[128,1792]{1,0:T(8,128)(2,1)S(1)}, bf16[128,1792]{1,0:T(8,128)(2,1)}, u32[]{:S(2)}) copy-start(bf16[128,1792]{1,0:T(8,128)(2,1)} %get-tuple-element.40) | copy-start | bytes 1376260
  134.3 8.7 %collective-permute-start.17 = (f32[128,1792]{1,0:T(8,128)S(1)}, f32[128,1792]{1,0:T(8,128)S(1)}, u32[]{:S(2)}, u32[]{:S(2)}) collective-permute-start(f32[128,1792]{1,0:T(8,128)S(1)} %convolution_multiply_fusion.right_ref), channel_id=1, source_target_pairs={{0,8},{8,0},{1,9},{9,1},{2,10},{10,2},{3,11},{11,3},{4,12},{12,4},... | collective-permute-start | bytes 2752520 | tf_op jit(solution)/shard_map/ppermute | solution.py:581

commit v6 on v5

--- a/solution.py
+++ b/solution.py
@@ -179,7 +179,7 @@
     return (minus_one_to(position) * minus_one_to(position & distances)).astype(F32) / math.sqrt(rows * group)
 
 
-def rotate_and_right(blocks, table, lefts, position, plane):
+def rotate_and_right(blocks, table, scales, lefts, position, plane):
     group = len(blocks)
     pieces = [len(block) for block in blocks]
     rows = blocks[0][0].shape[0]
@@ -306,7 +306,7 @@
         ),
         compiler_params=params(41),
         cost_estimate=cost(2 * size * (side + rank) * group, size * 2 * (2 * group - 1) + table.size * 2),
-    )(where, *flat, scales_of(position, group, rows), table, *lefts)
+    )(where, *flat, scales, table, *lefts)
 
 
 def project(accumulated, q_start, piece_at, position, group, out_types, after, copies=()):
@@ -357,12 +357,12 @@
     )(jnp.stack([piece_at, position]), accumulated, q_start, *after, *copies)
 
 
-def split_sum(own, others, place, pieces):
+def split_sum(own, others, place, pieces, after):
     rows, rank = own.shape
     piece = rows // pieces
 
     def body(where_ref, own_ref, *refs):
-        other_refs, out_refs = refs[: len(others)], refs[len(others) :]
+        other_refs, out_refs = refs[: len(others)], refs[len(others) + len(after) :]
         for d in range(pieces):
             at = pl.ds(pl.multiple_of((where_ref[0] ^ d) * piece, piece), piece)
             total = own_ref[at, :]
@@ -373,10 +373,10 @@
     return pl.pallas_call(
         body,
         out_shape=[jax.ShapeDtypeStruct((piece, rank), F32 if d == 0 else BF16) for d in range(pieces)],
-        in_specs=[pl.BlockSpec(memory_space=pltpu.SMEM)] + [pl.BlockSpec(memory_space=pltpu.VMEM)] * (1 + len(others)),
+        in_specs=[pl.BlockSpec(memory_space=pltpu.SMEM)] + [pl.BlockSpec(memory_space=pltpu.VMEM)] * (1 + len(others)) + [ANY] * len(after),
         out_specs=[pl.BlockSpec(memory_space=pltpu.VMEM)] * pieces,
         compiler_params=params(24),
-    )(place.reshape(1), own, *others)
+    )(place.reshape(1), own, *others, *after)
 
 
 def assemble(parts, place, after=()):
@@ -459,29 +459,40 @@
     rank = gram.shape[0]
     lane = lax.broadcasted_iota(jnp.int32, (8, rank), 1)
     row = lax.broadcasted_iota(jnp.int32, (8, rank), 0)
-    left = [gram[start : start + 8, :] for start in range(0, rank, 8)]
-    right = [jnp.where(lane == row + start, 1.0, 0.0).astype(F32) for start in range(0, rank, 8)]
-    scales = [jnp.zeros((8, rank), F32)] * len(left)
-    for k in range(rank):
-        home, inside = divmod(k, 8)
-        pivot_row = left[home][inside : inside + 1, :]
-        pivot = left[home][inside : inside + 1, k : k + 1]
-        made_row = right[home][inside : inside + 1, :]
-        root = lax.rsqrt(jnp.broadcast_to(pivot, (1, rank)))
-        scales[home] = jnp.where(row == inside, root, scales[home])
-        pivot_row, made_row = pivot_row * root * root, made_row * root * root
-        for block in range(home, len(left)):
-            if block == home and inside == 7:
-                continue
-            factor = jnp.broadcast_to(left[block][:, k : k + 1], (8, rank))
-            if block == home:
-                factor = jnp.where(row > inside, factor, 0.0)
-            left[block] = left[block] - factor * pivot_row
-            right[block] = right[block] - factor * made_row
+    starts = range(0, rank, 8)
+    left = [gram[start : start + 8, :] for start in starts]
+    right = [jnp.where(lane == row + start, 1.0, 0.0).astype(F32) for start in starts]
+    scales = []
+    for home, start in enumerate(starts):
+
+        def spread_columns(block):
+            return [jnp.broadcast_to(left[block][:, start + i : start + i + 1], (8, rank)) for i in range(8)]
+
+        columns, inverses = spread_columns(home), []
+        scale = jnp.zeros((8, rank), F32)
+        for i in range(8):
+            root = lax.rsqrt(jnp.broadcast_to(columns[i][i : i + 1, :], (8, rank)))
+            scale = jnp.where(row == i, root, scale)
+            inverses.append(root * root)
+            if i < 7:
+                factor = jnp.where(row > i, columns[i] * inverses[i], 0.0)
+                left[home] = left[home] - factor * left[home][i : i + 1, :]
+                right[home] = right[home] - factor * right[home][i : i + 1, :]
+                for after in range(i + 1, 8):
+                    columns[after] = columns[after] - factor * columns[after][i : i + 1, :]
+        scales.append(scale)
+        for block in range(home + 1, len(left)):
+            own = spread_columns(block)
+            for i in range(8):
+                factor = own[i] * inverses[i]
+                left[block] = left[block] - factor * left[home][i : i + 1, :]
+                right[block] = right[block] - factor * right[home][i : i + 1, :]
+                for after in range(i + 1, 8):
+                    own[after] = own[after] - factor * columns[after][i : i + 1, :]
     return jnp.concatenate([part * scale for part, scale in zip(right, scales)], axis=0)
 
 
-def basis_of(blocks, table, position):
+def basis_of(blocks, table, scales):
     group = len(blocks)
     rows, rank = blocks[0].shape
     _, count, side, _ = table.shape
@@ -530,7 +541,7 @@
         scratch_shapes=[pltpu.VMEM((count, side, rank), F32), pltpu.VMEM((rows, rank), F32)],
         compiler_params=params(10),
         cost_estimate=cost(8 * 10**9, 60 * 10**6),
-    )(*blocks, scales_of(position, group, rows), table)
+    )(*blocks, scales, table)
 
 
 def residual(rotated, basis16, right, columns, owner, resident, into=()):
@@ -620,11 +631,12 @@
                 other_pieces[e].append(from_distance(copy, "pos", e + 1))
             copies = ()
     table = signed_hadamard(signs, position, group, rows)
+    scales = scales_of(position, group, rows)
     if not shared:
         other_pieces = [[from_distance(accumulated, "pos", d)] for d in others]
     blocks = [[accumulated]] + other_pieces
 
-    own, *sent = split_sum(parts[0], came, line, lines)
+    own, *sent = split_sum(parts[0], came, line, lines, (table, scales))
     came = [from_line(sent[d - 1], d) for d in range(1, lines)]
     mine16 = sum([part.astype(F32) for part in came], own).astype(BF16)
     near16 = assemble([mine16] + [from_line(mine16, d) for d in range(1, lines)], line)
@@ -633,7 +645,7 @@
     around16 = [own16] + [from_distance(own16, "pos", d) for d in others]
 
     if shared:
-        *rotated, half = rotate_and_right(blocks, table, around16, position, plane)
+        *rotated, half = rotate_and_right(blocks, table, scales, around16, position, plane)
         rotated = rotated[:1] + [from_distance(part, "pos", d + 1) for d, part in enumerate(rotated[1:])]
         half = half.astype(F32) + from_distance(half, "rep", 1).astype(F32)
     else:
@@ -642,7 +654,7 @@
         for d in range(PLANE):
             *totals, _ = right_piece(accumulated, far16[d], plane ^ d, position, 1, totals)
         half = lax.psum(totals[0], ("rep", "pos"))
-    inverse, p_basis, basis16 = basis_of(around16, table, position)
+    inverse, p_basis, basis16 = basis_of(around16, table, scales)
 
     right = jnp.dot(inverse, half, precision=lax.Precision.HIGHEST) / REPLICAS
     if not shared:

time: 152 us -> 145 us (0.954)
  Pallas kernels: 96.2 us -> 88.7 us
  local copies, waits for them, and re-layouts: 4.6 us -> 7.18 us
  other arithmetic: 4.84 us -> 2.38 us
    pallas_call x1, Pallas kernels: 16.8 us -> 10.2 us  [basis_of(): pl.pallas_call(body, out_shape=[jax.ShapeDtypeStruct((rank, rank), F32),...]
    unnamed x20 -> x24, local copies, waits for them, and re-layouts: 4.59 us -> 7.17 us
    convert_element_type x1, other arithmetic: 3.26 us -> 1.31 us  [signed_hadamard(): return (sylvester(side) * flips).astype(BF16)]
    ppermute x12, waiting for transfers between devices: 8.96 us -> 10.9 us  [from_distance(): return lax.ppermute(block, axis, [(p, p ^ distance) for p in range(count)])]
  transfers between devices with their start and end apart: 18 -> 18, of which waited for: 10 -> 11; matrix products, arithmetic and copies ran while one was open for 4% -> 2% of each run, Pallas kernels for 29% -> 26%
where the time goes in v6:
time: 145 us
  Pallas kernels  88.7 us (61%)
  waiting for transfers between devices  25.4 us (18%)
  starting transfers between devices  19.2 us (13%)
  local copies, waits for them, and re-layouts  7.18 us (5%)
  other arithmetic  2.38 us (2%)
    pallas_call x1, Pallas kernels, rotate_and_right(): pl.pallas_call(body, out_shape=[pltpu.VMEM((rows, columns), BF16)] + [jax...  35.8 us
    pallas_call x4, Pallas kernels, project(): pl.pallas_call(body, out_shape=[jax.ShapeDtypeStruct((piece, rank), out_t...  25.4 us
    pallas_call x2, Pallas kernels, residual(): pl.pallas_call(body, out_shape=[jax.ShapeDtypeStruct((rows, columns), BF1...  17.1 us
    ppermute x6, waiting for transfers between devices, from_plane(): lax.ppermute(block, ('rep', 'mp'), [(p, p ^ change) for p in range(count)])  14.5 us
    ppermute x12, starting transfers between devices, from_distance(): return lax.ppermute(block, axis, [(p, p ^ distance) for p in range(count)])  11.2 us
    ppermute x12, waiting for transfers between devices, from_distance(): return lax.ppermute(block, axis, [(p, p ^ distance) for p in range(count)])  10.9 us
    pallas_call x1, Pallas kernels, basis_of(): pl.pallas_call(body, out_shape=[jax.ShapeDtypeStruct((rank, rank), F32),...  10.2 us
    ppermute x6, starting transfers between devices, from_plane(): lax.ppermute(block, ('rep', 'mp'), [(p, p ^ change) for p in range(count)])  8.02 us
  transfers between devices with their start and end apart: 18, of which 11 were waited for; matrix products, arithmetic and copies ran while one was open for 2% of the time, Pallas kernels for 26%

profile of v6, /device:TPU:0, one launch (start us, length us, event | category | flops | bytes accessed | tf_op | source)
XLA Modules:
  0.0 144.6 jit_solution(18336417914209107103)
XLA Ops:
  0.7 1.2 copy-done.2
  1.9 6.3 %shard_map.58 = (bf16[1024,128]{1,0:T(8,128)(2,1)S(1)}, bf16[2048,1792]{1,0:T(8,128)(2,1)}) custom-call(s32[2]{0:T(128)S(1)} %get-tuple-element.50.where_ref, bf16[4096,3584]{1,0:T(8,128)(2,1)} %refs_0_.1, bf16[3584,128]{1,0:T(8,128)(2,1)S(1)} %copy-done.2), custom_call_target="tpu_custom_call" | custom-call | flops 939524096 | bytes 11010048 | tf_op jit(solution)/shard_map/pallas_call | solution.py:339
  8.2 3.9 %collective-permute-start.1 = (bf16[1024,128]{1,0:T(8,128)(2,1)S(1)}, bf16[1024,128]{1,0:T(8,128)(2,1)S(1)}, u32[]{:S(2)}, u32[]{:S(2)}) collective-permute-start(bf16[1024,128]{1,0:T(8,128)(2,1)S(1)} %get-tuple-element.25.refs_0_), channel_id=1, source_target_pairs={{0,17},{1,16},{2,19},{3,18},{4,21},{5,20},{6,23},{7,22},{16,1},{17... | collective-permute-start | bytes 786440 | tf_op jit(solution)/shard_map/ppermute | solution.py:598
  12.1 6.4 %shard_map.59 = (bf16[1024,128]{1,0:T(8,128)(2,1)S(1)}, bf16[2048,1792]{1,0:T(8,128)(2,1)}) custom-call(s32[2]{0:T(128)S(1)} %get-tuple-element.49.where_ref, bf16[4096,3584]{1,0:T(8,128)(2,1)} %refs_0_.1, bf16[3584,128]{1,0:T(8,128)(2,1)S(1)} %copy-done.3, bf16[1024,128]{1,0:T(8,128)(2,1)S(1)} %get-tuple-element.25.refs_0_, ...), custom_call_target="tpu_custom_call", output_to_operand_aliasing={{1}: (4, {})} | custom-call | flops 939524096 | bytes 11010048 | tf_op jit(solution)/shard_map/pallas_call | solution.py:339
  18.6 6.3 %shard_map.60 = (bf16[1024,128]{1,0:T(8,128)(2,1)S(1)}, bf16[2048,1792]{1,0:T(8,128)(2,1)}) custom-call(s32[2]{0:T(128)S(1)} %pad_add_fusion.4.where_ref, bf16[4096,3584]{1,0:T(8,128)(2,1)} %refs_0_.1, bf16[3584,128]{1,0:T(8,128)(2,1)S(1)} %copy-done.3, bf16[1024,128]{1,0:T(8,128)(2,1)S(1)} %get-tuple-element.28.refs_0_), custom_call_target="tpu_custom_call" | custom-call | flops 939524096 | bytes 11010048 | tf_op jit(solution)/shard_map/pallas_call | solution.py:339
  25.0 6.4 %shard_map.61 = (f32[1024,128]{1,0:T(8,128)S(1)}, bf16[2048,1792]{1,0:T(8,128)(2,1)}) custom-call(s32[2]{0:T(128)S(1)} %pad_add_fusion.3.where_ref, bf16[4096,3584]{1,0:T(8,128)(2,1)} %refs_0_.1, bf16[3584,128]{1,0:T(8,128)(2,1)S(1)} %copy-done.3, bf16[1024,128]{1,0:T(8,128)(2,1)S(1)} %get-tuple-element.29.refs_0_, ...), custom_call_target="tpu_custom_call", output_to_operand_aliasing={{1}: (5, {})} | custom-call | flops 939524096 | bytes 11010048 | tf_op jit(solution)/shard_map/pallas_call | solution.py:339
  32.6 1.3 multiply_convert_fusion.refs_3_.refs_4_
  33.9 6.2 %collective-permute-done.3.refs_1_ = bf16[1024,128]{1,0:T(8,128)(2,1)S(1)} collective-permute-done((bf16[1024,128]{1,0:T(8,128)(2,1)S(1)}, bf16[1024,128]{1,0:T(8,128)(2,1)S(1)}, u32[]{:S(2)}, u32[]{:S(2)}) %collective-permute-start.3) | collective-permute-done | bytes 262176 | tf_op jit(solution)/shard_map/ppermute | solution.py:598
  40.5 2.0 %copy-done = bf16[2,16,256,256]{3,2,1,0:T(8,128)(2,1)} copy-done((bf16[2,16,256,256]{3,2,1,0:T(8,128)(2,1)}, bf16[2,16,256,256]{3,2,1,0:T(8,128)(2,1)S(1)}, u32[]{:S(2)}) %copy-start) | copy-done | bytes 4194328
  42.4 1.6 %collective-permute-start.5 = (bf16[256,128]{1,0:T(8,128)(2,1)S(1)}, bf16[256,128]{1,0:T(8,128)(2,1)S(1)}, u32[]{:S(2)}, u32[]{:S(2)}) collective-permute-start(bf16[256,128]{1,0:T(8,128)(2,1)S(1)} %get-tuple-element.34), channel_id=1, source_target_pairs={{0,2},{1,3},{2,0},{3,1},{4,6},{5,7},{6,4},{7,5},{8,10},{9,11},{10,... | collective-permute-start | bytes 196616 | tf_op jit(solution)/shard_map/ppermute | solution.py:592
  44.0 2.6 %collective-permute-start.6 = (bf16[256,128]{1,0:T(8,128)(2,1)S(1)}, bf16[256,128]{1,0:T(8,128)(2,1)S(1)}, u32[]{:S(2)}, u32[]{:S(2)}) collective-permute-start(bf16[256,128]{1,0:T(8,128)(2,1)S(1)} %get-tuple-element.35), channel_id=1, source_target_pairs={{0,4},{1,5},{2,6},{3,7},{4,0},{5,1},{6,2},{7,3},{8,12},{9,13},{10,... | collective-permute-start | bytes 196616 | tf_op jit(solution)/shard_map/ppermute | solution.py:592
  47.3 3.2 %collective-permute-done.6 = bf16[256,128]{1,0:T(8,128)(2,1)S(1)} collective-permute-done((bf16[256,128]{1,0:T(8,128)(2,1)S(1)}, bf16[256,128]{1,0:T(8,128)(2,1)S(1)}, u32[]{:S(2)}, u32[]{:S(2)}) %collective-permute-start.6) | collective-permute-done | bytes 65568 | tf_op jit(solution)/shard_map/ppermute | solution.py:592
  50.6 2.1 %collective-permute-done.7 = bf16[256,128]{1,0:T(8,128)(2,1)S(1)} collective-permute-done((bf16[256,128]{1,0:T(8,128)(2,1)S(1)}, bf16[256,128]{1,0:T(8,128)(2,1)S(1)}, u32[]{:S(2)}, u32[]{:S(2)}) %collective-permute-start.7) | collective-permute-done | bytes 65568 | tf_op jit(solution)/shard_map/ppermute | solution.py:592
  52.7 1.1 collective-permute-start.10
  54.3 2.9 %collective-permute-start.8 = (bf16[256,128]{1,0:T(8,128)(2,1)S(1)}, bf16[256,128]{1,0:T(8,128)(2,1)S(1)}, u32[]{:S(2)}, u32[]{:S(2)}) collective-permute-start(bf16[256,128]{1,0:T(8,128)(2,1)S(1)} %add_convert_fusion.refs_0_), channel_id=1, source_target_pairs={{0,2},{1,3},{2,0},{3,1},{4,6},{5,7},{6,4},{7,5},{8,10},{9,11},{10,... | collective-permute-start | bytes 196616 | tf_op jit(solution)/shard_map/ppermute | solution.py:592
  57.2 1.7 %collective-permute-done.10.refs_3_ = bf16[256,128]{1,0:T(8,128)(2,1)S(1)} collective-permute-done((bf16[256,128]{1,0:T(8,128)(2,1)S(1)}, bf16[256,128]{1,0:T(8,128)(2,1)S(1)}, u32[]{:S(2)}, u32[]{:S(2)}) %collective-permute-start.10) | collective-permute-done | bytes 65568 | tf_op jit(solution)/shard_map/ppermute | solution.py:592
  58.9 1.3 collective-permute-done.9.refs_2_
  60.3 1.5 %collective-permute-start.13 = (bf16[1024,128]{1,0:T(8,128)(2,1)S(1)}, bf16[1024,128]{1,0:T(8,128)(2,1)S(1)}, u32[]{:S(2)}, u32[]{:S(2)}) collective-permute-start(bf16[1024,128]{1,0:T(8,128)(2,1)S(1)} %shard_map.63.refs_0_), channel_id=1, source_target_pairs={{0,17},{1,16},{2,19},{3,18},{4,21},{5,20},{6,23},{7,22},{16,1},{17... | collective-permute-start | bytes 786440 | tf_op jit(solution)/shard_map/ppermute | solution.py:598
  62.3 1.5 %collective-permute-start.11 = (bf16[1024,128]{1,0:T(8,128)(2,1)S(1)}, bf16[1024,128]{1,0:T(8,128)(2,1)S(1)}, u32[]{:S(2)}, u32[]{:S(2)}) collective-permute-start(bf16[1024,128]{1,0:T(8,128)(2,1)S(1)} %shard_map.63.refs_0_), channel_id=1, source_target_pairs={{0,1},{1,0},{2,3},{3,2},{4,5},{5,4},{6,7},{7,6},{16,17},{17,16},{1... | collective-permute-start | bytes 786440 | tf_op jit(solution)/shard_map/ppermute | solution.py:598
  63.9 5.4 %collective-permute-done.13.refs_3_ = bf16[1024,128]{1,0:T(8,128)(2,1)S(1)} collective-permute-done((bf16[1024,128]{1,0:T(8,128)(2,1)S(1)}, bf16[1024,128]{1,0:T(8,128)(2,1)S(1)}, u32[]{:S(2)}, u32[]{:S(2)}) %collective-permute-start.13) | collective-permute-done | bytes 262176 | tf_op jit(solution)/shard_map/ppermute | solution.py:598
  69.3 1.7 %collective-permute-done.12.refs_2_ = bf16[1024,128]{1,0:T(8,128)(2,1)S(1)} collective-permute-done((bf16[1024,128]{1,0:T(8,128)(2,1)S(1)}, bf16[1024,128]{1,0:T(8,128)(2,1)S(1)}, u32[]{:S(2)}, u32[]{:S(2)}) %collective-permute-start.12) | collective-permute-done | bytes 262176 | tf_op jit(solution)/shard_map/ppermute | solution.py:598
  71.0 0.9 collective-permute-done.11.refs_1_
  72.8 1.9 %collective-permute-done.14.refs_6_.refs_1_ = bf16[4096,128]{1,0:T(8,128)(2,1)S(1)} collective-permute-done((bf16[4096,128]{1,0:T(8,128)(2,1)S(1)}, bf16[4096,128]{1,0:T(8,128)(2,1)S(1)}, u32[]{:S(2)}, u32[]{:S(2)}) %collective-permute-start.14) | collective-permute-done | bytes 1048608 | tf_op jit(solution)/shard_map/ppermute | solution.py:592
  74.8 0.9 copy-done.6
  75.7 35.8 %shard_map.65 = (bf16[4096,1792]{1,0:T(8,128)(2,1)S(1)}, bf16[4096,1792]{1,0:T(8,128)(2,1)}, bf16[128,1792]{1,0:T(8,128)(2,1)}) custom-call(s32[2]{0:T(128)} %pad_add_fusion.where_ref, bf16[4096,3584]{1,0:T(8,128)(2,1)} %refs_0_.1, bf16[2048,1792]{1,0:T(8,128)(2,1)} %collective-permute-done.refs_1_, bf16[2048,1792]{1,0:T(8,128)(2,1)} %collective-permute-done.2.refs_2_, ...), custom_call_target="tpu_custom_call" | custom-call | flops 11274289152 | bytes 48234496 | tf_op jit(solution)/shard_map/pallas_call | solution.py:288
  111.6 1.5 %collective-permute-start.16 = (bf16[128,1792]{1,0:T(8,128)(2,1)}, bf16[128,1792]{1,0:T(8,128)(2,1)S(1)}, u32[]{:S(2)}, u32[]{:S(2)}) collective-permute-start(bf16[128,1792]{1,0:T(8,128)(2,1)} %get-tuple-element.40), channel_id=1, source_target_pairs={{0,16},{16,0},{1,17},{17,1},{2,18},{18,2},{3,19},{19,3},{4,20},{20... | collective-permute-start | bytes 1376264 | tf_op jit(solution)/shard_map/ppermute | solution.py:592
  113.1 1.2 copy-done.5
  114.3 1.2 copy-done.7
  116.2 10.2 %shard_map.66 = (f32[128,128]{1,0:T(8,128)S(1)}, f32[4096,128]{1,0:T(8,128)}, bf16[4096,128]{1,0:T(8,128)(2,1)S(1)}) custom-call(bf16[4096,128]{1,0:T(8,128)(2,1)S(1)} %copy-done.5, bf16[4096,128]{1,0:T(8,128)(2,1)S(1)} %copy-done.7, f32[2]{0:T(128)S(1)} %copy-done.9, bf16[2,16,256,256]{3,2,1,0:T(8,128)(2,1)S(1)} %copy-done.1), custom_call_target="tpu_custom_call" | custom-call | flops 8000000000 | bytes 60000000 | tf_op jit(solution)/shard_map/pallas_call | solution.py:532
  126.3 0.9 convolution_multiply_fusion.right_ref
  127.4 8.5 %shard_map.67 = (bf16[4096,3584]{1,0:T(8,128)(2,1)}, f32[3584,128]{1,0:T(8,128)}) custom-call(s32[1]{0:T(128)} %bitcast.1.where_ref, bf16[4096,1792]{1,0:T(8,128)(2,1)S(1)} %get-tuple-element.41.rotated_ref, bf16[4096,128]{1,0:T(8,128)(2,1)S(1)} %get-tuple-element.38.basis_ref, f32[128,1792]{1,0:T(8,128)S(1)} %convolution_multiply_fusion.right_ref), custom_call_target="tpu_custom_call" | custom-call | flops 1879048192 | bytes 14680064 | tf_op jit(solution)/shard_map/pallas_call | solution.py:566
  136.0 8.6 %shard_map.68 = (bf16[4096,3584]{1,0:T(8,128)(2,1)}, f32[3584,128]{1,0:T(8,128)}) custom-call(s32[1]{0:T(128)} %bitcast.where_ref, bf16[4096,1792]{1,0:T(8,128)(2,1)S(1)} %collective-permute-done.15.rotated_ref, bf16[4096,128]{1,0:T(8,128)(2,1)S(1)} %get-tuple-element.38.basis_ref, ...), custom_call_target="tpu_custom_call", output_to_operand_aliasing={{0}: (4, {}), {1}: (5, {})} | custom-call | flops 1879048192 | bytes 14680064 | tf_op jit(solution)/shard_map/pallas_call | solution.py:566
  (52 shorter events, 5.3 us)
Async XLA Ops:
  0.7 1.2 copy-start.2
  1.9 10.2 %copy-start.3 = (bf16[3584,128]{1,0:T(8,128)(2,1)S(1)}, bf16[3584,128]{1,0:T(8,128)(2,1)}, u32[]{:S(2)}) copy-start(bf16[3584,128]{1,0:T(8,128)(2,1)} %q_ref.7) | copy-start | bytes 2752516
  8.2 16.8 %collective-permute-start.1 = (bf16[1024,128]{1,0:T(8,128)(2,1)S(1)}, bf16[1024,128]{1,0:T(8,128)(2,1)S(1)}, u32[]{:S(2)}, u32[]{:S(2)}) collective-permute-start(bf16[1024,128]{1,0:T(8,128)(2,1)S(1)} %get-tuple-element.25.refs_0_), channel_id=1, source_target_pairs={{0,17},{1,16},{2,19},{3,18},{4,21},{5,20},{6,23},{7,22},{16,1},{17... | collective-permute-start | bytes 786440 | tf_op jit(solution)/shard_map/ppermute | solution.py:598
  18.5 56.2 %collective-permute-start = (bf16[2048,1792]{1,0:T(8,128)(2,1)}, bf16[2048,1792]{1,0:T(8,128)(2,1)}, u32[]{:S(2)}, u32[]{:S(2)}) collective-permute-start(bf16[2048,1792]{1,0:T(8,128)(2,1)} %get-tuple-element.27), channel_id=1, source_target_pairs={{0,8},{8,0},{1,9},{9,1},{2,10},{10,2},{3,11},{11,3},{4,12},{12,4},... | collective-permute-start | bytes 22020104 | tf_op jit(solution)/shard_map/ppermute | solution.py:592
  25.0 7.4 %copy-start.11 = (s32[8192]{0:T(1024)S(1)}, s32[8192]{0:T(1024)}, u32[]{:S(2)}) copy-start(s32[8192]{0:T(1024)} %param.4) | copy-start | bytes 98308
  31.4 43.4 %collective-permute-start.2 = (bf16[2048,1792]{1,0:T(8,128)(2,1)}, bf16[2048,1792]{1,0:T(8,128)(2,1)}, u32[]{:S(2)}, u32[]{:S(2)}) collective-permute-start(bf16[2048,1792]{1,0:T(8,128)(2,1)} %get-tuple-element.31), channel_id=1, source_target_pairs={{0,8},{8,0},{1,9},{9,1},{2,10},{10,2},{3,11},{11,3},{4,12},{12,4},... | collective-permute-start | bytes 22020104 | tf_op jit(solution)/shard_map/ppermute | solution.py:592
  31.9 8.2 %collective-permute-start.3 = (bf16[1024,128]{1,0:T(8,128)(2,1)S(1)}, bf16[1024,128]{1,0:T(8,128)(2,1)S(1)}, u32[]{:S(2)}, u32[]{:S(2)}) collective-permute-start(bf16[1024,128]{1,0:T(8,128)(2,1)S(1)} %get-tuple-element.28.refs_0_), channel_id=1, source_target_pairs={{0,16},{1,17},{2,18},{3,19},{4,20},{5,21},{6,22},{7,23},{16,0},{17... | collective-permute-start | bytes 786440 | tf_op jit(solution)/shard_map/ppermute | solution.py:598
  32.4 7.9 %collective-permute-start.4 = (bf16[1024,128]{1,0:T(8,128)(2,1)S(1)}, bf16[1024,128]{1,0:T(8,128)(2,1)S(1)}, u32[]{:S(2)}, u32[]{:S(2)}) collective-permute-start(bf16[1024,128]{1,0:T(8,128)(2,1)S(1)} %get-tuple-element.29.refs_0_), channel_id=1, source_target_pairs={{0,1},{1,0},{2,3},{3,2},{4,5},{5,4},{6,7},{7,6},{16,17},{17,16},{1... | collective-permute-start | bytes 786440 | tf_op jit(solution)/shard_map/ppermute | solution.py:598
  32.5 42.2 %copy-start.8 = (f32[2]{0:T(128)}, f32[2]{0:T(128)S(1)}, u32[]{:S(2)}) copy-start(f32[2]{0:T(128)S(1)} %convert_multiply_fusion.refs_4_.refs_3_.refs_2_) | copy-start | bytes 28
  40.5 2.0 %copy-start = (bf16[2,16,256,256]{3,2,1,0:T(8,128)(2,1)}, bf16[2,16,256,256]{3,2,1,0:T(8,128)(2,1)S(1)}, u32[]{:S(2)}) copy-start(bf16[2,16,256,256]{3,2,1,0:T(8,128)(2,1)S(1)} %multiply_convert_fusion.refs_3_.refs_4_) | copy-start | bytes 12582916
  42.4 4.9 %collective-permute-start.5 = (bf16[256,128]{1,0:T(8,128)(2,1)S(1)}, bf16[256,128]{1,0:T(8,128)(2,1)S(1)}, u32[]{:S(2)}, u32[]{:S(2)}) collective-permute-start(bf16[256,128]{1,0:T(8,128)(2,1)S(1)} %get-tuple-element.34), channel_id=1, source_target_pairs={{0,2},{1,3},{2,0},{3,1},{4,6},{5,7},{6,4},{7,5},{8,10},{9,11},{10,... | collective-permute-start | bytes 196616 | tf_op jit(solution)/shard_map/ppermute | solution.py:592
  44.0 6.6 %collective-permute-start.6 = (bf16[256,128]{1,0:T(8,128)(2,1)S(1)}, bf16[256,128]{1,0:T(8,128)(2,1)S(1)}, u32[]{:S(2)}, u32[]{:S(2)}) collective-permute-start(bf16[256,128]{1,0:T(8,128)(2,1)S(1)} %get-tuple-element.35), channel_id=1, source_target_pairs={{0,4},{1,5},{2,6},{3,7},{4,0},{5,1},{6,2},{7,3},{8,12},{9,13},{10,... | collective-permute-start | bytes 196616 | tf_op jit(solution)/shard_map/ppermute | solution.py:592
  46.6 6.1 %collective-permute-start.7 = (bf16[256,128]{1,0:T(8,128)(2,1)S(1)}, bf16[256,128]{1,0:T(8,128)(2,1)S(1)}, u32[]{:S(2)}, u32[]{:S(2)}) collective-permute-start(bf16[256,128]{1,0:T(8,128)(2,1)S(1)} %get-tuple-element.36), channel_id=1, source_target_pairs={{0,6},{1,7},{2,4},{3,5},{4,2},{5,3},{6,0},{7,1},{8,14},{9,15},{10,... | collective-permute-start | bytes 196616 | tf_op jit(solution)/shard_map/ppermute | solution.py:592
  52.7 6.2 %collective-permute-start.10 = (bf16[256,128]{1,0:T(8,128)(2,1)S(1)}, bf16[256,128]{1,0:T(8,128)(2,1)S(1)}, u32[]{:S(2)}, u32[]{:S(2)}) collective-permute-start(bf16[256,128]{1,0:T(8,128)(2,1)S(1)} %add_convert_fusion.refs_0_), channel_id=1, source_target_pairs={{0,6},{1,7},{2,4},{3,5},{4,2},{5,3},{6,0},{7,1},{8,14},{9,15},{10,... | collective-permute-start | bytes 196616 | tf_op jit(solution)/shard_map/ppermute | solution.py:592
  53.9 6.4 %collective-permute-start.9 = (bf16[256,128]{1,0:T(8,128)(2,1)S(1)}, bf16[256,128]{1,0:T(8,128)(2,1)S(1)}, u32[]{:S(2)}, u32[]{:S(2)}) collective-permute-start(bf16[256,128]{1,0:T(8,128)(2,1)S(1)} %add_convert_fusion.refs_0_), channel_id=1, source_target_pairs={{0,4},{1,5},{2,6},{3,7},{4,0},{5,1},{6,2},{7,3},{8,12},{9,13},{10,... | collective-permute-start | bytes 196616 | tf_op jit(solution)/shard_map/ppermute | solution.py:592
  54.3 6.0 %collective-permute-start.8 = (bf16[256,128]{1,0:T(8,128)(2,1)S(1)}, bf16[256,128]{1,0:T(8,128)(2,1)S(1)}, u32[]{:S(2)}, u32[]{:S(2)}) collective-permute-start(bf16[256,128]{1,0:T(8,128)(2,1)S(1)} %add_convert_fusion.refs_0_), channel_id=1, source_target_pairs={{0,2},{1,3},{2,0},{3,1},{4,6},{5,7},{6,4},{7,5},{8,10},{9,11},{10,... | collective-permute-start | bytes 196616 | tf_op jit(solution)/shard_map/ppermute | solution.py:592
  60.3 9.0 %collective-permute-start.13 = (bf16[1024,128]{1,0:T(8,128)(2,1)S(1)}, bf16[1024,128]{1,0:T(8,128)(2,1)S(1)}, u32[]{:S(2)}, u32[]{:S(2)}) collective-permute-start(bf16[1024,128]{1,0:T(8,128)(2,1)S(1)} %shard_map.63.refs_0_), channel_id=1, source_target_pairs={{0,17},{1,16},{2,19},{3,18},{4,21},{5,20},{6,23},{7,22},{16,1},{17... | collective-permute-start | bytes 786440 | tf_op jit(solution)/shard_map/ppermute | solution.py:598
  61.8 9.2 %collective-permute-start.12 = (bf16[1024,128]{1,0:T(8,128)(2,1)S(1)}, bf16[1024,128]{1,0:T(8,128)(2,1)S(1)}, u32[]{:S(2)}, u32[]{:S(2)}) collective-permute-start(bf16[1024,128]{1,0:T(8,128)(2,1)S(1)} %shard_map.63.refs_0_), channel_id=1, source_target_pairs={{0,16},{1,17},{2,18},{3,19},{4,20},{5,21},{6,22},{7,23},{16,0},{17... | collective-permute-start | bytes 786440 | tf_op jit(solution)/shard_map/ppermute | solution.py:598
  62.3 9.6 %collective-permute-start.11 = (bf16[1024,128]{1,0:T(8,128)(2,1)S(1)}, bf16[1024,128]{1,0:T(8,128)(2,1)S(1)}, u32[]{:S(2)}, u32[]{:S(2)}) collective-permute-start(bf16[1024,128]{1,0:T(8,128)(2,1)S(1)} %shard_map.63.refs_0_), channel_id=1, source_target_pairs={{0,1},{1,0},{2,3},{3,2},{4,5},{5,4},{6,7},{7,6},{16,17},{17,16},{1... | collective-permute-start | bytes 786440 | tf_op jit(solution)/shard_map/ppermute | solution.py:598
  72.0 2.8 %copy-start.4 = (bf16[4096,128]{1,0:T(8,128)(2,1)}, bf16[4096,128]{1,0:T(8,128)(2,1)S(1)}, u32[]{:S(2)}) copy-start(bf16[4096,128]{1,0:T(8,128)(2,1)S(1)} %shard_map.64.refs_5_.refs_0_) | copy-start | bytes 3145732
  72.0 2.7 %collective-permute-start.14 = (bf16[4096,128]{1,0:T(8,128)(2,1)S(1)}, bf16[4096,128]{1,0:T(8,128)(2,1)S(1)}, u32[]{:S(2)}, u32[]{:S(2)}) collective-permute-start(bf16[4096,128]{1,0:T(8,128)(2,1)S(1)} %shard_map.64.refs_5_.refs_0_), channel_id=1, source_target_pairs={{0,8},{8,0},{1,9},{9,1},{2,10},{10,2},{3,11},{11,3},{4,12},{12,4},... | collective-permute-start | bytes 3145736 | tf_op jit(solution)/shard_map/ppermute | solution.py:592
  72.8 40.3 %copy-start.1 = (bf16[2,16,256,256]{3,2,1,0:T(8,128)(2,1)S(1)}, bf16[2,16,256,256]{3,2,1,0:T(8,128)(2,1)}, u32[]{:S(2)}) copy-start(bf16[2,16,256,256]{3,2,1,0:T(8,128)(2,1)} %copy-done) | copy-start | bytes 12582916
  74.7 1.0 copy-start.6
  111.5 24.5 %collective-permute-start.15 = (bf16[4096,1792]{1,0:T(8,128)(2,1)}, bf16[4096,1792]{1,0:T(8,128)(2,1)S(1)}, u32[]{:S(2)}, u32[]{:S(2)}) collective-permute-start(bf16[4096,1792]{1,0:T(8,128)(2,1)} %get-tuple-element.37), channel_id=1, source_target_pairs={{0,8},{8,0},{1,9},{9,1},{2,10},{10,2},{3,11},{11,3},{4,12},{12,4},... | collective-permute-start | bytes 44040200 | tf_op jit(solution)/shard_map/ppermute | solution.py:592
  111.6 14.7 %collective-permute-start.16 = (bf16[128,1792]{1,0:T(8,128)(2,1)}, bf16[128,1792]{1,0:T(8,128)(2,1)S(1)}, u32[]{:S(2)}, u32[]{:S(2)}) collective-permute-start(bf16[128,1792]{1,0:T(8,128)(2,1)} %get-tuple-element.40), channel_id=1, source_target_pairs={{0,16},{16,0},{1,17},{17,1},{2,18},{18,2},{3,19},{19,3},{4,20},{20... | collective-permute-start | bytes 1376264 | tf_op jit(solution)/shard_map/ppermute | solution.py:592
  113.1 1.2 copy-start.5
  114.3 1.2 copy-start.7
  115.6 0.6 copy-start.9
  116.2 10.2 %copy-start.10 = (bf16[128,1792]{1,0:T(8,128)(2,1)S(1)}, bf16[128,1792]{1,0:T(8,128)(2,1)}, u32[]{:S(2)}) copy-start(bf16[128,1792]{1,0:T(8,128)(2,1)} %get-tuple-element.40) | copy-start | bytes 1376260
  127.3 8.7 %collective-permute-start.17 = (f32[128,1792]{1,0:T(8,128)S(1)}, f32[128,1792]{1,0:T(8,128)S(1)}, u32[]{:S(2)}, u32[]{:S(2)}) collective-permute-start(f32[128,1792]{1,0:T(8,128)S(1)} %convolution_multiply_fusion.right_ref), channel_id=1, source_target_pairs={{0,8},{8,0},{1,9},{9,1},{2,10},{10,2},{3,11},{11,3},{4,12},{12,4},... | collective-permute-start | bytes 2752520 | tf_op jit(solution)/shard_map/ppermute | solution.py:592

commit v7 on v6

--- a/solution.py
+++ b/solution.py
@@ -373,7 +373,7 @@
     return pl.pallas_call(
         body,
         out_shape=[jax.ShapeDtypeStruct((piece, rank), F32 if d == 0 else BF16) for d in range(pieces)],
-        in_specs=[pl.BlockSpec(memory_space=pltpu.SMEM)] + [pl.BlockSpec(memory_space=pltpu.VMEM)] * (1 + len(others)) + [ANY] * len(after),
+        in_specs=[pl.BlockSpec(memory_space=pltpu.SMEM)] + [pl.BlockSpec(memory_space=pltpu.VMEM)] * (1 + len(others) + len(after)),
         out_specs=[pl.BlockSpec(memory_space=pltpu.VMEM)] * pieces,
         compiler_params=params(24),
     )(place.reshape(1), own, *others, *after)
@@ -636,7 +636,7 @@
         other_pieces = [[from_distance(accumulated, "pos", d)] for d in others]
     blocks = [[accumulated]] + other_pieces
 
-    own, *sent = split_sum(parts[0], came, line, lines, (table, scales))
+    own, *sent = split_sum(parts[0], came, line, lines, (table,))
     came = [from_line(sent[d - 1], d) for d in range(1, lines)]
     mine16 = sum([part.astype(F32) for part in came], own).astype(BF16)
     near16 = assemble([mine16] + [from_line(mine16, d) for d in range(1, lines)], line)

time: 145 us -> 144 us (level)
    unnamed x24 -> x22, local copies, waits for them, and re-layouts: 7.17 us -> 6.57 us
  transfers between devices with their start and end apart: 18 -> 18, of which waited for: 11 -> 11; matrix products, arithmetic and copies ran while one was open for 2% -> 3% of each run, Pallas kernels for 26% -> 26%
where the time goes in v7:
time: 144 us
  Pallas kernels  88.6 us (62%)
  waiting for transfers between devices  24.9 us (17%)
  starting transfers between devices  19.2 us (13%)
  local copies, waits for them, and re-layouts  6.59 us (5%)
  other arithmetic  2.82 us (2%)
    pallas_call x1, Pallas kernels, rotate_and_right(): pl.pallas_call(body, out_shape=[pltpu.VMEM((rows, columns), BF16)] + [jax...  35.8 us
    pallas_call x4, Pallas kernels, project(): pl.pallas_call(body, out_shape=[jax.ShapeDtypeStruct((piece, rank), out_t...  25.4 us
    pallas_call x2, Pallas kernels, residual(): pl.pallas_call(body, out_shape=[jax.ShapeDtypeStruct((rows, columns), BF1...  17.1 us
    ppermute x6, waiting for transfers between devices, from_plane(): lax.ppermute(block, ('rep', 'mp'), [(p, p ^ change) for p in range(count)])  14.5 us
    ppermute x12, starting transfers between devices, from_distance(): return lax.ppermute(block, axis, [(p, p ^ distance) for p in range(count)])  11.2 us
    ppermute x12, waiting for transfers between devices, from_distance(): return lax.ppermute(block, axis, [(p, p ^ distance) for p in range(count)])  10.4 us
    pallas_call x1, Pallas kernels, basis_of(): pl.pallas_call(body, out_shape=[jax.ShapeDtypeStruct((rank, rank), F32),...  10.2 us
    ppermute x6, starting transfers between devices, from_plane(): lax.ppermute(block, ('rep', 'mp'), [(p, p ^ change) for p in range(count)])  8.02 us
  transfers between devices with their start and end apart: 18, of which 11 were waited for; matrix products, arithmetic and copies ran while one was open for 3% of the time, Pallas kernels for 26%

profile of v7, /device:TPU:0, one launch (start us, length us, event | category | flops | bytes accessed | tf_op | source)
XLA Modules:
  0.0 143.9 jit_solution(13898262132268071165)
XLA Ops:
  0.7 1.2 copy-done.2
  1.9 6.3 %shard_map.58 = (bf16[1024,128]{1,0:T(8,128)(2,1)S(1)}, bf16[2048,1792]{1,0:T(8,128)(2,1)}) custom-call(s32[2]{0:T(128)S(1)} %get-tuple-element.50.where_ref, bf16[4096,3584]{1,0:T(8,128)(2,1)} %refs_0_.1, bf16[3584,128]{1,0:T(8,128)(2,1)S(1)} %copy-done.2), custom_call_target="tpu_custom_call" | custom-call | flops 939524096 | bytes 11010048 | tf_op jit(solution)/shard_map/pallas_call | solution.py:339
  8.2 3.9 %collective-permute-start.1 = (bf16[1024,128]{1,0:T(8,128)(2,1)S(1)}, bf16[1024,128]{1,0:T(8,128)(2,1)S(1)}, u32[]{:S(2)}, u32[]{:S(2)}) collective-permute-start(bf16[1024,128]{1,0:T(8,128)(2,1)S(1)} %get-tuple-element.25.refs_0_), channel_id=1, source_target_pairs={{0,17},{1,16},{2,19},{3,18},{4,21},{5,20},{6,23},{7,22},{16,1},{17... | collective-permute-start | bytes 786440 | tf_op jit(solution)/shard_map/ppermute | solution.py:598
  12.1 6.3 %shard_map.59 = (bf16[1024,128]{1,0:T(8,128)(2,1)S(1)}, bf16[2048,1792]{1,0:T(8,128)(2,1)}) custom-call(s32[2]{0:T(128)S(1)} %get-tuple-element.49.where_ref, bf16[4096,3584]{1,0:T(8,128)(2,1)} %refs_0_.1, bf16[3584,128]{1,0:T(8,128)(2,1)S(1)} %copy-done.3, bf16[1024,128]{1,0:T(8,128)(2,1)S(1)} %get-tuple-element.25.refs_0_, ...), custom_call_target="tpu_custom_call", output_to_operand_aliasing={{1}: (4, {})} | custom-call | flops 939524096 | bytes 11010048 | tf_op jit(solution)/shard_map/pallas_call | solution.py:339
  18.6 6.3 %shard_map.60 = (bf16[1024,128]{1,0:T(8,128)(2,1)S(1)}, bf16[2048,1792]{1,0:T(8,128)(2,1)}) custom-call(s32[2]{0:T(128)S(1)} %pad_add_fusion.4.where_ref, bf16[4096,3584]{1,0:T(8,128)(2,1)} %refs_0_.1, bf16[3584,128]{1,0:T(8,128)(2,1)S(1)} %copy-done.3, bf16[1024,128]{1,0:T(8,128)(2,1)S(1)} %get-tuple-element.28.refs_0_), custom_call_target="tpu_custom_call" | custom-call | flops 939524096 | bytes 11010048 | tf_op jit(solution)/shard_map/pallas_call | solution.py:339
  25.0 6.3 %shard_map.61 = (f32[1024,128]{1,0:T(8,128)S(1)}, bf16[2048,1792]{1,0:T(8,128)(2,1)}) custom-call(s32[2]{0:T(128)S(1)} %pad_add_fusion.3.where_ref, bf16[4096,3584]{1,0:T(8,128)(2,1)} %refs_0_.1, bf16[3584,128]{1,0:T(8,128)(2,1)S(1)} %copy-done.3, bf16[1024,128]{1,0:T(8,128)(2,1)S(1)} %get-tuple-element.29.refs_0_, ...), custom_call_target="tpu_custom_call", output_to_operand_aliasing={{1}: (5, {})} | custom-call | flops 939524096 | bytes 11010048 | tf_op jit(solution)/shard_map/pallas_call | solution.py:339
  32.5 1.3 multiply_convert_fusion.refs_3_.refs_4_
  33.8 6.2 %collective-permute-done.3.refs_1_ = bf16[1024,128]{1,0:T(8,128)(2,1)S(1)} collective-permute-done((bf16[1024,128]{1,0:T(8,128)(2,1)S(1)}, bf16[1024,128]{1,0:T(8,128)(2,1)S(1)}, u32[]{:S(2)}, u32[]{:S(2)}) %collective-permute-start.3) | collective-permute-done | bytes 262176 | tf_op jit(solution)/shard_map/ppermute | solution.py:598
  40.4 2.0 %copy-done = bf16[2,16,256,256]{3,2,1,0:T(8,128)(2,1)} copy-done((bf16[2,16,256,256]{3,2,1,0:T(8,128)(2,1)}, bf16[2,16,256,256]{3,2,1,0:T(8,128)(2,1)S(1)}, u32[]{:S(2)}) %copy-start) | copy-done | bytes 4194328
  42.4 1.6 %collective-permute-start.5 = (bf16[256,128]{1,0:T(8,128)(2,1)S(1)}, bf16[256,128]{1,0:T(8,128)(2,1)S(1)}, u32[]{:S(2)}, u32[]{:S(2)}) collective-permute-start(bf16[256,128]{1,0:T(8,128)(2,1)S(1)} %get-tuple-element.34), channel_id=1, source_target_pairs={{0,2},{1,3},{2,0},{3,1},{4,6},{5,7},{6,4},{7,5},{8,10},{9,11},{10,... | collective-permute-start | bytes 196616 | tf_op jit(solution)/shard_map/ppermute | solution.py:592
  44.0 2.6 %collective-permute-start.6 = (bf16[256,128]{1,0:T(8,128)(2,1)S(1)}, bf16[256,128]{1,0:T(8,128)(2,1)S(1)}, u32[]{:S(2)}, u32[]{:S(2)}) collective-permute-start(bf16[256,128]{1,0:T(8,128)(2,1)S(1)} %get-tuple-element.35), channel_id=1, source_target_pairs={{0,4},{1,5},{2,6},{3,7},{4,0},{5,1},{6,2},{7,3},{8,12},{9,13},{10,... | collective-permute-start | bytes 196616 | tf_op jit(solution)/shard_map/ppermute | solution.py:592
  47.3 3.2 %collective-permute-done.6 = bf16[256,128]{1,0:T(8,128)(2,1)S(1)} collective-permute-done((bf16[256,128]{1,0:T(8,128)(2,1)S(1)}, bf16[256,128]{1,0:T(8,128)(2,1)S(1)}, u32[]{:S(2)}, u32[]{:S(2)}) %collective-permute-start.6) | collective-permute-done | bytes 65568 | tf_op jit(solution)/shard_map/ppermute | solution.py:592
  50.5 2.1 %collective-permute-done.7 = bf16[256,128]{1,0:T(8,128)(2,1)S(1)} collective-permute-done((bf16[256,128]{1,0:T(8,128)(2,1)S(1)}, bf16[256,128]{1,0:T(8,128)(2,1)S(1)}, u32[]{:S(2)}, u32[]{:S(2)}) %collective-permute-start.7) | collective-permute-done | bytes 65568 | tf_op jit(solution)/shard_map/ppermute | solution.py:592
  52.7 1.1 collective-permute-start.10
  54.2 2.9 %collective-permute-start.8 = (bf16[256,128]{1,0:T(8,128)(2,1)S(1)}, bf16[256,128]{1,0:T(8,128)(2,1)S(1)}, u32[]{:S(2)}, u32[]{:S(2)}) collective-permute-start(bf16[256,128]{1,0:T(8,128)(2,1)S(1)} %add_convert_fusion.refs_0_), channel_id=1, source_target_pairs={{0,2},{1,3},{2,0},{3,1},{4,6},{5,7},{6,4},{7,5},{8,10},{9,11},{10,... | collective-permute-start | bytes 196616 | tf_op jit(solution)/shard_map/ppermute | solution.py:592
  57.1 1.7 %collective-permute-done.10.refs_3_ = bf16[256,128]{1,0:T(8,128)(2,1)S(1)} collective-permute-done((bf16[256,128]{1,0:T(8,128)(2,1)S(1)}, bf16[256,128]{1,0:T(8,128)(2,1)S(1)}, u32[]{:S(2)}, u32[]{:S(2)}) %collective-permute-start.10) | collective-permute-done | bytes 65568 | tf_op jit(solution)/shard_map/ppermute | solution.py:592
  58.9 1.3 collective-permute-done.9.refs_2_
  60.2 1.5 %collective-permute-start.13 = (bf16[1024,128]{1,0:T(8,128)(2,1)S(1)}, bf16[1024,128]{1,0:T(8,128)(2,1)S(1)}, u32[]{:S(2)}, u32[]{:S(2)}) collective-permute-start(bf16[1024,128]{1,0:T(8,128)(2,1)S(1)} %shard_map.63.refs_0_), channel_id=1, source_target_pairs={{0,17},{1,16},{2,19},{3,18},{4,21},{5,20},{6,23},{7,22},{16,1},{17... | collective-permute-start | bytes 786440 | tf_op jit(solution)/shard_map/ppermute | solution.py:598
  62.3 1.5 %collective-permute-start.11 = (bf16[1024,128]{1,0:T(8,128)(2,1)S(1)}, bf16[1024,128]{1,0:T(8,128)(2,1)S(1)}, u32[]{:S(2)}, u32[]{:S(2)}) collective-permute-start(bf16[1024,128]{1,0:T(8,128)(2,1)S(1)} %shard_map.63.refs_0_), channel_id=1, source_target_pairs={{0,1},{1,0},{2,3},{3,2},{4,5},{5,4},{6,7},{7,6},{16,17},{17,16},{1... | collective-permute-start | bytes 786440 | tf_op jit(solution)/shard_map/ppermute | solution.py:598
  63.8 5.4 %collective-permute-done.13.refs_3_ = bf16[1024,128]{1,0:T(8,128)(2,1)S(1)} collective-permute-done((bf16[1024,128]{1,0:T(8,128)(2,1)S(1)}, bf16[1024,128]{1,0:T(8,128)(2,1)S(1)}, u32[]{:S(2)}, u32[]{:S(2)}) %collective-permute-start.13) | collective-permute-done | bytes 262176 | tf_op jit(solution)/shard_map/ppermute | solution.py:598
  69.2 1.7 %collective-permute-done.12.refs_2_ = bf16[1024,128]{1,0:T(8,128)(2,1)S(1)} collective-permute-done((bf16[1024,128]{1,0:T(8,128)(2,1)S(1)}, bf16[1024,128]{1,0:T(8,128)(2,1)S(1)}, u32[]{:S(2)}, u32[]{:S(2)}) %collective-permute-start.12) | collective-permute-done | bytes 262176 | tf_op jit(solution)/shard_map/ppermute | solution.py:598
  70.9 0.9 collective-permute-done.11.refs_1_
  73.2 1.5 %collective-permute-done.14.refs_6_.refs_1_ = bf16[4096,128]{1,0:T(8,128)(2,1)S(1)} collective-permute-done((bf16[4096,128]{1,0:T(8,128)(2,1)S(1)}, bf16[4096,128]{1,0:T(8,128)(2,1)S(1)}, u32[]{:S(2)}, u32[]{:S(2)}) %collective-permute-start.14) | collective-permute-done | bytes 1048608 | tf_op jit(solution)/shard_map/ppermute | solution.py:592
  74.7 0.9 copy-done.6
  75.6 35.8 %shard_map.65 = (bf16[4096,1792]{1,0:T(8,128)(2,1)S(1)}, bf16[4096,1792]{1,0:T(8,128)(2,1)}, bf16[128,1792]{1,0:T(8,128)(2,1)}) custom-call(s32[2]{0:T(128)} %pad_add_fusion.where_ref, bf16[4096,3584]{1,0:T(8,128)(2,1)} %refs_0_.1, bf16[2048,1792]{1,0:T(8,128)(2,1)} %collective-permute-done.refs_1_, bf16[2048,1792]{1,0:T(8,128)(2,1)} %collective-permute-done.2.refs_2_, ...), custom_call_target="tpu_custom_call" | custom-call | flops 11274289152 | bytes 48234496 | tf_op jit(solution)/shard_map/pallas_call | solution.py:288
  111.6 1.5 %collective-permute-start.16 = (bf16[128,1792]{1,0:T(8,128)(2,1)}, bf16[128,1792]{1,0:T(8,128)(2,1)S(1)}, u32[]{:S(2)}, u32[]{:S(2)}) collective-permute-start(bf16[128,1792]{1,0:T(8,128)(2,1)} %get-tuple-element.40), channel_id=1, source_target_pairs={{0,16},{16,0},{1,17},{17,1},{2,18},{18,2},{3,19},{19,3},{4,20},{20... | collective-permute-start | bytes 1376264 | tf_op jit(solution)/shard_map/ppermute | solution.py:592
  113.1 1.2 copy-done.5
  114.3 1.2 copy-done.7
  115.5 10.2 %shard_map.66 = (f32[128,128]{1,0:T(8,128)S(1)}, f32[4096,128]{1,0:T(8,128)}, bf16[4096,128]{1,0:T(8,128)(2,1)S(1)}) custom-call(bf16[4096,128]{1,0:T(8,128)(2,1)S(1)} %copy-done.5, bf16[4096,128]{1,0:T(8,128)(2,1)S(1)} %copy-done.7, f32[2]{0:T(128)S(1)} %copy-done.8, bf16[2,16,256,256]{3,2,1,0:T(8,128)(2,1)S(1)} %copy-done.1), custom_call_target="tpu_custom_call" | custom-call | flops 8000000000 | bytes 60000000 | tf_op jit(solution)/shard_map/pallas_call | solution.py:532
  125.7 0.9 convolution_multiply_fusion.right_ref
  126.8 8.5 %shard_map.67 = (bf16[4096,3584]{1,0:T(8,128)(2,1)}, f32[3584,128]{1,0:T(8,128)}) custom-call(s32[1]{0:T(128)} %bitcast.1.where_ref, bf16[4096,1792]{1,0:T(8,128)(2,1)S(1)} %get-tuple-element.41.rotated_ref, bf16[4096,128]{1,0:T(8,128)(2,1)S(1)} %get-tuple-element.38.basis_ref, f32[128,1792]{1,0:T(8,128)S(1)} %convolution_multiply_fusion.right_ref), custom_call_target="tpu_custom_call" | custom-call | flops 1879048192 | bytes 14680064 | tf_op jit(solution)/shard_map/pallas_call | solution.py:566
  135.3 8.6 %shard_map.68 = (bf16[4096,3584]{1,0:T(8,128)(2,1)}, f32[3584,128]{1,0:T(8,128)}) custom-call(s32[1]{0:T(128)} %bitcast.where_ref, bf16[4096,1792]{1,0:T(8,128)(2,1)S(1)} %collective-permute-done.15.rotated_ref, bf16[4096,128]{1,0:T(8,128)(2,1)S(1)} %get-tuple-element.38.basis_ref, ...), custom_call_target="tpu_custom_call", output_to_operand_aliasing={{0}: (4, {}), {1}: (5, {})} | custom-call | flops 1879048192 | bytes 14680064 | tf_op jit(solution)/shard_map/pallas_call | solution.py:566
  (50 shorter events, 5.2 us)
Async XLA Ops:
  0.7 1.2 copy-start.2
  1.9 10.2 %copy-start.3 = (bf16[3584,128]{1,0:T(8,128)(2,1)S(1)}, bf16[3584,128]{1,0:T(8,128)(2,1)}, u32[]{:S(2)}) copy-start(bf16[3584,128]{1,0:T(8,128)(2,1)} %q_ref.7) | copy-start | bytes 2752516
  8.2 16.7 %collective-permute-start.1 = (bf16[1024,128]{1,0:T(8,128)(2,1)S(1)}, bf16[1024,128]{1,0:T(8,128)(2,1)S(1)}, u32[]{:S(2)}, u32[]{:S(2)}) collective-permute-start(bf16[1024,128]{1,0:T(8,128)(2,1)S(1)} %get-tuple-element.25.refs_0_), channel_id=1, source_target_pairs={{0,17},{1,16},{2,19},{3,18},{4,21},{5,20},{6,23},{7,22},{16,1},{17... | collective-permute-start | bytes 786440 | tf_op jit(solution)/shard_map/ppermute | solution.py:598
  18.5 56.2 %collective-permute-start = (bf16[2048,1792]{1,0:T(8,128)(2,1)}, bf16[2048,1792]{1,0:T(8,128)(2,1)}, u32[]{:S(2)}, u32[]{:S(2)}) collective-permute-start(bf16[2048,1792]{1,0:T(8,128)(2,1)} %get-tuple-element.27), channel_id=1, source_target_pairs={{0,8},{8,0},{1,9},{9,1},{2,10},{10,2},{3,11},{11,3},{4,12},{12,4},... | collective-permute-start | bytes 22020104 | tf_op jit(solution)/shard_map/ppermute | solution.py:592
  25.0 7.4 %copy-start.10 = (s32[8192]{0:T(1024)S(1)}, s32[8192]{0:T(1024)}, u32[]{:S(2)}) copy-start(s32[8192]{0:T(1024)} %param.4) | copy-start | bytes 98308
  31.3 43.4 %collective-permute-start.2 = (bf16[2048,1792]{1,0:T(8,128)(2,1)}, bf16[2048,1792]{1,0:T(8,128)(2,1)}, u32[]{:S(2)}, u32[]{:S(2)}) collective-permute-start(bf16[2048,1792]{1,0:T(8,128)(2,1)} %get-tuple-element.31), channel_id=1, source_target_pairs={{0,8},{8,0},{1,9},{9,1},{2,10},{10,2},{3,11},{11,3},{4,12},{12,4},... | collective-permute-start | bytes 22020104 | tf_op jit(solution)/shard_map/ppermute | solution.py:592
  31.8 8.2 %collective-permute-start.3 = (bf16[1024,128]{1,0:T(8,128)(2,1)S(1)}, bf16[1024,128]{1,0:T(8,128)(2,1)S(1)}, u32[]{:S(2)}, u32[]{:S(2)}) collective-permute-start(bf16[1024,128]{1,0:T(8,128)(2,1)S(1)} %get-tuple-element.28.refs_0_), channel_id=1, source_target_pairs={{0,16},{1,17},{2,18},{3,19},{4,20},{5,21},{6,22},{7,23},{16,0},{17... | collective-permute-start | bytes 786440 | tf_op jit(solution)/shard_map/ppermute | solution.py:598
  32.4 7.9 %collective-permute-start.4 = (bf16[1024,128]{1,0:T(8,128)(2,1)S(1)}, bf16[1024,128]{1,0:T(8,128)(2,1)S(1)}, u32[]{:S(2)}, u32[]{:S(2)}) collective-permute-start(bf16[1024,128]{1,0:T(8,128)(2,1)S(1)} %get-tuple-element.29.refs_0_), channel_id=1, source_target_pairs={{0,1},{1,0},{2,3},{3,2},{4,5},{5,4},{6,7},{7,6},{16,17},{17,16},{1... | collective-permute-start | bytes 786440 | tf_op jit(solution)/shard_map/ppermute | solution.py:598
  40.4 2.0 %copy-start = (bf16[2,16,256,256]{3,2,1,0:T(8,128)(2,1)}, bf16[2,16,256,256]{3,2,1,0:T(8,128)(2,1)S(1)}, u32[]{:S(2)}) copy-start(bf16[2,16,256,256]{3,2,1,0:T(8,128)(2,1)S(1)} %multiply_convert_fusion.refs_3_.refs_4_) | copy-start | bytes 12582916
  42.4 4.9 %collective-permute-start.5 = (bf16[256,128]{1,0:T(8,128)(2,1)S(1)}, bf16[256,128]{1,0:T(8,128)(2,1)S(1)}, u32[]{:S(2)}, u32[]{:S(2)}) collective-permute-start(bf16[256,128]{1,0:T(8,128)(2,1)S(1)} %get-tuple-element.34), channel_id=1, source_target_pairs={{0,2},{1,3},{2,0},{3,1},{4,6},{5,7},{6,4},{7,5},{8,10},{9,11},{10,... | collective-permute-start | bytes 196616 | tf_op jit(solution)/shard_map/ppermute | solution.py:592
  44.0 6.6 %collective-permute-start.6 = (bf16[256,128]{1,0:T(8,128)(2,1)S(1)}, bf16[256,128]{1,0:T(8,128)(2,1)S(1)}, u32[]{:S(2)}, u32[]{:S(2)}) collective-permute-start(bf16[256,128]{1,0:T(8,128)(2,1)S(1)} %get-tuple-element.35), channel_id=1, source_target_pairs={{0,4},{1,5},{2,6},{3,7},{4,0},{5,1},{6,2},{7,3},{8,12},{9,13},{10,... | collective-permute-start | bytes 196616 | tf_op jit(solution)/shard_map/ppermute | solution.py:592
  46.6 6.1 %collective-permute-start.7 = (bf16[256,128]{1,0:T(8,128)(2,1)S(1)}, bf16[256,128]{1,0:T(8,128)(2,1)S(1)}, u32[]{:S(2)}, u32[]{:S(2)}) collective-permute-start(bf16[256,128]{1,0:T(8,128)(2,1)S(1)} %get-tuple-element.36), channel_id=1, source_target_pairs={{0,6},{1,7},{2,4},{3,5},{4,2},{5,3},{6,0},{7,1},{8,14},{9,15},{10,... | collective-permute-start | bytes 196616 | tf_op jit(solution)/shard_map/ppermute | solution.py:592
  52.7 6.2 %collective-permute-start.10 = (bf16[256,128]{1,0:T(8,128)(2,1)S(1)}, bf16[256,128]{1,0:T(8,128)(2,1)S(1)}, u32[]{:S(2)}, u32[]{:S(2)}) collective-permute-start(bf16[256,128]{1,0:T(8,128)(2,1)S(1)} %add_convert_fusion.refs_0_), channel_id=1, source_target_pairs={{0,6},{1,7},{2,4},{3,5},{4,2},{5,3},{6,0},{7,1},{8,14},{9,15},{10,... | collective-permute-start | bytes 196616 | tf_op jit(solution)/shard_map/ppermute | solution.py:592
  53.8 6.4 %collective-permute-start.9 = (bf16[256,128]{1,0:T(8,128)(2,1)S(1)}, bf16[256,128]{1,0:T(8,128)(2,1)S(1)}, u32[]{:S(2)}, u32[]{:S(2)}) collective-permute-start(bf16[256,128]{1,0:T(8,128)(2,1)S(1)} %add_convert_fusion.refs_0_), channel_id=1, source_target_pairs={{0,4},{1,5},{2,6},{3,7},{4,0},{5,1},{6,2},{7,3},{8,12},{9,13},{10,... | collective-permute-start | bytes 196616 | tf_op jit(solution)/shard_map/ppermute | solution.py:592
  54.2 6.0 %collective-permute-start.8 = (bf16[256,128]{1,0:T(8,128)(2,1)S(1)}, bf16[256,128]{1,0:T(8,128)(2,1)S(1)}, u32[]{:S(2)}, u32[]{:S(2)}) collective-permute-start(bf16[256,128]{1,0:T(8,128)(2,1)S(1)} %add_convert_fusion.refs_0_), channel_id=1, source_target_pairs={{0,2},{1,3},{2,0},{3,1},{4,6},{5,7},{6,4},{7,5},{8,10},{9,11},{10,... | collective-permute-start | bytes 196616 | tf_op jit(solution)/shard_map/ppermute | solution.py:592
  60.2 8.9 %collective-permute-start.13 = (bf16[1024,128]{1,0:T(8,128)(2,1)S(1)}, bf16[1024,128]{1,0:T(8,128)(2,1)S(1)}, u32[]{:S(2)}, u32[]{:S(2)}) collective-permute-start(bf16[1024,128]{1,0:T(8,128)(2,1)S(1)} %shard_map.63.refs_0_), channel_id=1, source_target_pairs={{0,17},{1,16},{2,19},{3,18},{4,21},{5,20},{6,23},{7,22},{16,1},{17... | collective-permute-start | bytes 786440 | tf_op jit(solution)/shard_map/ppermute | solution.py:598
  61.7 9.2 %collective-permute-start.12 = (bf16[1024,128]{1,0:T(8,128)(2,1)S(1)}, bf16[1024,128]{1,0:T(8,128)(2,1)S(1)}, u32[]{:S(2)}, u32[]{:S(2)}) collective-permute-start(bf16[1024,128]{1,0:T(8,128)(2,1)S(1)} %shard_map.63.refs_0_), channel_id=1, source_target_pairs={{0,16},{1,17},{2,18},{3,19},{4,20},{5,21},{6,22},{7,23},{16,0},{17... | collective-permute-start | bytes 786440 | tf_op jit(solution)/shard_map/ppermute | solution.py:598
  62.3 9.6 %collective-permute-start.11 = (bf16[1024,128]{1,0:T(8,128)(2,1)S(1)}, bf16[1024,128]{1,0:T(8,128)(2,1)S(1)}, u32[]{:S(2)}, u32[]{:S(2)}) collective-permute-start(bf16[1024,128]{1,0:T(8,128)(2,1)S(1)} %shard_map.63.refs_0_), channel_id=1, source_target_pairs={{0,1},{1,0},{2,3},{3,2},{4,5},{5,4},{6,7},{7,6},{16,17},{17,16},{1... | collective-permute-start | bytes 786440 | tf_op jit(solution)/shard_map/ppermute | solution.py:598
  71.9 2.8 %copy-start.4 = (bf16[4096,128]{1,0:T(8,128)(2,1)}, bf16[4096,128]{1,0:T(8,128)(2,1)S(1)}, u32[]{:S(2)}) copy-start(bf16[4096,128]{1,0:T(8,128)(2,1)S(1)} %shard_map.64.refs_5_.refs_0_) | copy-start | bytes 3145732
  71.9 2.7 %collective-permute-start.14 = (bf16[4096,128]{1,0:T(8,128)(2,1)S(1)}, bf16[4096,128]{1,0:T(8,128)(2,1)S(1)}, u32[]{:S(2)}, u32[]{:S(2)}) collective-permute-start(bf16[4096,128]{1,0:T(8,128)(2,1)S(1)} %shard_map.64.refs_5_.refs_0_), channel_id=1, source_target_pairs={{0,8},{8,0},{1,9},{9,1},{2,10},{10,2},{3,11},{11,3},{4,12},{12,4},... | collective-permute-start | bytes 3145736 | tf_op jit(solution)/shard_map/ppermute | solution.py:592
  73.2 39.9 %copy-start.1 = (bf16[2,16,256,256]{3,2,1,0:T(8,128)(2,1)S(1)}, bf16[2,16,256,256]{3,2,1,0:T(8,128)(2,1)}, u32[]{:S(2)}) copy-start(bf16[2,16,256,256]{3,2,1,0:T(8,128)(2,1)} %copy-done) | copy-start | bytes 12582916
  73.2 39.9 %copy-start.8 = (f32[2]{0:T(128)S(1)}, f32[2]{0:T(128)}, u32[]{:S(2)}) copy-start(f32[2]{0:T(128)} %convert_multiply_fusion.refs_3_.refs_2_) | copy-start | bytes 28
  74.7 1.0 copy-start.6
  111.4 23.9 %collective-permute-start.15 = (bf16[4096,1792]{1,0:T(8,128)(2,1)}, bf16[4096,1792]{1,0:T(8,128)(2,1)S(1)}, u32[]{:S(2)}, u32[]{:S(2)}) collective-permute-start(bf16[4096,1792]{1,0:T(8,128)(2,1)} %get-tuple-element.37), channel_id=1, source_target_pairs={{0,8},{8,0},{1,9},{9,1},{2,10},{10,2},{3,11},{11,3},{4,12},{12,4},... | collective-permute-start | bytes 44040200 | tf_op jit(solution)/shard_map/ppermute | solution.py:592
  111.6 14.1 %collective-permute-start.16 = (bf16[128,1792]{1,0:T(8,128)(2,1)}, bf16[128,1792]{1,0:T(8,128)(2,1)S(1)}, u32[]{:S(2)}, u32[]{:S(2)}) collective-permute-start(bf16[128,1792]{1,0:T(8,128)(2,1)} %get-tuple-element.40), channel_id=1, source_target_pairs={{0,16},{16,0},{1,17},{17,1},{2,18},{18,2},{3,19},{19,3},{4,20},{20... | collective-permute-start | bytes 1376264 | tf_op jit(solution)/shard_map/ppermute | solution.py:592
  113.1 1.2 copy-start.5
  114.3 1.2 copy-start.7
  115.5 10.2 %copy-start.9 = (bf16[128,1792]{1,0:T(8,128)(2,1)S(1)}, bf16[128,1792]{1,0:T(8,128)(2,1)}, u32[]{:S(2)}) copy-start(bf16[128,1792]{1,0:T(8,128)(2,1)} %get-tuple-element.40) | copy-start | bytes 1376260
  126.6 8.7 %collective-permute-start.17 = (f32[128,1792]{1,0:T(8,128)S(1)}, f32[128,1792]{1,0:T(8,128)S(1)}, u32[]{:S(2)}, u32[]{:S(2)}) collective-permute-start(f32[128,1792]{1,0:T(8,128)S(1)} %convolution_multiply_fusion.right_ref), channel_id=1, source_target_pairs={{0,8},{8,0},{1,9},{9,1},{2,10},{10,2},{3,11},{11,3},{4,12},{12,4},... | collective-permute-start | bytes 2752520 | tf_op jit(solution)/shard_map/ppermute | solution.py:592
